TPU v7x, 256 devices: a whole 4x4x8 slice. The times are simulated.
256 devices in a mesh: band: 64 (over z, y, core), pw: 4 (over x).
Axes of the slice: x: 4, y: 4, z: 8, core: 2. Of those that a mesh axis runs over, the one named last changes fastest.
Arguments:
- densities: float32 [2, 1024, 10240], P(None, 'band', 'pw'), may hold values from -6 to 6
- screened: float32 [2, 4, 2560, 10240], P(None, None, 'band', 'pw'), may hold values from -0.0625 to 0.0625
- pairs: int32 [256, 2], replicated, may hold values from 0 to 63, as said below
- owners: int32 [256], replicated, may hold values from 0 to 63, as said below
Outputs:
- kernel_panel: float32 [64, 12, 2, 16, 16], P('band', None, None, 'pw')
Inputs may be any that keep to these rules, and one draw needn't show every extreme that they name: `pairs`: every block number is some slot's left block; the right blocks take exactly 32 distinct values. `owners`: at most 12 slots share an owner and some owner has exactly 12; every block number owns some slot.
All inputs are finite; a program needn't handle non-finite values.
Results may differ from a plain program's by a relative error of at most 0.000096.
Values sent between devices are 32-bit elements; how exact they have to be, the bound alone decides.
No kernel may reach another device: no remote copies, remote signals or barrier semaphores. Data moves between devices by JAX's collectives and lax.ppermute only.
A program may use at most 128 MiB of HBM per device.

v0:
```python
import functools

import jax
import jax.numpy as jnp
from jax import lax
from jax.experimental import pallas as pl
from jax.experimental.pallas import tpu as pltpu
from jax.sharding import Mesh
from jax.sharding import PartitionSpec as P

NG = 10240
CAP = 12
BLK = 16
USED = 32
HALF = USED // 2 * BLK
BAND = ("z", "y", "core")
SWAP = ((0, 1), (1, 0))
SMEM = pl.BlockSpec(memory_space=pltpu.SMEM)
VMEM = pl.BlockSpec(memory_space=pltpu.VMEM)
SPAN = 80
PLANE = 320
NEAR = (0, 7, 1, 6, 2)
MIDDLE = (5, 3)
FAR = (4,)
ROOM = 224


def ring(n, shift):
    return [(i, (i + shift) % n) for i in range(n)]


def params(mib):
    return pltpu.CompilerParams(vmem_limit_bytes=mib * 1024 * 1024)


def split(x):
    high = x.astype(jnp.bfloat16)
    return high, (x - high.astype(jnp.float32)).astype(jnp.bfloat16)


def dot(former, latter):
    return jnp.dot(former, latter, preferred_element_type=jnp.float32)


def dot3(high, low, former, latter):
    return dot(high, former) + dot(high, latter) + dot(low, former)


def plan_kernel(place, pairs_ref, owners_ref, out_ref):
    size = 256
    down = lax.broadcasted_iota(jnp.int32, (size, size), 0)
    across = lax.broadcasted_iota(jnp.int32, (size, size), 1)
    one = lambda condition: jnp.where(condition, 1.0, 0.0)
    to_row = lambda column: jnp.sum(jnp.where(down == across, column, 0.0), axis=0, keepdims=True)
    to_column = lambda row: jnp.sum(jnp.where(down == across, row, 0.0), axis=1, keepdims=True)
    rows, columns = down.astype(jnp.float32), across.astype(jnp.float32)
    left, right = pairs_ref[:, 0:1].astype(jnp.float32), pairs_ref[:, 1:2].astype(jnp.float32)
    owner_row = owners_ref[...].astype(jnp.float32)
    owner = to_column(owner_row)

    used = jnp.max(one(right == columns), axis=0, keepdims=True)
    used_column = to_column(used)
    rank = jnp.sum(jnp.where(columns < rows, used, 0.0), axis=1, keepdims=True)
    used_list = jnp.sum(jnp.where((rank == columns) & (used_column > 0), rows, 0.0), axis=0, keepdims=True)
    right_rank = jnp.sum(jnp.where(columns < right, used, 0.0), axis=1, keepdims=True)

    parity = lambda value: value - 2.0 * jnp.floor(value * 0.5)
    count = jnp.sum(one(owner == columns), axis=0, keepdims=True)
    same = parity(rows) == parity(columns)
    offset = jnp.sum(jnp.where((rows < columns) & same, to_column(count), 0.0), axis=0, keepdims=True)
    ahead = (owner_row < owner) | ((owner_row == owner) & (across < down))
    ahead = ahead & (parity(owner_row) == parity(owner))
    position = jnp.sum(one(ahead), axis=1, keepdims=True)

    core = place[3].astype(jnp.float32)
    local = right_rank - core * (USED // 2)
    here = (local >= 0) & (local < USED // 2)
    local = jnp.where(here, local, 0.0)
    lane = lax.broadcasted_iota(jnp.int32, (1, size), 1)
    groups = jnp.zeros((1, size), jnp.float32)
    for half in range(2):
        hit = (position == columns) & (parity(owner) == half)
        pick = lambda column: jnp.sum(jnp.where(hit, column, 0.0), axis=0, keepdims=True).astype(jnp.int32)
        at = pick(local)
        out_ref[4 * half : 4 * half + 1, :] = pick(left) * BLK
        out_ref[4 * half + 1 : 4 * half + 2, :] = at // 8 * 128
        out_ref[4 * half + 2 : 4 * half + 3, :] = (lane + 8 - at % 8) % 8 * BLK
        out_ref[4 * half + 3 : 4 * half + 4, :] = jnp.where(pick(one(here)) > 0, lane % 8, -1)
        total = jnp.sum(one(parity(owner_row) == half))
        groups = jnp.where(lane == half, jnp.floor((total + 7.0) / 8.0), groups)
    for at, row in enumerate((offset, count, used_list, groups)):
        out_ref[8 + at : 9 + at, :] = row.astype(jnp.int32)


def plan_call(place, pairs, owners):
    return pl.pallas_call(
        plan_kernel,
        out_shape=jax.ShapeDtypeStruct((16, pairs.shape[0]), jnp.int32),
        in_specs=[SMEM, VMEM, VMEM],
        out_specs=VMEM,
        compiler_params=params(8),
        name="plan",
    )(place, pairs, owners)


def padded(planes):
    return (len(planes) * PLANE + 127) // 128 * 128


def screen_kernel(place, own_ref, other_ref, *outs):
    z = place[0]
    rows = 16
    lane = lax.broadcasted_iota(jnp.int32, (rows, 128), 1)

    def plane_of(ref, row, delta, offset):
        plane = lax.rem(z + delta, 8)
        odd = lax.rem(plane, 2)
        column = pl.multiple_of(plane * PLANE - odd * 64, 128)
        window = ref[row, pl.ds(column, 384)]
        turned = pltpu.roll(window, 64 if offset else 320, 1)
        return jnp.where((odd == 1) if offset else (odd == 0), window, turned)

    for source, ref in enumerate((own_ref, other_ref)):

        def body(step, carry, source=source, ref=ref):
            part = step // 10
            row = pl.ds(pl.multiple_of(step * rows, rows), rows)
            target = pl.multiple_of(part * PLANE + source * (PLANE // 2) + (step - part * 10) * rows, rows)
            for group, planes in enumerate((NEAR, MIDDLE, FAR)):
                for at in range(0, len(planes), 2):
                    a = plane_of(ref, row, planes[at], False)
                    if at + 1 < len(planes):
                        b = plane_of(ref, row, planes[at + 1], True)
                        middle = jnp.where(lane < 64, a[:, 256:], b[:, :128])
                        whole = jnp.concatenate([a[:, :256], middle, b[:, 128:]], axis=1)
                    else:
                        whole = jnp.concatenate([a[:, :256], jnp.where(lane < 64, a[:, 256:], 0.0)], axis=1)
                    top, rest = split(whole)
                    columns = slice(at * PLANE, at * PLANE + whole.shape[1])
                    outs[2 * group][pl.ds(target, rows), columns] = top
                    outs[2 * group + 1][pl.ds(target, rows), columns] = rest
            return carry

        lax.fori_loop(0, 20, body, 0)


def screen_call(place, own, other):
    shapes = [
        jax.ShapeDtypeStruct((2 * own.shape[0], padded(planes)), jnp.bfloat16)
        for planes in (NEAR, MIDDLE, FAR)
        for _ in range(2)
    ]
    return pl.pallas_call(
        screen_kernel,
        out_shape=shapes,
        in_specs=[SMEM, VMEM, VMEM],
        out_specs=[VMEM] * 6,
        compiler_params=params(20),
        name="screen",
    )(place, own, other)


def left_kernel(place, *refs):
    pieces, (high_ref, low_ref, work) = refs[:8], refs[8:]
    x = place[1]
    span = pieces[0].shape[0] // 2
    for core in range(2):
        for shift in range(4):
            shard = lax.rem(x - shift + 4, 4)
            for part in range(2):
                row = pl.multiple_of(part * 8 * span + core * 4 * span + shard * span, 8)
                work[pl.ds(row, span), :] = pieces[core * 4 + shift][part * span : (part + 1) * span, :]

    def body(block, carry):
        at = pl.ds(pl.multiple_of(block * 128, 128), 128)
        high_ref[at, :], low_ref[at, :] = split(work[:, at].T)
        return carry

    lax.fori_loop(0, work.shape[1] // 128, body, 0)


def left_call(place, pieces):
    depth, width = pieces[0].shape
    shape = jax.ShapeDtypeStruct((width, 8 * depth), jnp.bfloat16)
    return pl.pallas_call(
        left_kernel,
        out_shape=(shape, shape),
        in_specs=[SMEM] + [VMEM] * 8,
        out_specs=(VMEM, VMEM),
        scratch_shapes=[pltpu.VMEM((8 * depth, width), jnp.float32)],
        compiler_params=params(20),
        name="left",
    )(place, *pieces)


def load_right(place, runs, planes, high, low):
    y = place[2]
    for delta, ref, start, first, count in runs:
        spread = lax.rem(y + delta, 4) * SPAN

        def body(step, carry, ref=ref, start=start, first=first, spread=spread):
            unit = first + step
            row = pl.ds(pl.multiple_of(unit // 2 * PLANE + spread, 16), SPAN)
            column = pl.ds(pl.multiple_of(lax.rem(unit, 2) * HALF, HALF), HALF)
            top, rest = split(ref[pl.ds(pl.multiple_of(start + step * SPAN, 8), SPAN), :])
            high[row, column] = top
            low[row, column] = rest
            return carry

        lax.fori_loop(0, count, body, 0)
    used = planes * PLANE
    if used < high.shape[0]:
        for ref in (high, low):
            ref[used:, :] = jnp.zeros((ref.shape[0] - used, ref.shape[1]), ref.dtype)


def near_runs(first, first_down, first_up, second, second_down, second_up, two_down, two_up):
    skip = 3 * SPAN
    return (
        ((0, first, 0, 0, 6), (3, first_down, 0, 0, 6), (1, first_up, 0, 0, 6))
        + ((0, second, 0, 6, 4), (3, second_down, 0, 6, 4), (1, second_up, 0, 6, 4))
        + ((2, two_down, 0, 0, 3), (2, two_up, 0, 3, 3), (2, two_down, skip, 6, 2), (2, two_up, skip, 8, 2))
    )


def middle_runs(z_below, z_above, y_below, y_above):
    runs = ()
    for first, sides, across in ((0, z_below, y_below), (2, z_above, y_above)):
        runs += ((3, sides, 0, first, 2), (1, sides, 2 * SPAN, first, 2), (0, sides, 4 * SPAN, first, 2))
        runs += ((2, across, 0, first, 2),)
    return runs


def far_runs(below, above, across_low, across_high):
    return (
        ((3, below, 0, 0, 2), (1, above, 0, 0, 2), (0, below, 2 * SPAN, 0, 1), (0, above, 2 * SPAN, 1, 1))
        + ((2, across_low, 0, 0, 1), (2, across_high, 0, 1, 1))
    )


def group_kernel(runs, planes, place, *refs):
    count = len(refs) - 5 - (runs is middle_runs)
    rights, (high_ref, low_ref), rest = refs[:count], refs[count : count + 2], refs[count + 2 :]
    out_ref, rh, rl = rest[-3:]
    load_right(place, runs(*rights), planes, rh, rl)
    value = dot3(high_ref[...], low_ref[...], rh[...], rl[...])
    out_ref[...] = value if len(rest) == 3 else value + rest[0][...]


def group_call(runs, planes, place, rights, screens, total):
    rows, width = screens[0].shape
    return pl.pallas_call(
        functools.partial(group_kernel, runs, planes),
        out_shape=jax.ShapeDtypeStruct((rows, 2 * HALF), jnp.float32),
        in_specs=[SMEM] + [VMEM] * (len(rights) + 2 + len(total)),
        out_specs=VMEM,
        scratch_shapes=[pltpu.VMEM((width, 2 * HALF), jnp.bfloat16)] * 2,
        compiler_params=params(32),
        name="group",
    )(place, *rights, *screens, *total)


def pair_kernel(place, table, *refs):
    rights, (high_ref, low_ref, sum_ref, left_high, left_low, give_ref, kern, rh, rl) = refs[:4], refs[4:]
    load_right(place, far_runs(*rights), len(FAR), rh, rl)
    product = sum_ref[...] + dot3(high_ref[...], low_ref[...], rh[...], rl[...])
    mid = product.shape[0] // 2
    real = product[:mid, :HALF] - product[mid:, HALF:]
    imag = product[mid:, :HALF] + product[:mid, HALF:]
    applied = NG ** (-0.5) * jnp.concatenate(
        [jnp.concatenate([real, imag], axis=0), jnp.concatenate([imag, -real], axis=0)], axis=1
    )
    kern[...] = dot3(left_high[...], left_low[...], *split(applied))

    extract(place, table, 1 - place[3], kern, give_ref)


def extract(place, table, half, kern, out_ref):
    at = lambda x: lax.rem(x + 4 - place[1], 4)
    lane = lax.broadcasted_iota(jnp.int32, (8, 128), 1) // BLK
    upper = lax.broadcasted_iota(jnp.int32, (8, 128), 0) < 4

    def groups(pair, carry):
        for g in (pair * 2, pair * 2 + 1):
            tiles = [[jnp.zeros((8, 128), jnp.float32) for _ in range(2)] for _ in range(2)]
            for u in range(8):
                slot = g * 8 + u
                row = pl.multiple_of(table[4 * half, slot], BLK)
                column = pl.multiple_of(table[4 * half + 1, slot], 128)
                shift = table[4 * half + 2, slot]
                target = table[4 * half + 3, slot]
                for part in range(2):
                    for side in range(2):
                        tile = kern[pl.ds(row + side * 8, 8), pl.ds(column + part * HALF, 128)]
                        tile = pltpu.roll(tile, shift, 1)
                        tiles[part][side] = jnp.where(lane == target, tile, tiles[part][side])
            lanes = pl.ds(pl.multiple_of(g * 128, 128), 128)
            for side in range(2):
                real, imag = tiles[0][side], tiles[1][side]
                out_ref[at(2 * side), :, lanes] = jnp.where(upper, real, pltpu.roll(imag, 4, 0))
                out_ref[at(2 * side + 1), :, lanes] = jnp.where(upper, pltpu.roll(real, 4, 0), imag)
        return carry

    out_ref[...] = jnp.zeros_like(out_ref)
    lax.fori_loop(0, (table[11, half] + 1) // 2, groups, 0)


def pair_call(place, table, rights, screens, total, left_high, left_low):
    rows = left_high.shape[0]
    return pl.pallas_call(
        pair_kernel,
        out_shape=(
            jax.ShapeDtypeStruct((4, 8, ROOM * BLK), jnp.float32),
            jax.ShapeDtypeStruct((rows, 2 * HALF), jnp.float32),
        ),
        in_specs=[SMEM, SMEM] + [VMEM] * (len(rights) + 5),
        out_specs=(VMEM, VMEM),
        scratch_shapes=[pltpu.VMEM((screens[0].shape[1], 2 * HALF), jnp.bfloat16)] * 2,
        compiler_params=params(24),
        name="pair",
    )(place, table, *rights, *screens, total, left_high, left_low)


def extract_kernel(place, table, kern, out_ref):
    extract(place, table, place[3], kern, out_ref)


def extract_call(place, table, kern):
    return pl.pallas_call(
        extract_kernel,
        out_shape=jax.ShapeDtypeStruct((4, 8, ROOM * BLK), jnp.float32),
        in_specs=[SMEM, SMEM, VMEM],
        out_specs=VMEM,
        compiler_params=params(8),
        name="extract",
    )(place, table, kern)


def add_kernel(one_ref, two_ref, *outs):
    for at, out_ref in enumerate(outs):
        out_ref[...] = one_ref[at] + two_ref[at]


def add_call(one, two):
    return pl.pallas_call(
        add_kernel,
        out_shape=[jax.ShapeDtypeStruct(one.shape[1:], one.dtype)] * one.shape[0],
        in_specs=[VMEM, VMEM],
        out_specs=[VMEM] * one.shape[0],
        compiler_params=params(8),
        name="add",
    )(one, two)


def owner_kernel(place, table, one_ref, two_ref, three_ref, four_ref, out_ref, work):
    total = (one_ref[...] + two_ref[...]) + (three_ref[...] + four_ref[...])
    width = total.shape[1]
    work[:, :width] = total
    work[:, width:] = jnp.zeros((8, work.shape[1] - width), jnp.float32)
    for chip in range(out_ref.shape[0]):
        start = table[8, chip * 2 + place[3]]
        column = pl.multiple_of(start // 8 * 128, 128)
        shift = lax.rem(384 - lax.rem(start, 8) * BLK, 384)
        out_ref[chip] = pltpu.roll(work[:, pl.ds(column, 384)], shift, 1)[:, :256]


def owner_call(place, table, parts):
    return pl.pallas_call(
        owner_kernel,
        out_shape=jax.ShapeDtypeStruct((32, 8, 256), jnp.float32),
        in_specs=[SMEM, SMEM] + [VMEM] * 4,
        out_specs=VMEM,
        scratch_shapes=[pltpu.VMEM((8, parts[0].shape[1] + 384), jnp.float32)],
        compiler_params=params(8),
        name="owner",
    )(place, table, *parts)


def last_kernel(place, table, parts_ref, out_ref):
    total = parts_ref[0]
    for chip in range(1, parts_ref.shape[0]):
        total = total + parts_ref[chip]
    held = table[9, (place[0] * 4 + place[2]) * 2 + place[3]]
    for slot in range(CAP):
        tile = total[:, slot // 8 * 128 : slot // 8 * 128 + 128]
        tile = pltpu.roll(tile, (128 - slot % 8 * BLK) % 128, 1)
        out_ref[slot] = jnp.where(slot < held, tile[:, :BLK], 0.0)


def last_call(place, table, parts):
    return pl.pallas_call(
        last_kernel,
        out_shape=jax.ShapeDtypeStruct((CAP, 8, BLK), jnp.float32),
        in_specs=[SMEM, SMEM, VMEM],
        out_specs=VMEM,
        compiler_params=params(8),
        name="last",
    )(place, table, parts)


def pack_kernel(place, own_ref, other_ref, out_ref, work):
    core = place[3]
    width = own_ref.shape[2]
    for block in range(width // 128):
        lanes = pl.ds(block * 128, 128)
        rows = []
        for part in range(2):
            own, other = own_ref[part, :, lanes], other_ref[part, :, lanes]
            rows += [jnp.where(core == 0, own, other), jnp.where(core == 0, other, own)]
        rows = jnp.concatenate(rows + rows, axis=0)
        work[block * 128 : (block + 1) * 128, :] = rows.T
    half = lax.broadcasted_iota(jnp.int32, (8, 128), 1) < 64
    for chip in range(32):
        at = pl.multiple_of(chip * 80 + core * 40, 8)
        tiles = [work[pl.ds(at + 8 * t, 8), :] for t in range(5)]
        out_ref[chip * 20 : chip * 20 + 8, :] = jnp.where(half, tiles[0], tiles[1])
        out_ref[chip * 20 + 8 : chip * 20 + 16, :] = jnp.where(half, tiles[2], tiles[3])
        last = jnp.where(half, tiles[4], pltpu.roll(tiles[4], 4, 0))
        out_ref[chip * 20 + 16 : chip * 20 + 20, :] = last[:4]


def pack_call(place, own, other):
    width = own.shape[2]
    return pl.pallas_call(
        pack_kernel,
        out_shape=jax.ShapeDtypeStruct((32 * 20, 128), jnp.float32),
        in_specs=[SMEM, VMEM, VMEM],
        out_specs=VMEM,
        scratch_shapes=[pltpu.VMEM((width, 128), jnp.float32)],
        name="pack",
    )(place, own, other)


def unpack_kernel(place, table, in_ref, columns_ref, keep_ref, give_ref):
    core = place[3]
    quarter = lax.broadcasted_iota(jnp.int32, (8, 128), 1) // 32
    upper = lax.broadcasted_iota(jnp.int32, (8, 128), 0) < 4
    for group in range(8):
        tiles = [[None] * 5 for _ in range(2)]
        for u in range(4):
            at = (group * 4 + u) * 20
            one, two = in_ref[at : at + 8, :], in_ref[at + 8 : at + 16, :]
            end = in_ref[at + 12 : at + 20, :]
            end = jnp.where(upper, pltpu.roll(end, 4, 0), pltpu.roll(end, 64, 1))
            for t, (source, first) in enumerate(((one, 0), (one, 64), (two, 0), (two, 64), (end, 0))):
                for part in range(2):
                    by = (u * 32 - first - part * 32) % 128
                    turned = pltpu.roll(source, by, 1) if by else source
                    old = tiles[part][t]
                    tiles[part][t] = turned if old is None else jnp.where(quarter == u, turned, old)
        for part in range(2):
            for t in range(5):
                row = part * 40 + t * 8
                columns_ref[row : row + 8, group * 128 : (group + 1) * 128] = tiles[part][t]
    select(table, 1 - core, columns_ref, give_ref)
    select(table, core, columns_ref, keep_ref)


def select(table, which, columns_ref, out_ref):
    eighth = lax.broadcasted_iota(jnp.int32, (80, 128), 1) // BLK
    for group in range(2):
        slab = None
        for u in range(8):
            block = table[10, which * (USED // 2) + group * 8 + u]
            column = pl.multiple_of(block // 8 * 128, 128)
            by = lax.rem(u * BLK + 128 - lax.rem(block, 8) * BLK, 128)
            turned = pltpu.roll(columns_ref[:, pl.ds(column, 128)], by, 1)
            slab = turned if slab is None else jnp.where(eighth == u, turned, slab)
        out_ref[:, group * 128 : (group + 1) * 128] = slab


def unpack_call(place, table, pieces):
    return pl.pallas_call(
        unpack_kernel,
        out_shape=(
            jax.ShapeDtypeStruct((80, 1024), jnp.float32),
            jax.ShapeDtypeStruct((80, HALF), jnp.float32),
            jax.ShapeDtypeStruct((80, HALF), jnp.float32),
        ),
        in_specs=[SMEM, SMEM, VMEM],
        out_specs=(VMEM, VMEM, VMEM),
        compiler_params=params(8),
        name="unpack",
    )(place, table, pieces)


def shard_kernel(place, keep_ref, take_ref, out_ref):
    core = place[3]
    for part in range(2):
        out_ref[pl.ds(pl.multiple_of(part * 80 + core * 40, 8), 40), :] = keep_ref[part * 40 : part * 40 + 40, :]
        out_ref[pl.ds(pl.multiple_of(part * 80 + 40 - core * 40, 8), 40), :] = take_ref[part * 40 : part * 40 + 40, :]


def shard_call(place, keep, take):
    return pl.pallas_call(
        shard_kernel,
        out_shape=jax.ShapeDtypeStruct((160, HALF), jnp.float32),
        in_specs=[SMEM, VMEM, VMEM],
        out_specs=VMEM,
        compiler_params=params(8),
        name="shard",
    )(place, keep, take)


def after(array, *others):
    return lax.optimization_barrier((array, *others))[0]


def shards(densities, screened, pairs, owners):
    span = screened.shape[2]
    place = jnp.stack([lax.axis_index(axis) for axis in ("z", "x", "y", "core")]).astype(jnp.int32)
    shift = lambda array, axis, by: lax.ppermute(array, axis, ring(lax.axis_size(axis), by))
    swap = lambda array: lax.ppermute(array, "core", SWAP)
    join = lambda *arrays: jnp.concatenate(arrays, axis=0)
    hold = lax.optimization_barrier

    pieces = pack_call(place, densities, swap(densities))
    table = plan_call(place, after(pairs, pieces), owners.reshape(1, -1))
    mine = lax.all_to_all(pieces.reshape(32, 1, -1), ("z", "y"), 0, 0, tiled=True).reshape(pieces.shape)

    screen = screened.reshape(2 * 4 * span, -1)
    mine, other = hold((mine, swap(after(screen, pieces))))

    columns, keep, give = unpack_call(place, table, mine)
    shard = shard_call(place, keep, swap(give))

    block = 2 * SPAN
    below2, above2 = shift(shard, "z", 2), shift(shard, "z", -2)
    below, above, columns = hold((shift(shard, "z", 1), shift(shard, "z", -1), columns))
    first = join(shard, below, above)
    first_down, first_up = shift(first, "y", 1), shift(first, "y", -1)
    around = [columns, shift(columns, "x", 1), None, None]
    below2, above2, first, columns = hold((below2, above2, first, columns))
    second = join(below2, above2)
    second_down, second_up = shift(second, "y", 1), shift(second, "y", -1)
    around[3] = shift(columns, "x", 3)
    screens = screen_call(place, after(screen, second), other)
    first_down, first_up, around[1], below2, above2, *screens = hold(
        (first_down, first_up, around[1], below2, above2, *screens)
    )
    around[2] = shift(after(columns, first_down), "x", 2)
    swapped = [swap(columns), swap(around[1]), None, None]
    second_down, second_up, first_down, swapped[0], swapped[1] = hold(
        (second_down, second_up, first_down, swapped[0], swapped[1])
    )

    z_below = shift(join(second_down[:block], second_up[:block], second[:block]), "z", 1)
    z_above = shift(join(second_down[block:], second_up[block:], second[block:]), "z", -1)
    two_down = shift(join(first_down[: 3 * SPAN], second_down[:block]), "y", 1)
    two_up = shift(join(first_up[3 * SPAN :], second_up[block:]), "y", -1)
    swapped[3] = swap(around[3])
    two_down, two_up, z_below, z_above, around[2], swapped[3] = hold(
        (two_down, two_up, z_below, z_above, around[2], swapped[3])
    )

    y_below, y_above = shift(z_below[:block], "y", 1), shift(z_above[block : 2 * block], "y", -1)
    far_below = shift(join(z_below[:block], z_below[2 * block : 2 * block + SPAN]), "z", 1)
    far_above = shift(join(z_above[block : 2 * block], z_above[2 * block + SPAN :]), "z", -1)
    rights = (first, first_down, first_up, second, second_down, second_up, two_down, two_up)
    total = group_call(near_runs, len(NEAR), place, rights, screens[:2], ())
    swapped[2] = swap(around[2])
    y_below, y_above, far_below, far_above, total, swapped[2] = hold(
        (y_below, y_above, far_below, far_above, total, swapped[2])
    )

    across_low, across_high = shift(far_below[:SPAN], "y", 1), shift(far_above[SPAN : 2 * SPAN], "y", -1)
    rights = (z_below, z_above, y_below, y_above)
    total = group_call(middle_runs, len(MIDDLE), place, rights, screens[2:4], (total,))
    left_high, left_low = left_call(place, around + swapped)
    across_low, across_high, total, left_high, left_low = hold((across_low, across_high, total, left_high, left_low))
    rights = (far_below, far_above, across_low, across_high)
    give, kern = pair_call(place, table, rights, screens[4:], total, left_high, left_low)

    parts = add_call(extract_call(place, table, kern), swap(give))
    parts = [parts[0]] + [shift(parts[by], "x", by) for by in (1, 2, 3)]
    parts = owner_call(place, table, parts)
    parts = lax.all_to_all(parts, ("z", "y"), 0, 0, tiled=True)
    return last_call(place, table, parts).reshape(1, CAP, 2, 4, BLK)


def solution(mesh):
    fine = Mesh(mesh.devices.reshape(8, 4, 2, 4), ("z", "y", "core", "x"))
    in_specs = (P(None, BAND, "x"), P(None, None, BAND, "x"), P(), P())
    out_specs = P(BAND, None, None, "x", None)
    return jax.shard_map(shards, mesh=fine, in_specs=in_specs, out_specs=out_specs, check_vma=False)
```

profile of v0, /device:TPU:2, one launch (start us, length us, event | category | flops | bytes accessed | tf_op | source)
XLA Modules:
  0.0 156.1 jit_solution(4967266251691423234)
XLA Ops:
  2.0 2.2 %pack.1 = f32[640,128]{1,0:T(8,128)} custom-call(s32[4]{0:T(128)} %pad_add_fusion.place, f32[2,16,2560]{2,1,0:T(8,128)} %own_ref.1, f32[2,16,2560]{2,1,0:T(8,128)} %collective-permute-done.other_ref), custom_call_target="tpu_custom_call" | custom-call | tf_op jit(solution)/shard_map/pack/pallas_call | solution.py:424
  4.4 11.6 %all-to-all-start = ((f32[32,1,2560]{2,1,0:T(1,128)}), f32[32,1,2560]{2,1,0:T(1,128)}, u32[]{:S(2)}, u32[]{:S(2)}) async-start(f32[32,1,2560]{2,1,0:T(1,128)} %bitcast.12), calls=%async_computation | async-start | bytes 655360 | tf_op jit(solution)/shard_map/all_to_all | solution.py:519
  19.4 11.4 %all-to-all-done = f32[32,1,2560]{2,1,0:T(1,128)} async-done(((f32[32,1,2560]{2,1,0:T(1,128)}), f32[32,1,2560]{2,1,0:T(1,128)}, u32[]{:S(2)}, u32[]{:S(2)}) %all-to-all-start) | async-done | bytes 327712 | tf_op jit(solution)/shard_map/all_to_all | solution.py:519
  31.5 2.5 %unpack.1 = (f32[80,1024]{1,0:T(8,128)S(1)}, f32[80,256]{1,0:T(8,128)S(1)}, f32[80,256]{1,0:T(8,128)S(1)}) custom-call(s32[4]{0:T(128)S(1)} %copy-done.2, s32[16,256]{1,0:T(8,128)S(1)} %plan.1.table, f32[640,128]{1,0:T(8,128)} %bitcast.6.in_ref), custom_call_target="tpu_custom_call" | custom-call | tf_op jit(solution)/shard_map/unpack/pallas_call | solution.py:473
  36.2 1.8 %collective-permute-start.5 = (f32[160,256]{1,0:T(8,128)S(1)}, f32[160,256]{1,0:T(8,128)S(1)}, u32[]{:S(2)}, u32[]{:S(2)}) collective-permute-start(f32[160,256]{1,0:T(8,128)S(1)} %shard.1), channel_id=1, source_target_pairs={{0,32},{32,64},{64,96},{96,128},{128,160},{160,192},{192,224},{224... | collective-permute-start | bytes 491528 | tf_op jit(solution)/shard_map/ppermute | solution.py:512
  38.0 4.2 %collective-permute-done.6 = f32[160,256]{1,0:T(8,128)S(1)} collective-permute-done((f32[160,256]{1,0:T(8,128)S(1)}, f32[160,256]{1,0:T(8,128)S(1)}, u32[]{:S(2)}, u32[]{:S(2)}) %collective-permute-start.6) | collective-permute-done | bytes 163872 | tf_op jit(solution)/shard_map/ppermute | solution.py:512
  45.7 2.9 %collective-permute-start.3 = (f32[160,256]{1,0:T(8,128)S(1)}, f32[160,256]{1,0:T(8,128)S(1)}, u32[]{:S(2)}, u32[]{:S(2)}) collective-permute-start(f32[160,256]{1,0:T(8,128)S(1)} %shard.1), channel_id=1, source_target_pairs={{0,64},{32,96},{64,128},{96,160},{128,192},{160,224},{192,0},{224,... | collective-permute-start | bytes 491528 | tf_op jit(solution)/shard_map/ppermute | solution.py:512
  48.6 1.5 collective-permute-start.11
  50.1 4.5 %collective-permute-done.4 = f32[160,256]{1,0:T(8,128)S(1)} collective-permute-done((f32[160,256]{1,0:T(8,128)S(1)}, f32[160,256]{1,0:T(8,128)S(1)}, u32[]{:S(2)}, u32[]{:S(2)}) %collective-permute-start.4) | collective-permute-done | bytes 163872 | tf_op jit(solution)/shard_map/ppermute | solution.py:512
  55.9 2.4 %collective-permute-start.8 = (f32[320,256]{1,0:T(8,128)S(1)}, f32[320,256]{1,0:T(8,128)S(1)}, u32[]{:S(2)}, u32[]{:S(2)}) collective-permute-start(f32[320,256]{1,0:T(8,128)S(1)} %constant_dynamic-update-slice_fusion.refs_3_), channel_id=1, source_target_pairs={{0,24},{8,0},{16,8},{24,16},{1,25},{9,1},{17,9},{25,17},{2,26},{10... | collective-permute-start | bytes 983048 | tf_op jit(solution)/shard_map/ppermute | solution.py:512
  58.4 7.4 %screen.1 = (bf16[640,1664]{1,0:T(8,128)(2,1)S(1)}, bf16[640,1664]{1,0:T(8,128)(2,1)S(1)}, bf16[640,640]{1,0:T(8,128)(2,1)S(1)}, bf16[640,640]{1,0:T(8,128)(2,1)...) custom-call(s32[4]{0:T(128)S(1)} %copy-done.3, f32[320,2560]{1,0:T(8,128)S(1)} %bitcast.10, ...), custom_call_target="tpu_custom_call" | custom-call | tf_op jit(solution)/shard_map/screen/pallas_call | solution.py:153
  66.9 6.8 %collective-permute-done.19.refs_3_ = f32[80,1024]{1,0:T(8,128)S(1)} collective-permute-done((f32[80,1024]{1,0:T(8,128)S(1)}, f32[80,1024]{1,0:T(8,128)S(1)}, u32[]{:S(2)}, u32[]{:S(2)}) %collective-permute-start.19) | collective-permute-done | bytes 327712 | tf_op jit(solution)/shard_map/ppermute | solution.py:512
  74.0 2.1 %collective-permute-start.16 = (f32[480,256]{1,0:T(8,128)S(1)}, f32[480,256]{1,0:T(8,128)S(1)}, u32[]{:S(2)}, u32[]{:S(2)}) collective-permute-start(f32[480,256]{1,0:T(8,128)S(1)} %pad_maximum_fusion.1), channel_id=1, source_target_pairs={{0,32},{32,64},{64,96},{96,128},{128,160},{160,192},{192,224},{224... | collective-permute-start | bytes 1474568 | tf_op jit(solution)/shard_map/ppermute | solution.py:512
  76.2 3.0 %collective-permute-start.15 = (f32[400,256]{1,0:T(8,128)S(1)}, f32[400,256]{1,0:T(8,128)S(1)}, u32[]{:S(2)}, u32[]{:S(2)}) collective-permute-start(f32[400,256]{1,0:T(8,128)S(1)} %pad_maximum_fusion.4), channel_id=1, source_target_pairs={{0,24},{8,0},{16,8},{24,16},{1,25},{9,1},{17,9},{25,17},{2,26},{10... | collective-permute-start | bytes 1228808 | tf_op jit(solution)/shard_map/ppermute | solution.py:512
  79.2 3.3 %collective-permute-start.18 = (f32[80,1024]{1,0:T(8,128)S(1)}, f32[80,1024]{1,0:T(8,128)S(1)}, u32[]{:S(2)}, u32[]{:S(2)}) collective-permute-start(f32[80,1024]{1,0:T(8,128)S(1)} %get-tuple-element.92.refs_0_), channel_id=1, source_target_pairs={{0,2},{1,3},{2,0},{3,1},{4,6},{5,7},{6,4},{7,5},{8,10},{9,11},{10,... | collective-permute-start | bytes 983048 | tf_op jit(solution)/shard_map/ppermute | solution.py:512
  82.6 7.5 %collective-permute-done.18.refs_2_ = f32[80,1024]{1,0:T(8,128)S(1)} collective-permute-done((f32[80,1024]{1,0:T(8,128)S(1)}, f32[80,1024]{1,0:T(8,128)S(1)}, u32[]{:S(2)}, u32[]{:S(2)}) %collective-permute-start.18) | collective-permute-done | bytes 327712 | tf_op jit(solution)/shard_map/ppermute | solution.py:512
  91.6 1.7 %collective-permute-start.23 = (f32[240,256]{1,0:T(8,128)S(1)}, f32[240,256]{1,0:T(8,128)S(1)}, u32[]{:S(2)}, u32[]{:S(2)}) collective-permute-start(f32[240,256]{1,0:T(8,128)S(1)} %pad_maximum_fusion.5), channel_id=1, source_target_pairs={{0,32},{32,64},{64,96},{96,128},{128,160},{160,192},{192,224},{224... | collective-permute-start | bytes 737288 | tf_op jit(solution)/shard_map/ppermute | solution.py:512
  93.3 1.7 %collective-permute-start.24 = (f32[240,256]{1,0:T(8,128)S(1)}, f32[240,256]{1,0:T(8,128)S(1)}, u32[]{:S(2)}, u32[]{:S(2)}) collective-permute-start(f32[240,256]{1,0:T(8,128)S(1)} %pad_maximum_fusion.6), channel_id=1, source_target_pairs={{0,224},{32,0},{64,32},{96,64},{128,96},{160,128},{192,160},{224,1... | collective-permute-start | bytes 737288 | tf_op jit(solution)/shard_map/ppermute | solution.py:512
  95.0 1.6 %collective-permute-start.22 = (f32[160,256]{1,0:T(8,128)S(1)}, f32[160,256]{1,0:T(8,128)S(1)}, u32[]{:S(2)}, u32[]{:S(2)}) collective-permute-start(f32[160,256]{1,0:T(8,128)S(1)} %slice.47), channel_id=1, source_target_pairs={{0,24},{8,0},{16,8},{24,16},{1,25},{9,1},{17,9},{25,17},{2,26},{10... | collective-permute-start | bytes 491528 | tf_op jit(solution)/shard_map/ppermute | solution.py:512
  97.0 5.0 %group.2.refs_6_ = f32[640,512]{1,0:T(8,128)S(1)} custom-call(s32[4]{0:T(128)S(1)} %copy-done.3, f32[480,256]{1,0:T(8,128)S(1)} %pad_maximum_fusion.refs_0_, f32[480,256]{1,0:T(8,128)S(1)} %collective-permute-done.9.refs_1_, f32[480,256]{1,0:T(8,128)S(1)} %collective-permute-done.10.refs_2_, f32[320,256]{1,0:T(8,128)S(1)} %constant_dynamic-update-slice_fusion.refs_3_, ...), custom_call_target="tpu_custom_call" | custom-call | tf_op jit(solution)/shard_map/group/pallas_call | solution.py:252
  102.0 1.8 %collective-permute-done.21.refs_2_ = f32[160,256]{1,0:T(8,128)S(1)} collective-permute-done((f32[160,256]{1,0:T(8,128)S(1)}, f32[160,256]{1,0:T(8,128)S(1)}, u32[]{:S(2)}, u32[]{:S(2)}) %collective-permute-start.21) | collective-permute-done | bytes 163872 | tf_op jit(solution)/shard_map/ppermute | solution.py:512
  106.0 2.5 %group.3.refs_6_ = f32[640,512]{1,0:T(8,128)S(1)} custom-call(s32[4]{0:T(128)S(1)} %copy-done.3, f32[480,256]{1,0:T(8,128)S(1)} %collective-permute-done.16.refs_0_, f32[480,256]{1,0:T(8,128)S(1)} %collective-permute-done.17.refs_1_, f32[160,256]{1,0:T(8,128)S(1)} %collective-permute-done.21.refs_2_, f32[160,256]{1,0:T(8,128)S(1)} %collective-permute-done.22.refs_3_, ...), custom_call_target="tpu_custom_call" | custom-call | tf_op jit(solution)/shard_map/group/pallas_call | solution.py:252
  108.5 2.1 %left.1 = (bf16[1024,640]{1,0:T(8,128)(2,1)S(1)}, bf16[1024,640]{1,0:T(8,128)(2,1)S(1)}) custom-call(s32[4]{0:T(128)S(1)} %copy-done.3, f32[80,1024]{1,0:T(8,128)S(1)} %get-tuple-element.92.refs_0_, f32[80,1024]{1,0:T(8,128)S(1)} %collective-permute-done.11.refs_1_, f32[80,1024]{1,0:T(8,128)S(1)} %collective-permute-done.18.refs_2_, ...), custom_call_target="tpu_custom_call" | custom-call | tf_op jit(solution)/shard_map/left/pallas_call | solution.py:185
  110.7 9.1 %pair.1 = (f32[4,8,3584]{2,1,0:T(8,128)S(1)}, f32[1024,512]{1,0:T(8,128)S(1)}) custom-call(s32[4]{0:T(128)S(1)} %copy-done.3, s32[16,256]{1,0:T(8,128)S(1)} %plan.1.table, f32[240,256]{1,0:T(8,128)S(1)} %collective-permute-done.23.refs_0_, f32[240,256]{1,0:T(8,128)S(1)} %collective-permute-done.24.refs_1_, f32[80,256]{1,0:T(8,128)S(1)} %collective-permute-done.26.refs_2_, ...), custom_call_target="tpu_custom_call" | custom-call | tf_op jit(solution)/shard_map/pair/pallas_call | solution.py:310
  119.9 3.0 %extract.1.one_ref = f32[4,8,3584]{2,1,0:T(8,128)S(1)} custom-call(s32[4]{0:T(128)S(1)} %copy-done.3, s32[16,256]{1,0:T(8,128)S(1)} %plan.1.table, f32[1024,512]{1,0:T(8,128)S(1)} %get-tuple-element.121.kern), custom_call_target="tpu_custom_call" | custom-call | tf_op jit(solution)/shard_map/extract/pallas_call | solution.py:329
  123.0 1.5 collective-permute-start.29
  124.4 1.9 %collective-permute-start.30 = (f32[8,3584]{1,0:T(8,128)S(1)}, f32[8,3584]{1,0:T(8,128)S(1)}, u32[]{:S(2)}, u32[]{:S(2)}) collective-permute-start(f32[8,3584]{1,0:T(8,128)S(1)} %get-tuple-element.125), channel_id=1, source_target_pairs={{0,2},{1,3},{2,0},{3,1},{4,6},{5,7},{6,4},{7,5},{8,10},{9,11},{10,... | collective-permute-start | bytes 344072 | tf_op jit(solution)/shard_map/ppermute | solution.py:512
  126.4 2.5 %collective-permute-start.31 = (f32[8,3584]{1,0:T(8,128)S(1)}, f32[8,3584]{1,0:T(8,128)S(1)}, u32[]{:S(2)}, u32[]{:S(2)}) collective-permute-start(f32[8,3584]{1,0:T(8,128)S(1)} %get-tuple-element.126), channel_id=1, source_target_pairs={{0,3},{1,0},{2,1},{3,2},{4,7},{5,4},{6,5},{7,6},{8,11},{9,8},{10,9... | collective-permute-start | bytes 344072 | tf_op jit(solution)/shard_map/ppermute | solution.py:512
  128.9 3.0 %collective-permute-done.30.three_ref = f32[8,3584]{1,0:T(8,128)S(1)} collective-permute-done((f32[8,3584]{1,0:T(8,128)S(1)}, f32[8,3584]{1,0:T(8,128)S(1)}, u32[]{:S(2)}, u32[]{:S(2)}) %collective-permute-start.30) | collective-permute-done | bytes 114720 | tf_op jit(solution)/shard_map/ppermute | solution.py:512
  131.9 2.0 %collective-permute-done.31.four_ref = f32[8,3584]{1,0:T(8,128)S(1)} collective-permute-done((f32[8,3584]{1,0:T(8,128)S(1)}, f32[8,3584]{1,0:T(8,128)S(1)}, u32[]{:S(2)}, u32[]{:S(2)}) %collective-permute-start.31) | collective-permute-done | bytes 114720 | tf_op jit(solution)/shard_map/ppermute | solution.py:512
  135.2 19.4 %all_to_all.10.parts_ref = f32[32,8,256]{2,1,0:T(8,128)S(1)} all-to-all(f32[32,8,256]{2,1,0:T(8,128)S(1)} %owner.1), channel_id=1, replica_groups=mesh['z'=8,'y'=4,'core'=2,'x'=4] {'z','y'}, dimensions={0} | all-to-all | bytes 524288 | tf_op jit(solution)/shard_map/all_to_all | solution.py:577
  154.6 1.5 last.1
  (79 shorter events, 20.0 us)
Async XLA Ops:
  0.0 2.0 %collective-permute-start = (f32[2,16,2560]{2,1,0:T(8,128)}, f32[2,16,2560]{2,1,0:T(8,128)}, u32[]{:S(2)}, u32[]{:S(2)}) collective-permute-start(f32[2,16,2560]{2,1,0:T(8,128)} %own_ref.1), channel_id=1, source_target_pairs={{0,4},{4,0},{1,5},{5,1},{2,6},{6,2},{3,7},{7,3},{8,12},{12,8},{9,1... | collective-permute-start | bytes 983048 | tf_op jit(solution)/shard_map/ppermute | solution.py:513
  4.2 26.6 %collective-permute-start.1 = (f32[320,2560]{1,0:T(8,128)}, f32[320,2560]{1,0:T(8,128)}, u32[]{:S(2)}, u32[]{:S(2)}) collective-permute-start(f32[320,2560]{1,0:T(8,128)} %bitcast.9), channel_id=1, source_target_pairs={{0,4},{4,0},{1,5},{5,1},{2,6},{6,2},{3,7},{7,3},{8,12},{12,8},{9,1... | collective-permute-start | bytes 9830408 | tf_op jit(solution)/shard_map/ppermute | solution.py:513
  4.4 26.4 %all-to-all-start = ((f32[32,1,2560]{2,1,0:T(1,128)}), f32[32,1,2560]{2,1,0:T(1,128)}, u32[]{:S(2)}, u32[]{:S(2)}) async-start(f32[32,1,2560]{2,1,0:T(1,128)} %bitcast.12), calls=%async_computation | async-start | bytes 655360 | tf_op jit(solution)/shard_map/all_to_all | solution.py:519
  35.9 6.3 %collective-permute-start.6 = (f32[160,256]{1,0:T(8,128)S(1)}, f32[160,256]{1,0:T(8,128)S(1)}, u32[]{:S(2)}, u32[]{:S(2)}) collective-permute-start(f32[160,256]{1,0:T(8,128)S(1)} %shard.1), channel_id=1, source_target_pairs={{0,224},{32,0},{64,32},{96,64},{128,96},{160,128},{192,160},{224,1... | collective-permute-start | bytes 491528 | tf_op jit(solution)/shard_map/ppermute | solution.py:512
  36.2 7.4 %collective-permute-start.5 = (f32[160,256]{1,0:T(8,128)S(1)}, f32[160,256]{1,0:T(8,128)S(1)}, u32[]{:S(2)}, u32[]{:S(2)}) collective-permute-start(f32[160,256]{1,0:T(8,128)S(1)} %shard.1), channel_id=1, source_target_pairs={{0,32},{32,64},{64,96},{96,128},{128,160},{160,192},{192,224},{224... | collective-permute-start | bytes 491528 | tf_op jit(solution)/shard_map/ppermute | solution.py:512
  43.6 22.8 %collective-permute-start.10 = (f32[480,256]{1,0:T(8,128)S(1)}, f32[480,256]{1,0:T(8,128)S(1)}, u32[]{:S(2)}, u32[]{:S(2)}) collective-permute-start(f32[480,256]{1,0:T(8,128)S(1)} %pad_maximum_fusion.refs_0_), channel_id=1, source_target_pairs={{0,24},{8,0},{16,8},{24,16},{1,25},{9,1},{17,9},{25,17},{2,26},{10... | collective-permute-start | bytes 1474568 | tf_op jit(solution)/shard_map/ppermute | solution.py:512
  45.0 21.4 %collective-permute-start.9 = (f32[480,256]{1,0:T(8,128)S(1)}, f32[480,256]{1,0:T(8,128)S(1)}, u32[]{:S(2)}, u32[]{:S(2)}) collective-permute-start(f32[480,256]{1,0:T(8,128)S(1)} %pad_maximum_fusion.refs_0_), channel_id=1, source_target_pairs={{0,8},{8,16},{16,24},{24,0},{1,9},{9,17},{17,25},{25,1},{2,10},{10... | collective-permute-start | bytes 1474568 | tf_op jit(solution)/shard_map/ppermute | solution.py:512
  45.7 8.9 %collective-permute-start.4 = (f32[160,256]{1,0:T(8,128)S(1)}, f32[160,256]{1,0:T(8,128)S(1)}, u32[]{:S(2)}, u32[]{:S(2)}) collective-permute-start(f32[160,256]{1,0:T(8,128)S(1)} %shard.1), channel_id=1, source_target_pairs={{0,192},{32,224},{64,0},{96,32},{128,64},{160,96},{192,128},{224,1... | collective-permute-start | bytes 491528 | tf_op jit(solution)/shard_map/ppermute | solution.py:512
  45.7 10.2 %collective-permute-start.3 = (f32[160,256]{1,0:T(8,128)S(1)}, f32[160,256]{1,0:T(8,128)S(1)}, u32[]{:S(2)}, u32[]{:S(2)}) collective-permute-start(f32[160,256]{1,0:T(8,128)S(1)} %shard.1), channel_id=1, source_target_pairs={{0,64},{32,96},{64,128},{96,160},{128,192},{160,224},{192,0},{224,... | collective-permute-start | bytes 491528 | tf_op jit(solution)/shard_map/ppermute | solution.py:512
  48.6 17.1 %collective-permute-start.11 = (f32[80,1024]{1,0:T(8,128)S(1)}, f32[80,1024]{1,0:T(8,128)S(1)}, u32[]{:S(2)}, u32[]{:S(2)}) collective-permute-start(f32[80,1024]{1,0:T(8,128)S(1)} %get-tuple-element.92.refs_0_), channel_id=1, source_target_pairs={{0,1},{1,2},{2,3},{3,0},{4,5},{5,6},{6,7},{7,4},{8,9},{9,10},{10,1... | collective-permute-start | bytes 983048 | tf_op jit(solution)/shard_map/ppermute | solution.py:512
  55.9 17.8 %collective-permute-start.8 = (f32[320,256]{1,0:T(8,128)S(1)}, f32[320,256]{1,0:T(8,128)S(1)}, u32[]{:S(2)}, u32[]{:S(2)}) collective-permute-start(f32[320,256]{1,0:T(8,128)S(1)} %constant_dynamic-update-slice_fusion.refs_3_), channel_id=1, source_target_pairs={{0,24},{8,0},{16,8},{24,16},{1,25},{9,1},{17,9},{25,17},{2,26},{10... | collective-permute-start | bytes 983048 | tf_op jit(solution)/shard_map/ppermute | solution.py:512
  58.4 15.4 %collective-permute-start.7 = (f32[320,256]{1,0:T(8,128)S(1)}, f32[320,256]{1,0:T(8,128)S(1)}, u32[]{:S(2)}, u32[]{:S(2)}) collective-permute-start(f32[320,256]{1,0:T(8,128)S(1)} %constant_dynamic-update-slice_fusion.refs_3_), channel_id=1, source_target_pairs={{0,8},{8,16},{16,24},{24,0},{1,9},{9,17},{17,25},{25,1},{2,10},{10... | collective-permute-start | bytes 983048 | tf_op jit(solution)/shard_map/ppermute | solution.py:512
  65.8 8.0 %collective-permute-start.19 = (f32[80,1024]{1,0:T(8,128)S(1)}, f32[80,1024]{1,0:T(8,128)S(1)}, u32[]{:S(2)}, u32[]{:S(2)}) collective-permute-start(f32[80,1024]{1,0:T(8,128)S(1)} %get-tuple-element.92.refs_0_), channel_id=1, source_target_pairs={{0,3},{1,0},{2,1},{3,2},{4,7},{5,4},{6,5},{7,6},{8,11},{9,8},{10,9... | collective-permute-start | bytes 983048 | tf_op jit(solution)/shard_map/ppermute | solution.py:512
  66.4 7.4 %collective-permute-start.12 = (f32[80,1024]{1,0:T(8,128)S(1)}, f32[80,1024]{1,0:T(8,128)S(1)}, u32[]{:S(2)}, u32[]{:S(2)}) collective-permute-start(f32[80,1024]{1,0:T(8,128)S(1)} %get-tuple-element.92.refs_0_), channel_id=1, source_target_pairs={{0,4},{4,0},{1,5},{5,1},{2,6},{6,2},{3,7},{7,3},{8,12},{12,8},{9,1... | collective-permute-start | bytes 983048 | tf_op jit(solution)/shard_map/ppermute | solution.py:513
  66.4 7.4 %collective-permute-start.13 = (f32[80,1024]{1,0:T(8,128)S(1)}, f32[80,1024]{1,0:T(8,128)S(1)}, u32[]{:S(2)}, u32[]{:S(2)}) collective-permute-start(f32[80,1024]{1,0:T(8,128)S(1)} %collective-permute-done.11.refs_1_), channel_id=1, source_target_pairs={{0,4},{4,0},{1,5},{5,1},{2,6},{6,2},{3,7},{7,3},{8,12},{12,8},{9,1... | collective-permute-start | bytes 983048 | tf_op jit(solution)/shard_map/ppermute | solution.py:513
  73.7 5.5 %collective-permute-start.20 = (f32[80,1024]{1,0:T(8,128)S(1)}, f32[80,1024]{1,0:T(8,128)S(1)}, u32[]{:S(2)}, u32[]{:S(2)}) collective-permute-start(f32[80,1024]{1,0:T(8,128)S(1)} %collective-permute-done.19.refs_3_), channel_id=1, source_target_pairs={{0,4},{4,0},{1,5},{5,1},{2,6},{6,2},{3,7},{7,3},{8,12},{12,8},{9,1... | collective-permute-start | bytes 983048 | tf_op jit(solution)/shard_map/ppermute | solution.py:513
  73.9 17.6 %collective-permute-start.17 = (f32[480,256]{1,0:T(8,128)S(1)}, f32[480,256]{1,0:T(8,128)S(1)}, u32[]{:S(2)}, u32[]{:S(2)}) collective-permute-start(f32[480,256]{1,0:T(8,128)S(1)} %pad_maximum_fusion.2), channel_id=1, source_target_pairs={{0,224},{32,0},{64,32},{96,64},{128,96},{160,128},{192,160},{224,1... | collective-permute-start | bytes 1474568 | tf_op jit(solution)/shard_map/ppermute | solution.py:512
  74.0 17.4 %collective-permute-start.16 = (f32[480,256]{1,0:T(8,128)S(1)}, f32[480,256]{1,0:T(8,128)S(1)}, u32[]{:S(2)}, u32[]{:S(2)}) collective-permute-start(f32[480,256]{1,0:T(8,128)S(1)} %pad_maximum_fusion.1), channel_id=1, source_target_pairs={{0,32},{32,64},{64,96},{96,128},{128,160},{160,192},{192,224},{224... | collective-permute-start | bytes 1474568 | tf_op jit(solution)/shard_map/ppermute | solution.py:512
  76.2 13.9 %collective-permute-start.15 = (f32[400,256]{1,0:T(8,128)S(1)}, f32[400,256]{1,0:T(8,128)S(1)}, u32[]{:S(2)}, u32[]{:S(2)}) collective-permute-start(f32[400,256]{1,0:T(8,128)S(1)} %pad_maximum_fusion.4), channel_id=1, source_target_pairs={{0,24},{8,0},{16,8},{24,16},{1,25},{9,1},{17,9},{25,17},{2,26},{10... | collective-permute-start | bytes 1228808 | tf_op jit(solution)/shard_map/ppermute | solution.py:512
  79.2 12.2 %collective-permute-start.14 = (f32[400,256]{1,0:T(8,128)S(1)}, f32[400,256]{1,0:T(8,128)S(1)}, u32[]{:S(2)}, u32[]{:S(2)}) collective-permute-start(f32[400,256]{1,0:T(8,128)S(1)} %pad_maximum_fusion.3), channel_id=1, source_target_pairs={{0,8},{8,16},{16,24},{24,0},{1,9},{9,17},{17,25},{25,1},{2,10},{10... | collective-permute-start | bytes 1228808 | tf_op jit(solution)/shard_map/ppermute | solution.py:512
  79.2 10.9 %collective-permute-start.18 = (f32[80,1024]{1,0:T(8,128)S(1)}, f32[80,1024]{1,0:T(8,128)S(1)}, u32[]{:S(2)}, u32[]{:S(2)}) collective-permute-start(f32[80,1024]{1,0:T(8,128)S(1)} %get-tuple-element.92.refs_0_), channel_id=1, source_target_pairs={{0,2},{1,3},{2,0},{3,1},{4,6},{5,7},{6,4},{7,5},{8,10},{9,11},{10,... | collective-permute-start | bytes 983048 | tf_op jit(solution)/shard_map/ppermute | solution.py:512
  91.6 12.3 %collective-permute-start.23 = (f32[240,256]{1,0:T(8,128)S(1)}, f32[240,256]{1,0:T(8,128)S(1)}, u32[]{:S(2)}, u32[]{:S(2)}) collective-permute-start(f32[240,256]{1,0:T(8,128)S(1)} %pad_maximum_fusion.5), channel_id=1, source_target_pairs={{0,32},{32,64},{64,96},{96,128},{128,160},{160,192},{192,224},{224... | collective-permute-start | bytes 737288 | tf_op jit(solution)/shard_map/ppermute | solution.py:512
  93.3 10.6 %collective-permute-start.25 = (f32[80,1024]{1,0:T(8,128)S(1)}, f32[80,1024]{1,0:T(8,128)S(1)}, u32[]{:S(2)}, u32[]{:S(2)}) collective-permute-start(f32[80,1024]{1,0:T(8,128)S(1)} %collective-permute-done.18.refs_2_), channel_id=1, source_target_pairs={{0,4},{4,0},{1,5},{5,1},{2,6},{6,2},{3,7},{7,3},{8,12},{12,8},{9,1... | collective-permute-start | bytes 983048 | tf_op jit(solution)/shard_map/ppermute | solution.py:513
  93.3 10.6 %collective-permute-start.24 = (f32[240,256]{1,0:T(8,128)S(1)}, f32[240,256]{1,0:T(8,128)S(1)}, u32[]{:S(2)}, u32[]{:S(2)}) collective-permute-start(f32[240,256]{1,0:T(8,128)S(1)} %pad_maximum_fusion.6), channel_id=1, source_target_pairs={{0,224},{32,0},{64,32},{96,64},{128,96},{160,128},{192,160},{224,1... | collective-permute-start | bytes 737288 | tf_op jit(solution)/shard_map/ppermute | solution.py:512
  95.0 7.0 %collective-permute-start.22 = (f32[160,256]{1,0:T(8,128)S(1)}, f32[160,256]{1,0:T(8,128)S(1)}, u32[]{:S(2)}, u32[]{:S(2)}) collective-permute-start(f32[160,256]{1,0:T(8,128)S(1)} %slice.47), channel_id=1, source_target_pairs={{0,24},{8,0},{16,8},{24,16},{1,25},{9,1},{17,9},{25,17},{2,26},{10... | collective-permute-start | bytes 491528 | tf_op jit(solution)/shard_map/ppermute | solution.py:512
  96.6 7.3 %collective-permute-start.21 = (f32[160,256]{1,0:T(8,128)S(1)}, f32[160,256]{1,0:T(8,128)S(1)}, u32[]{:S(2)}, u32[]{:S(2)}) collective-permute-start(f32[160,256]{1,0:T(8,128)S(1)} %slice.46), channel_id=1, source_target_pairs={{0,8},{8,16},{16,24},{24,0},{1,9},{9,17},{17,25},{25,1},{2,10},{10... | collective-permute-start | bytes 491528 | tf_op jit(solution)/shard_map/ppermute | solution.py:512
  103.9 6.8 %collective-permute-start.27 = (f32[80,256]{1,0:T(8,128)S(1)}, f32[80,256]{1,0:T(8,128)S(1)}, u32[]{:S(2)}, u32[]{:S(2)}) collective-permute-start(f32[80,256]{1,0:T(8,128)S(1)} %slice.51), channel_id=1, source_target_pairs={{0,24},{8,0},{16,8},{24,16},{1,25},{9,1},{17,9},{25,17},{2,26},{10... | collective-permute-start | bytes 245768 | tf_op jit(solution)/shard_map/ppermute | solution.py:512
  105.0 5.7 %collective-permute-start.26 = (f32[80,256]{1,0:T(8,128)S(1)}, f32[80,256]{1,0:T(8,128)S(1)}, u32[]{:S(2)}, u32[]{:S(2)}) collective-permute-start(f32[80,256]{1,0:T(8,128)S(1)} %slice.50), channel_id=1, source_target_pairs={{0,8},{8,16},{16,24},{24,0},{1,9},{9,17},{17,25},{25,1},{2,10},{10... | collective-permute-start | bytes 245768 | tf_op jit(solution)/shard_map/ppermute | solution.py:512
  119.8 3.1 %collective-permute-start.28 = (f32[4,8,3584]{2,1,0:T(8,128)S(1)}, f32[4,8,3584]{2,1,0:T(8,128)S(1)}, u32[]{:S(2)}, u32[]{:S(2)}) collective-permute-start(f32[4,8,3584]{2,1,0:T(8,128)S(1)} %get-tuple-element.122), channel_id=1, source_target_pairs={{0,4},{4,0},{1,5},{5,1},{2,6},{6,2},{3,7},{7,3},{8,12},{12,8},{9,1... | collective-permute-start | bytes 1376264 | tf_op jit(solution)/shard_map/ppermute | solution.py:513
  123.0 6.0 %collective-permute-start.29 = (f32[8,3584]{1,0:T(8,128)S(1)}, f32[8,3584]{1,0:T(8,128)S(1)}, u32[]{:S(2)}, u32[]{:S(2)}) collective-permute-start(f32[8,3584]{1,0:T(8,128)S(1)} %get-tuple-element.124), channel_id=1, source_target_pairs={{0,1},{1,2},{2,3},{3,0},{4,5},{5,6},{6,7},{7,4},{8,9},{9,10},{10,1... | collective-permute-start | bytes 344072 | tf_op jit(solution)/shard_map/ppermute | solution.py:512
  124.4 7.5 %collective-permute-start.30 = (f32[8,3584]{1,0:T(8,128)S(1)}, f32[8,3584]{1,0:T(8,128)S(1)}, u32[]{:S(2)}, u32[]{:S(2)}) collective-permute-start(f32[8,3584]{1,0:T(8,128)S(1)} %get-tuple-element.125), channel_id=1, source_target_pairs={{0,2},{1,3},{2,0},{3,1},{4,6},{5,7},{6,4},{7,5},{8,10},{9,11},{10,... | collective-permute-start | bytes 344072 | tf_op jit(solution)/shard_map/ppermute | solution.py:512
  126.4 7.5 %collective-permute-start.31 = (f32[8,3584]{1,0:T(8,128)S(1)}, f32[8,3584]{1,0:T(8,128)S(1)}, u32[]{:S(2)}, u32[]{:S(2)}) collective-permute-start(f32[8,3584]{1,0:T(8,128)S(1)} %get-tuple-element.126), channel_id=1, source_target_pairs={{0,3},{1,0},{2,1},{3,2},{4,7},{5,4},{6,5},{7,6},{8,11},{9,8},{10,9... | collective-permute-start | bytes 344072 | tf_op jit(solution)/shard_map/ppermute | solution.py:512
  (6 other events, 88.0 us)
where the time goes:
time: 156 us
  waiting for transfers between devices  47.9 us (31%)
  starting transfers between devices  46.2 us (30%)
  Pallas kernels  38.5 us (25%)
  blocking collectives  19.4 us (12%)
  local copies, waits for them, and re-layouts  2.98 us (2%)
    ppermute x24, waiting for transfers between devices, shards(): lax.ppermute(array, axis, ring(lax.axis_size(axis), by))  33.9 us
    ppermute x24, starting transfers between devices, shards(): lax.ppermute(array, axis, ring(lax.axis_size(axis), by))  33.7 us
    all_to_all x1, blocking collectives, shards(): parts = lax.all_to_all(parts, ('z', 'y'), 0, 0, tiled=True)  19.4 us
    all_to_all x1, starting transfers between devices, shards(): lax.all_to_all(pieces.reshape(32, 1, -1), ('z', 'y'), 0, 0, tiled=True)  11.6 us
    all_to_all x1, waiting for transfers between devices, shards(): lax.all_to_all(pieces.reshape(32, 1, -1), ('z', 'y'), 0, 0, tiled=True)  11.4 us
    pallas_call x1, Pallas kernels, pair_call(): pl.pallas_call(pair_kernel, out_shape=(jax.ShapeDtypeStruct((4, 8, ROOM *...  9.15 us
    pallas_call x2, Pallas kernels, group_call(): pl.pallas_call(functools.partial(group_kernel, runs, planes), out_shape=j...  7.54 us
    pallas_call x1, Pallas kernels, screen_call(): pl.pallas_call(screen_kernel, out_shape=shapes, in_specs=[SMEM, VMEM, VME...  7.35 us
  transfers between devices with their start and end apart: 33, of which 13 were waited for; matrix products, arithmetic and copies ran while one was open for 1% of the time, Pallas kernels for 14%

commit v1 on v0

--- a/solution.py
+++ b/solution.py
@@ -525,42 +525,37 @@
     shard = shard_call(place, keep, swap(give))
 
     block = 2 * SPAN
+    columns, shard = hold((columns, shard))
     below2, above2 = shift(shard, "z", 2), shift(shard, "z", -2)
-    below, above, columns = hold((shift(shard, "z", 1), shift(shard, "z", -1), columns))
+    below, above = hold((shift(shard, "z", 1), shift(shard, "z", -1)))
     first = join(shard, below, above)
     first_down, first_up = shift(first, "y", 1), shift(first, "y", -1)
-    around = [columns, shift(columns, "x", 1), None, None]
-    below2, above2, first, columns = hold((below2, above2, first, columns))
+    around = [columns, shift(columns, "x", 1)]
+    below2, above2, first, columns, around[1] = hold((below2, above2, first, columns, around[1]))
     second = join(below2, above2)
     second_down, second_up = shift(second, "y", 1), shift(second, "y", -1)
-    around[3] = shift(columns, "x", 3)
+    around += [shift(columns, "x", 2), shift(columns, "x", 3)]
     screens = screen_call(place, after(screen, second), other)
-    first_down, first_up, around[1], below2, above2, *screens = hold(
-        (first_down, first_up, around[1], below2, above2, *screens)
-    )
-    around[2] = shift(after(columns, first_down), "x", 2)
-    swapped = [swap(columns), swap(around[1]), None, None]
-    second_down, second_up, first_down, swapped[0], swapped[1] = hold(
-        (second_down, second_up, first_down, swapped[0], swapped[1])
-    )
+    first_down, first_up, *screens = hold((first_down, first_up, *screens))
+    swapped = [swap(columns)]
+    second_down, second_up, first_down, *rest = hold((second_down, second_up, first_down, *around[2:], *swapped))
+    around[2:], swapped = rest[:2], rest[2:]
 
     z_below = shift(join(second_down[:block], second_up[:block], second[:block]), "z", 1)
     z_above = shift(join(second_down[block:], second_up[block:], second[block:]), "z", -1)
     two_down = shift(join(first_down[: 3 * SPAN], second_down[:block]), "y", 1)
     two_up = shift(join(first_up[3 * SPAN :], second_up[block:]), "y", -1)
-    swapped[3] = swap(around[3])
-    two_down, two_up, z_below, z_above, around[2], swapped[3] = hold(
-        (two_down, two_up, z_below, z_above, around[2], swapped[3])
-    )
+    swapped += [swap(around[1]), swap(around[2])]
+    two_down, two_up, z_below, z_above, *swapped = hold((two_down, two_up, z_below, z_above, *swapped))
 
     y_below, y_above = shift(z_below[:block], "y", 1), shift(z_above[block : 2 * block], "y", -1)
     far_below = shift(join(z_below[:block], z_below[2 * block : 2 * block + SPAN]), "z", 1)
     far_above = shift(join(z_above[block : 2 * block], z_above[2 * block + SPAN :]), "z", -1)
     rights = (first, first_down, first_up, second, second_down, second_up, two_down, two_up)
     total = group_call(near_runs, len(NEAR), place, rights, screens[:2], ())
-    swapped[2] = swap(around[2])
-    y_below, y_above, far_below, far_above, total, swapped[2] = hold(
-        (y_below, y_above, far_below, far_above, total, swapped[2])
+    swapped.append(swap(around[3]))
+    y_below, y_above, far_below, far_above, total, swapped[3] = hold(
+        (y_below, y_above, far_below, far_above, total, swapped[3])
     )
 
     across_low, across_high = shift(far_below[:SPAN], "y", 1), shift(far_above[SPAN : 2 * SPAN], "y", -1)

time: 156 us -> 156 us (level)
  waiting for transfers between devices: 47.9 us -> 40.8 us
  starting transfers between devices: 46.2 us -> 52.8 us
    ppermute x24, waiting for transfers between devices: 33.9 us -> 25.2 us  [shards(): lax.ppermute(array, axis, ring(lax.axis_size(axis), by))]
    ppermute x24, starting transfers between devices: 33.7 us -> 40.1 us  [shards(): lax.ppermute(array, axis, ring(lax.axis_size(axis), by))]
    ppermute x8, waiting for transfers between devices: 2.59 us -> 4.21 us  [shards(): swap = lambda array: lax.ppermute(array, 'core', SWAP)]
  transfers between devices with their start and end apart: 33 -> 33, of which waited for: 13 -> 14; matrix products, arithmetic and copies ran while one was open for 1% -> 1% of each run, Pallas kernels for 14% -> 14%
where the time goes in v1:
time: 156 us; the launch traced here: 155 us
  starting transfers between devices  52.8 us (34%)
  waiting for transfers between devices  40.8 us (26%)
  Pallas kernels  38.5 us (25%)
  blocking collectives  18.6 us (12%)
  local copies, waits for them, and re-layouts  3.02 us (2%)
    ppermute x24, starting transfers between devices, shards(): lax.ppermute(array, axis, ring(lax.axis_size(axis), by))  40.1 us
    ppermute x24, waiting for transfers between devices, shards(): lax.ppermute(array, axis, ring(lax.axis_size(axis), by))  25.2 us
    all_to_all x1, blocking collectives, shards(): parts = lax.all_to_all(parts, ('z', 'y'), 0, 0, tiled=True)  18.6 us
    all_to_all x1, starting transfers between devices, shards(): lax.all_to_all(pieces.reshape(32, 1, -1), ('z', 'y'), 0, 0, tiled=True)  11.6 us
    all_to_all x1, waiting for transfers between devices, shards(): lax.all_to_all(pieces.reshape(32, 1, -1), ('z', 'y'), 0, 0, tiled=True)  11.4 us
    pallas_call x1, Pallas kernels, pair_call(): pl.pallas_call(pair_kernel, out_shape=(jax.ShapeDtypeStruct((4, 8, ROOM *...  8.88 us
    pallas_call x2, Pallas kernels, group_call(): pl.pallas_call(functools.partial(group_kernel, runs, planes), out_shape=j...  7.55 us
    pallas_call x1, Pallas kernels, screen_call(): pl.pallas_call(screen_kernel, out_shape=shapes, in_specs=[SMEM, VMEM, VME...  7.35 us
  transfers between devices with their start and end apart: 33, of which 14 were waited for; matrix products, arithmetic and copies ran while one was open for 1% of the time, Pallas kernels for 14%

profile of v1, /device:TPU:2, one launch (start us, length us, event | category | flops | bytes accessed | tf_op | source)
XLA Modules:
  0.0 154.9 jit_solution(9585320981927189755)
XLA Ops:
  2.0 2.2 %pack.1 = f32[640,128]{1,0:T(8,128)} custom-call(s32[4]{0:T(128)} %pad_add_fusion.place, f32[2,16,2560]{2,1,0:T(8,128)} %own_ref.1, f32[2,16,2560]{2,1,0:T(8,128)} %collective-permute-done.other_ref), custom_call_target="tpu_custom_call" | custom-call | tf_op jit(solution)/shard_map/pack/pallas_call | solution.py:424
  4.4 11.6 %all-to-all-start = ((f32[32,1,2560]{2,1,0:T(1,128)}), f32[32,1,2560]{2,1,0:T(1,128)}, u32[]{:S(2)}, u32[]{:S(2)}) async-start(f32[32,1,2560]{2,1,0:T(1,128)} %bitcast.12), calls=%async_computation | async-start | bytes 655360 | tf_op jit(solution)/shard_map/all_to_all | solution.py:519
  19.4 11.4 %all-to-all-done = f32[32,1,2560]{2,1,0:T(1,128)} async-done(((f32[32,1,2560]{2,1,0:T(1,128)}), f32[32,1,2560]{2,1,0:T(1,128)}, u32[]{:S(2)}, u32[]{:S(2)}) %all-to-all-start) | async-done | bytes 327712 | tf_op jit(solution)/shard_map/all_to_all | solution.py:519
  31.5 2.5 %unpack.1 = (f32[80,1024]{1,0:T(8,128)S(1)}, f32[80,256]{1,0:T(8,128)S(1)}, f32[80,256]{1,0:T(8,128)S(1)}) custom-call(s32[4]{0:T(128)S(1)} %copy-done.2, s32[16,256]{1,0:T(8,128)S(1)} %plan.1.table, f32[640,128]{1,0:T(8,128)} %bitcast.6.in_ref), custom_call_target="tpu_custom_call" | custom-call | tf_op jit(solution)/shard_map/unpack/pallas_call | solution.py:473
  36.9 2.3 %collective-permute-start.6 = (f32[160,256]{1,0:T(8,128)S(1)}, f32[160,256]{1,0:T(8,128)S(1)}, u32[]{:S(2)}, u32[]{:S(2)}) collective-permute-start(f32[160,256]{1,0:T(8,128)S(1)} %shard.1), channel_id=1, source_target_pairs={{0,224},{32,0},{64,32},{96,64},{128,96},{160,128},{192,160},{224,1... | collective-permute-start | bytes 491528 | tf_op jit(solution)/shard_map/ppermute | solution.py:512
  39.2 1.5 collective-permute-start.7
  40.7 2.7 %collective-permute-done.5 = f32[160,256]{1,0:T(8,128)S(1)} collective-permute-done((f32[160,256]{1,0:T(8,128)S(1)}, f32[160,256]{1,0:T(8,128)S(1)}, u32[]{:S(2)}, u32[]{:S(2)}) %collective-permute-start.5) | collective-permute-done | bytes 163872 | tf_op jit(solution)/shard_map/ppermute | solution.py:512
  43.7 3.1 %collective-permute-start.11 = (f32[480,256]{1,0:T(8,128)S(1)}, f32[480,256]{1,0:T(8,128)S(1)}, u32[]{:S(2)}, u32[]{:S(2)}) collective-permute-start(f32[480,256]{1,0:T(8,128)S(1)} %constant_dynamic-update-slice_fusion.refs_0_), channel_id=1, source_target_pairs={{0,24},{8,0},{16,8},{24,16},{1,25},{9,1},{17,9},{25,17},{2,26},{10... | collective-permute-start | bytes 1474568 | tf_op jit(solution)/shard_map/ppermute | solution.py:512
  47.1 3.8 %collective-permute-start.4 = (f32[160,256]{1,0:T(8,128)S(1)}, f32[160,256]{1,0:T(8,128)S(1)}, u32[]{:S(2)}, u32[]{:S(2)}) collective-permute-start(f32[160,256]{1,0:T(8,128)S(1)} %shard.1), channel_id=1, source_target_pairs={{0,192},{32,224},{64,0},{96,32},{128,64},{160,96},{192,128},{224,1... | collective-permute-start | bytes 491528 | tf_op jit(solution)/shard_map/ppermute | solution.py:512
  50.9 5.2 %collective-permute-done.3 = f32[160,256]{1,0:T(8,128)S(1)} collective-permute-done((f32[160,256]{1,0:T(8,128)S(1)}, f32[160,256]{1,0:T(8,128)S(1)}, u32[]{:S(2)}, u32[]{:S(2)}) %collective-permute-start.3) | collective-permute-done | bytes 163872 | tf_op jit(solution)/shard_map/ppermute | solution.py:512
  56.4 3.2 %collective-permute-start.9 = (f32[320,256]{1,0:T(8,128)S(1)}, f32[320,256]{1,0:T(8,128)S(1)}, u32[]{:S(2)}, u32[]{:S(2)}) collective-permute-start(f32[320,256]{1,0:T(8,128)S(1)} %constant_dynamic-update-slice_fusion.3.refs_3_), channel_id=1, source_target_pairs={{0,24},{8,0},{16,8},{24,16},{1,25},{9,1},{17,9},{25,17},{2,26},{10... | collective-permute-start | bytes 983048 | tf_op jit(solution)/shard_map/ppermute | solution.py:512
  59.6 2.1 %collective-permute-start.12 = (f32[80,1024]{1,0:T(8,128)S(1)}, f32[80,1024]{1,0:T(8,128)S(1)}, u32[]{:S(2)}, u32[]{:S(2)}) collective-permute-start(f32[80,1024]{1,0:T(8,128)S(1)} %get-tuple-element.89.refs_0_), channel_id=1, source_target_pairs={{0,2},{1,3},{2,0},{3,1},{4,6},{5,7},{6,4},{7,5},{8,10},{9,11},{10,... | collective-permute-start | bytes 983048 | tf_op jit(solution)/shard_map/ppermute | solution.py:512
  63.2 7.4 %screen.1 = (bf16[640,1664]{1,0:T(8,128)(2,1)S(1)}, bf16[640,1664]{1,0:T(8,128)(2,1)S(1)}, bf16[640,640]{1,0:T(8,128)(2,1)S(1)}, bf16[640,640]{1,0:T(8,128)(2,1)...) custom-call(s32[4]{0:T(128)S(1)} %copy-done.3, f32[320,2560]{1,0:T(8,128)S(1)} %bitcast.10, ...), custom_call_target="tpu_custom_call" | custom-call | tf_op jit(solution)/shard_map/screen/pallas_call | solution.py:153
  71.2 2.5 %collective-permute-done.13.refs_3_ = f32[80,1024]{1,0:T(8,128)S(1)} collective-permute-done((f32[80,1024]{1,0:T(8,128)S(1)}, f32[80,1024]{1,0:T(8,128)S(1)}, u32[]{:S(2)}, u32[]{:S(2)}) %collective-permute-start.13) | collective-permute-done | bytes 327712 | tf_op jit(solution)/shard_map/ppermute | solution.py:512
  73.8 5.2 %collective-permute-start.18 = (f32[480,256]{1,0:T(8,128)S(1)}, f32[480,256]{1,0:T(8,128)S(1)}, u32[]{:S(2)}, u32[]{:S(2)}) collective-permute-start(f32[480,256]{1,0:T(8,128)S(1)} %pad_maximum_fusion.1), channel_id=1, source_target_pairs={{0,224},{32,0},{64,32},{96,64},{128,96},{160,128},{192,160},{224,1... | collective-permute-start | bytes 1474568 | tf_op jit(solution)/shard_map/ppermute | solution.py:512
  79.6 1.8 %collective-permute-start.15 = (f32[400,256]{1,0:T(8,128)S(1)}, f32[400,256]{1,0:T(8,128)S(1)}, u32[]{:S(2)}, u32[]{:S(2)}) collective-permute-start(f32[400,256]{1,0:T(8,128)S(1)} %pad_maximum_fusion.2), channel_id=1, source_target_pairs={{0,8},{8,16},{16,24},{24,0},{1,9},{9,17},{17,25},{25,1},{2,10},{10... | collective-permute-start | bytes 1228808 | tf_op jit(solution)/shard_map/ppermute | solution.py:512
  81.5 1.6 %collective-permute-done.20.refs_6_ = f32[80,1024]{1,0:T(8,128)S(1)} collective-permute-done((f32[80,1024]{1,0:T(8,128)S(1)}, f32[80,1024]{1,0:T(8,128)S(1)}, u32[]{:S(2)}, u32[]{:S(2)}) %collective-permute-start.20) | collective-permute-done | bytes 327712 | tf_op jit(solution)/shard_map/ppermute | solution.py:513
  83.2 7.2 %collective-permute-done.16.refs_7_ = f32[400,256]{1,0:T(8,128)S(1)} collective-permute-done((f32[400,256]{1,0:T(8,128)S(1)}, f32[400,256]{1,0:T(8,128)S(1)}, u32[]{:S(2)}, u32[]{:S(2)}) %collective-permute-start.16) | collective-permute-done | bytes 409632 | tf_op jit(solution)/shard_map/ppermute | solution.py:512
  93.3 1.6 %collective-permute-start.24 = (f32[240,256]{1,0:T(8,128)S(1)}, f32[240,256]{1,0:T(8,128)S(1)}, u32[]{:S(2)}, u32[]{:S(2)}) collective-permute-start(f32[240,256]{1,0:T(8,128)S(1)} %pad_maximum_fusion.5), channel_id=1, source_target_pairs={{0,224},{32,0},{64,32},{96,64},{128,96},{160,128},{192,160},{224,1... | collective-permute-start | bytes 737288 | tf_op jit(solution)/shard_map/ppermute | solution.py:512
  95.6 3.2 %collective-permute-start.22 = (f32[160,256]{1,0:T(8,128)S(1)}, f32[160,256]{1,0:T(8,128)S(1)}, u32[]{:S(2)}, u32[]{:S(2)}) collective-permute-start(f32[160,256]{1,0:T(8,128)S(1)} %slice.47), channel_id=1, source_target_pairs={{0,24},{8,0},{16,8},{24,16},{1,25},{9,1},{17,9},{25,17},{2,26},{10... | collective-permute-start | bytes 491528 | tf_op jit(solution)/shard_map/ppermute | solution.py:512
  98.7 5.0 %group.2.refs_6_ = f32[640,512]{1,0:T(8,128)S(1)} custom-call(s32[4]{0:T(128)S(1)} %copy-done.3, f32[480,256]{1,0:T(8,128)S(1)} %constant_dynamic-update-slice_fusion.refs_0_, f32[480,256]{1,0:T(8,128)S(1)} %collective-permute-done.10.refs_1_, f32[480,256]{1,0:T(8,128)S(1)} %collective-permute-done.11.refs_2_, ...), custom_call_target="tpu_custom_call" | custom-call | tf_op jit(solution)/shard_map/group/pallas_call | solution.py:252
  103.9 3.2 %collective-permute-start.27 = (f32[80,256]{1,0:T(8,128)S(1)}, f32[80,256]{1,0:T(8,128)S(1)}, u32[]{:S(2)}, u32[]{:S(2)}) collective-permute-start(f32[80,256]{1,0:T(8,128)S(1)} %slice.51), channel_id=1, source_target_pairs={{0,24},{8,0},{16,8},{24,16},{1,25},{9,1},{17,9},{25,17},{2,26},{10... | collective-permute-start | bytes 245768 | tf_op jit(solution)/shard_map/ppermute | solution.py:512
  107.2 2.1 %left.1 = (bf16[1024,640]{1,0:T(8,128)(2,1)S(1)}, bf16[1024,640]{1,0:T(8,128)(2,1)S(1)}) custom-call(s32[4]{0:T(128)S(1)} %copy-done.3, f32[80,1024]{1,0:T(8,128)S(1)} %get-tuple-element.89.refs_0_, f32[80,1024]{1,0:T(8,128)S(1)} %collective-permute-done.7.refs_1_, f32[80,1024]{1,0:T(8,128)S(1)} %collective-permute-done.12.refs_2_, ...), custom_call_target="tpu_custom_call" | custom-call | tf_op jit(solution)/shard_map/left/pallas_call | solution.py:185
  109.3 2.5 %group.3.refs_6_ = f32[640,512]{1,0:T(8,128)S(1)} custom-call(s32[4]{0:T(128)S(1)} %copy-done.3, f32[480,256]{1,0:T(8,128)S(1)} %collective-permute-done.17.refs_0_, f32[480,256]{1,0:T(8,128)S(1)} %collective-permute-done.18.refs_1_, f32[160,256]{1,0:T(8,128)S(1)} %collective-permute-done.21.refs_2_, f32[160,256]{1,0:T(8,128)S(1)} %collective-permute-done.22.refs_3_, ...), custom_call_target="tpu_custom_call" | custom-call | tf_op jit(solution)/shard_map/group/pallas_call | solution.py:252
  111.8 8.9 %pair.1 = (f32[4,8,3584]{2,1,0:T(8,128)S(1)}, f32[1024,512]{1,0:T(8,128)S(1)}) custom-call(s32[4]{0:T(128)S(1)} %copy-done.3, s32[16,256]{1,0:T(8,128)S(1)} %plan.1.table, f32[240,256]{1,0:T(8,128)S(1)} %collective-permute-done.23.refs_0_, f32[240,256]{1,0:T(8,128)S(1)} %collective-permute-done.24.refs_1_, f32[80,256]{1,0:T(8,128)S(1)} %collective-permute-done.26.refs_2_, ...), custom_call_target="tpu_custom_call" | custom-call | tf_op jit(solution)/shard_map/pair/pallas_call | solution.py:310
  120.8 3.2 %extract.1.one_ref = f32[4,8,3584]{2,1,0:T(8,128)S(1)} custom-call(s32[4]{0:T(128)S(1)} %copy-done.3, s32[16,256]{1,0:T(8,128)S(1)} %plan.1.table, f32[1024,512]{1,0:T(8,128)S(1)} %get-tuple-element.125.kern), custom_call_target="tpu_custom_call" | custom-call | tf_op jit(solution)/shard_map/extract/pallas_call | solution.py:329
  124.2 2.2 %collective-permute-start.30 = (f32[8,3584]{1,0:T(8,128)S(1)}, f32[8,3584]{1,0:T(8,128)S(1)}, u32[]{:S(2)}, u32[]{:S(2)}) collective-permute-start(f32[8,3584]{1,0:T(8,128)S(1)} %get-tuple-element.129), channel_id=1, source_target_pairs={{0,2},{1,3},{2,0},{3,1},{4,6},{5,7},{6,4},{7,5},{8,10},{9,11},{10,... | collective-permute-start | bytes 344072 | tf_op jit(solution)/shard_map/ppermute | solution.py:512
  126.4 2.5 %collective-permute-start.31 = (f32[8,3584]{1,0:T(8,128)S(1)}, f32[8,3584]{1,0:T(8,128)S(1)}, u32[]{:S(2)}, u32[]{:S(2)}) collective-permute-start(f32[8,3584]{1,0:T(8,128)S(1)} %get-tuple-element.130), channel_id=1, source_target_pairs={{0,3},{1,0},{2,1},{3,2},{4,7},{5,4},{6,5},{7,6},{8,11},{9,8},{10,9... | collective-permute-start | bytes 344072 | tf_op jit(solution)/shard_map/ppermute | solution.py:512
  129.5 2.3 %collective-permute-done.30.three_ref = f32[8,3584]{1,0:T(8,128)S(1)} collective-permute-done((f32[8,3584]{1,0:T(8,128)S(1)}, f32[8,3584]{1,0:T(8,128)S(1)}, u32[]{:S(2)}, u32[]{:S(2)}) %collective-permute-start.30) | collective-permute-done | bytes 114720 | tf_op jit(solution)/shard_map/ppermute | solution.py:512
  131.8 1.8 %collective-permute-done.31.four_ref = f32[8,3584]{1,0:T(8,128)S(1)} collective-permute-done((f32[8,3584]{1,0:T(8,128)S(1)}, f32[8,3584]{1,0:T(8,128)S(1)}, u32[]{:S(2)}, u32[]{:S(2)}) %collective-permute-start.31) | collective-permute-done | bytes 114720 | tf_op jit(solution)/shard_map/ppermute | solution.py:512
  134.8 18.6 %all_to_all.10.parts_ref = f32[32,8,256]{2,1,0:T(8,128)S(1)} all-to-all(f32[32,8,256]{2,1,0:T(8,128)S(1)} %owner.1), channel_id=1, replica_groups=mesh['z'=8,'y'=4,'core'=2,'x'=4] {'z','y'}, dimensions={0} | all-to-all | bytes 524288 | tf_op jit(solution)/shard_map/all_to_all | solution.py:572
  153.4 1.5 last.1
  (81 shorter events, 18.4 us)
Async XLA Ops:
  0.0 2.0 %collective-permute-start = (f32[2,16,2560]{2,1,0:T(8,128)}, f32[2,16,2560]{2,1,0:T(8,128)}, u32[]{:S(2)}, u32[]{:S(2)}) collective-permute-start(f32[2,16,2560]{2,1,0:T(8,128)} %own_ref.1), channel_id=1, source_target_pairs={{0,4},{4,0},{1,5},{5,1},{2,6},{6,2},{3,7},{7,3},{8,12},{12,8},{9,1... | collective-permute-start | bytes 983048 | tf_op jit(solution)/shard_map/ppermute | solution.py:513
  4.2 26.6 %collective-permute-start.1 = (f32[320,2560]{1,0:T(8,128)}, f32[320,2560]{1,0:T(8,128)}, u32[]{:S(2)}, u32[]{:S(2)}) collective-permute-start(f32[320,2560]{1,0:T(8,128)} %bitcast.9), channel_id=1, source_target_pairs={{0,4},{4,0},{1,5},{5,1},{2,6},{6,2},{3,7},{7,3},{8,12},{12,8},{9,1... | collective-permute-start | bytes 9830408 | tf_op jit(solution)/shard_map/ppermute | solution.py:513
  4.4 26.4 %all-to-all-start = ((f32[32,1,2560]{2,1,0:T(1,128)}), f32[32,1,2560]{2,1,0:T(1,128)}, u32[]{:S(2)}, u32[]{:S(2)}) async-start(f32[32,1,2560]{2,1,0:T(1,128)} %bitcast.12), calls=%async_computation | async-start | bytes 655360 | tf_op jit(solution)/shard_map/all_to_all | solution.py:519
  35.9 7.5 %collective-permute-start.5 = (f32[160,256]{1,0:T(8,128)S(1)}, f32[160,256]{1,0:T(8,128)S(1)}, u32[]{:S(2)}, u32[]{:S(2)}) collective-permute-start(f32[160,256]{1,0:T(8,128)S(1)} %shard.1), channel_id=1, source_target_pairs={{0,32},{32,64},{64,96},{96,128},{128,160},{160,192},{192,224},{224... | collective-permute-start | bytes 491528 | tf_op jit(solution)/shard_map/ppermute | solution.py:512
  36.9 6.6 %collective-permute-start.6 = (f32[160,256]{1,0:T(8,128)S(1)}, f32[160,256]{1,0:T(8,128)S(1)}, u32[]{:S(2)}, u32[]{:S(2)}) collective-permute-start(f32[160,256]{1,0:T(8,128)S(1)} %shard.1), channel_id=1, source_target_pairs={{0,224},{32,0},{64,32},{96,64},{128,96},{160,128},{192,160},{224,1... | collective-permute-start | bytes 491528 | tf_op jit(solution)/shard_map/ppermute | solution.py:512
  39.2 17.1 %collective-permute-start.7 = (f32[80,1024]{1,0:T(8,128)S(1)}, f32[80,1024]{1,0:T(8,128)S(1)}, u32[]{:S(2)}, u32[]{:S(2)}) collective-permute-start(f32[80,1024]{1,0:T(8,128)S(1)} %get-tuple-element.89.refs_0_), channel_id=1, source_target_pairs={{0,1},{1,2},{2,3},{3,0},{4,5},{5,6},{6,7},{7,4},{8,9},{9,10},{10,1... | collective-permute-start | bytes 983048 | tf_op jit(solution)/shard_map/ppermute | solution.py:512
  43.5 18.3 %collective-permute-start.10 = (f32[480,256]{1,0:T(8,128)S(1)}, f32[480,256]{1,0:T(8,128)S(1)}, u32[]{:S(2)}, u32[]{:S(2)}) collective-permute-start(f32[480,256]{1,0:T(8,128)S(1)} %constant_dynamic-update-slice_fusion.refs_0_), channel_id=1, source_target_pairs={{0,8},{8,16},{16,24},{24,0},{1,9},{9,17},{17,25},{25,1},{2,10},{10... | collective-permute-start | bytes 1474568 | tf_op jit(solution)/shard_map/ppermute | solution.py:512
  43.7 19.5 %collective-permute-start.11 = (f32[480,256]{1,0:T(8,128)S(1)}, f32[480,256]{1,0:T(8,128)S(1)}, u32[]{:S(2)}, u32[]{:S(2)}) collective-permute-start(f32[480,256]{1,0:T(8,128)S(1)} %constant_dynamic-update-slice_fusion.refs_0_), channel_id=1, source_target_pairs={{0,24},{8,0},{16,8},{24,16},{1,25},{9,1},{17,9},{25,17},{2,26},{10... | collective-permute-start | bytes 1474568 | tf_op jit(solution)/shard_map/ppermute | solution.py:512
  46.8 9.4 %collective-permute-start.3 = (f32[160,256]{1,0:T(8,128)S(1)}, f32[160,256]{1,0:T(8,128)S(1)}, u32[]{:S(2)}, u32[]{:S(2)}) collective-permute-start(f32[160,256]{1,0:T(8,128)S(1)} %shard.1), channel_id=1, source_target_pairs={{0,64},{32,96},{64,128},{96,160},{128,192},{160,224},{192,0},{224,... | collective-permute-start | bytes 491528 | tf_op jit(solution)/shard_map/ppermute | solution.py:512
  47.1 9.1 %collective-permute-start.4 = (f32[160,256]{1,0:T(8,128)S(1)}, f32[160,256]{1,0:T(8,128)S(1)}, u32[]{:S(2)}, u32[]{:S(2)}) collective-permute-start(f32[160,256]{1,0:T(8,128)S(1)} %shard.1), channel_id=1, source_target_pairs={{0,192},{32,224},{64,0},{96,32},{128,64},{160,96},{192,128},{224,1... | collective-permute-start | bytes 491528 | tf_op jit(solution)/shard_map/ppermute | solution.py:512
  56.3 14.3 %collective-permute-start.8 = (f32[320,256]{1,0:T(8,128)S(1)}, f32[320,256]{1,0:T(8,128)S(1)}, u32[]{:S(2)}, u32[]{:S(2)}) collective-permute-start(f32[320,256]{1,0:T(8,128)S(1)} %constant_dynamic-update-slice_fusion.3.refs_3_), channel_id=1, source_target_pairs={{0,8},{8,16},{16,24},{24,0},{1,9},{9,17},{17,25},{25,1},{2,10},{10... | collective-permute-start | bytes 983048 | tf_op jit(solution)/shard_map/ppermute | solution.py:512
  56.4 14.8 %collective-permute-start.9 = (f32[320,256]{1,0:T(8,128)S(1)}, f32[320,256]{1,0:T(8,128)S(1)}, u32[]{:S(2)}, u32[]{:S(2)}) collective-permute-start(f32[320,256]{1,0:T(8,128)S(1)} %constant_dynamic-update-slice_fusion.3.refs_3_), channel_id=1, source_target_pairs={{0,24},{8,0},{16,8},{24,16},{1,25},{9,1},{17,9},{25,17},{2,26},{10... | collective-permute-start | bytes 983048 | tf_op jit(solution)/shard_map/ppermute | solution.py:512
  59.6 11.5 %collective-permute-start.12 = (f32[80,1024]{1,0:T(8,128)S(1)}, f32[80,1024]{1,0:T(8,128)S(1)}, u32[]{:S(2)}, u32[]{:S(2)}) collective-permute-start(f32[80,1024]{1,0:T(8,128)S(1)} %get-tuple-element.89.refs_0_), channel_id=1, source_target_pairs={{0,2},{1,3},{2,0},{3,1},{4,6},{5,7},{6,4},{7,5},{8,10},{9,11},{10,... | collective-permute-start | bytes 983048 | tf_op jit(solution)/shard_map/ppermute | solution.py:512
  61.8 11.9 %collective-permute-start.13 = (f32[80,1024]{1,0:T(8,128)S(1)}, f32[80,1024]{1,0:T(8,128)S(1)}, u32[]{:S(2)}, u32[]{:S(2)}) collective-permute-start(f32[80,1024]{1,0:T(8,128)S(1)} %get-tuple-element.89.refs_0_), channel_id=1, source_target_pairs={{0,3},{1,0},{2,1},{3,2},{4,7},{5,4},{6,5},{7,6},{8,11},{9,8},{10,9... | collective-permute-start | bytes 983048 | tf_op jit(solution)/shard_map/ppermute | solution.py:512
  63.2 10.5 %collective-permute-start.14 = (f32[80,1024]{1,0:T(8,128)S(1)}, f32[80,1024]{1,0:T(8,128)S(1)}, u32[]{:S(2)}, u32[]{:S(2)}) collective-permute-start(f32[80,1024]{1,0:T(8,128)S(1)} %get-tuple-element.89.refs_0_), channel_id=1, source_target_pairs={{0,4},{4,0},{1,5},{5,1},{2,6},{6,2},{3,7},{7,3},{8,12},{12,8},{9,1... | collective-permute-start | bytes 983048 | tf_op jit(solution)/shard_map/ppermute | solution.py:513
  70.6 10.9 %collective-permute-start.19 = (f32[80,1024]{1,0:T(8,128)S(1)}, f32[80,1024]{1,0:T(8,128)S(1)}, u32[]{:S(2)}, u32[]{:S(2)}) collective-permute-start(f32[80,1024]{1,0:T(8,128)S(1)} %collective-permute-done.7.refs_1_), channel_id=1, source_target_pairs={{0,4},{4,0},{1,5},{5,1},{2,6},{6,2},{3,7},{7,3},{8,12},{12,8},{9,1... | collective-permute-start | bytes 983048 | tf_op jit(solution)/shard_map/ppermute | solution.py:513
  73.8 18.0 %collective-permute-start.18 = (f32[480,256]{1,0:T(8,128)S(1)}, f32[480,256]{1,0:T(8,128)S(1)}, u32[]{:S(2)}, u32[]{:S(2)}) collective-permute-start(f32[480,256]{1,0:T(8,128)S(1)} %pad_maximum_fusion.1), channel_id=1, source_target_pairs={{0,224},{32,0},{64,32},{96,64},{128,96},{160,128},{192,160},{224,1... | collective-permute-start | bytes 1474568 | tf_op jit(solution)/shard_map/ppermute | solution.py:512
  79.1 14.2 %collective-permute-start.17 = (f32[480,256]{1,0:T(8,128)S(1)}, f32[480,256]{1,0:T(8,128)S(1)}, u32[]{:S(2)}, u32[]{:S(2)}) collective-permute-start(f32[480,256]{1,0:T(8,128)S(1)} %pad_maximum_fusion), channel_id=1, source_target_pairs={{0,32},{32,64},{64,96},{96,128},{128,160},{160,192},{192,224},{224... | collective-permute-start | bytes 1474568 | tf_op jit(solution)/shard_map/ppermute | solution.py:512
  79.2 11.2 %collective-permute-start.16 = (f32[400,256]{1,0:T(8,128)S(1)}, f32[400,256]{1,0:T(8,128)S(1)}, u32[]{:S(2)}, u32[]{:S(2)}) collective-permute-start(f32[400,256]{1,0:T(8,128)S(1)} %pad_maximum_fusion.3), channel_id=1, source_target_pairs={{0,24},{8,0},{16,8},{24,16},{1,25},{9,1},{17,9},{25,17},{2,26},{10... | collective-permute-start | bytes 1228808 | tf_op jit(solution)/shard_map/ppermute | solution.py:512
  79.6 12.1 %collective-permute-start.15 = (f32[400,256]{1,0:T(8,128)S(1)}, f32[400,256]{1,0:T(8,128)S(1)}, u32[]{:S(2)}, u32[]{:S(2)}) collective-permute-start(f32[400,256]{1,0:T(8,128)S(1)} %pad_maximum_fusion.2), channel_id=1, source_target_pairs={{0,8},{8,16},{16,24},{24,0},{1,9},{9,17},{17,25},{25,1},{2,10},{10... | collective-permute-start | bytes 1228808 | tf_op jit(solution)/shard_map/ppermute | solution.py:512
  81.5 1.6 %collective-permute-start.20 = (f32[80,1024]{1,0:T(8,128)S(1)}, f32[80,1024]{1,0:T(8,128)S(1)}, u32[]{:S(2)}, u32[]{:S(2)}) collective-permute-start(f32[80,1024]{1,0:T(8,128)S(1)} %collective-permute-done.12.refs_2_), channel_id=1, source_target_pairs={{0,4},{4,0},{1,5},{5,1},{2,6},{6,2},{3,7},{7,3},{8,12},{12,8},{9,1... | collective-permute-start | bytes 983048 | tf_op jit(solution)/shard_map/ppermute | solution.py:513
  83.1 20.7 %collective-permute-start.25 = (f32[80,1024]{1,0:T(8,128)S(1)}, f32[80,1024]{1,0:T(8,128)S(1)}, u32[]{:S(2)}, u32[]{:S(2)}) collective-permute-start(f32[80,1024]{1,0:T(8,128)S(1)} %collective-permute-done.13.refs_3_), channel_id=1, source_target_pairs={{0,4},{4,0},{1,5},{5,1},{2,6},{6,2},{3,7},{7,3},{8,12},{12,8},{9,1... | collective-permute-start | bytes 983048 | tf_op jit(solution)/shard_map/ppermute | solution.py:513
  93.3 10.5 %collective-permute-start.24 = (f32[240,256]{1,0:T(8,128)S(1)}, f32[240,256]{1,0:T(8,128)S(1)}, u32[]{:S(2)}, u32[]{:S(2)}) collective-permute-start(f32[240,256]{1,0:T(8,128)S(1)} %pad_maximum_fusion.5), channel_id=1, source_target_pairs={{0,224},{32,0},{64,32},{96,64},{128,96},{160,128},{192,160},{224,1... | collective-permute-start | bytes 737288 | tf_op jit(solution)/shard_map/ppermute | solution.py:512
  94.9 8.9 %collective-permute-start.23 = (f32[240,256]{1,0:T(8,128)S(1)}, f32[240,256]{1,0:T(8,128)S(1)}, u32[]{:S(2)}, u32[]{:S(2)}) collective-permute-start(f32[240,256]{1,0:T(8,128)S(1)} %pad_maximum_fusion.4), channel_id=1, source_target_pairs={{0,32},{32,64},{64,96},{96,128},{128,160},{160,192},{192,224},{224... | collective-permute-start | bytes 737288 | tf_op jit(solution)/shard_map/ppermute | solution.py:512
  95.5 8.3 %collective-permute-start.21 = (f32[160,256]{1,0:T(8,128)S(1)}, f32[160,256]{1,0:T(8,128)S(1)}, u32[]{:S(2)}, u32[]{:S(2)}) collective-permute-start(f32[160,256]{1,0:T(8,128)S(1)} %slice.46), channel_id=1, source_target_pairs={{0,8},{8,16},{16,24},{24,0},{1,9},{9,17},{17,25},{25,1},{2,10},{10... | collective-permute-start | bytes 491528 | tf_op jit(solution)/shard_map/ppermute | solution.py:512
  95.6 8.2 %collective-permute-start.22 = (f32[160,256]{1,0:T(8,128)S(1)}, f32[160,256]{1,0:T(8,128)S(1)}, u32[]{:S(2)}, u32[]{:S(2)}) collective-permute-start(f32[160,256]{1,0:T(8,128)S(1)} %slice.47), channel_id=1, source_target_pairs={{0,24},{8,0},{16,8},{24,16},{1,25},{9,1},{17,9},{25,17},{2,26},{10... | collective-permute-start | bytes 491528 | tf_op jit(solution)/shard_map/ppermute | solution.py:512
  103.8 8.0 %collective-permute-start.26 = (f32[80,256]{1,0:T(8,128)S(1)}, f32[80,256]{1,0:T(8,128)S(1)}, u32[]{:S(2)}, u32[]{:S(2)}) collective-permute-start(f32[80,256]{1,0:T(8,128)S(1)} %slice.50), channel_id=1, source_target_pairs={{0,8},{8,16},{16,24},{24,0},{1,9},{9,17},{17,25},{25,1},{2,10},{10... | collective-permute-start | bytes 245768 | tf_op jit(solution)/shard_map/ppermute | solution.py:512
  103.9 7.9 %collective-permute-start.27 = (f32[80,256]{1,0:T(8,128)S(1)}, f32[80,256]{1,0:T(8,128)S(1)}, u32[]{:S(2)}, u32[]{:S(2)}) collective-permute-start(f32[80,256]{1,0:T(8,128)S(1)} %slice.51), channel_id=1, source_target_pairs={{0,24},{8,0},{16,8},{24,16},{1,25},{9,1},{17,9},{25,17},{2,26},{10... | collective-permute-start | bytes 245768 | tf_op jit(solution)/shard_map/ppermute | solution.py:512
  120.7 3.3 %collective-permute-start.28 = (f32[4,8,3584]{2,1,0:T(8,128)S(1)}, f32[4,8,3584]{2,1,0:T(8,128)S(1)}, u32[]{:S(2)}, u32[]{:S(2)}) collective-permute-start(f32[4,8,3584]{2,1,0:T(8,128)S(1)} %get-tuple-element.126), channel_id=1, source_target_pairs={{0,4},{4,0},{1,5},{5,1},{2,6},{6,2},{3,7},{7,3},{8,12},{12,8},{9,1... | collective-permute-start | bytes 1376264 | tf_op jit(solution)/shard_map/ppermute | solution.py:513
  124.1 5.4 %collective-permute-start.29 = (f32[8,3584]{1,0:T(8,128)S(1)}, f32[8,3584]{1,0:T(8,128)S(1)}, u32[]{:S(2)}, u32[]{:S(2)}) collective-permute-start(f32[8,3584]{1,0:T(8,128)S(1)} %get-tuple-element.128), channel_id=1, source_target_pairs={{0,1},{1,2},{2,3},{3,0},{4,5},{5,6},{6,7},{7,4},{8,9},{9,10},{10,1... | collective-permute-start | bytes 344072 | tf_op jit(solution)/shard_map/ppermute | solution.py:512
  124.2 7.6 %collective-permute-start.30 = (f32[8,3584]{1,0:T(8,128)S(1)}, f32[8,3584]{1,0:T(8,128)S(1)}, u32[]{:S(2)}, u32[]{:S(2)}) collective-permute-start(f32[8,3584]{1,0:T(8,128)S(1)} %get-tuple-element.129), channel_id=1, source_target_pairs={{0,2},{1,3},{2,0},{3,1},{4,6},{5,7},{6,4},{7,5},{8,10},{9,11},{10,... | collective-permute-start | bytes 344072 | tf_op jit(solution)/shard_map/ppermute | solution.py:512
  126.4 7.1 %collective-permute-start.31 = (f32[8,3584]{1,0:T(8,128)S(1)}, f32[8,3584]{1,0:T(8,128)S(1)}, u32[]{:S(2)}, u32[]{:S(2)}) collective-permute-start(f32[8,3584]{1,0:T(8,128)S(1)} %get-tuple-element.130), channel_id=1, source_target_pairs={{0,3},{1,0},{2,1},{3,2},{4,7},{5,4},{6,5},{7,6},{8,11},{9,8},{10,9... | collective-permute-start | bytes 344072 | tf_op jit(solution)/shard_map/ppermute | solution.py:512
  (6 other events, 97.7 us)

commit v2 on v0

--- a/solution.py
+++ b/solution.py
@@ -223,17 +223,17 @@
     )
 
 
-def middle_runs(z_below, z_above, y_below, y_above):
+def middle_runs(below, above, z_below, z_above, y_below, y_above):
     runs = ()
-    for first, sides, across in ((0, z_below, y_below), (2, z_above, y_above)):
-        runs += ((3, sides, 0, first, 2), (1, sides, 2 * SPAN, first, 2), (0, sides, 4 * SPAN, first, 2))
+    for first, own, sides, across in ((0, below, z_below, y_below), (2, above, z_above, y_above)):
+        runs += ((0, own, 0, first, 2), (3, sides, 0, first, 2), (1, sides, 2 * SPAN, first, 2))
         runs += ((2, across, 0, first, 2),)
     return runs
 
 
-def far_runs(below, above, across_low, across_high):
+def far_runs(z_below, z_above, below, above, across_low, across_high):
     return (
-        ((3, below, 0, 0, 2), (1, above, 0, 0, 2), (0, below, 2 * SPAN, 0, 1), (0, above, 2 * SPAN, 1, 1))
+        ((0, z_below, 4 * SPAN, 0, 1), (0, z_above, 4 * SPAN, 1, 1), (3, below, 0, 0, 2), (1, above, 0, 0, 2))
         + ((2, across_low, 0, 0, 1), (2, across_high, 0, 1, 1))
     )
 
@@ -261,7 +261,7 @@
 
 
 def pair_kernel(place, table, *refs):
-    rights, (high_ref, low_ref, sum_ref, left_high, left_low, give_ref, kern, rh, rl) = refs[:4], refs[4:]
+    rights, (high_ref, low_ref, sum_ref, left_high, left_low, give_ref, kern, rh, rl) = refs[:6], refs[6:]
     load_right(place, far_runs(*rights), len(FAR), rh, rl)
     product = sum_ref[...] + dot3(high_ref[...], low_ref[...], rh[...], rl[...])
     mid = product.shape[0] // 2
@@ -538,24 +538,21 @@
     first_down, first_up, around[1], below2, above2, *screens = hold(
         (first_down, first_up, around[1], below2, above2, *screens)
     )
-    around[2] = shift(after(columns, first_down), "x", 2)
-    swapped = [swap(columns), swap(around[1]), None, None]
-    second_down, second_up, first_down, swapped[0], swapped[1] = hold(
-        (second_down, second_up, first_down, swapped[0], swapped[1])
-    )
-
-    z_below = shift(join(second_down[:block], second_up[:block], second[:block]), "z", 1)
-    z_above = shift(join(second_down[block:], second_up[block:], second[block:]), "z", -1)
+    below3, above3 = shift(below2, "z", 1), shift(above2, "z", -1)
+    below3, above3, second_down, second_up, around[3] = hold((below3, above3, second_down, second_up, around[3]))
+
+    z_below = shift(join(second_down[:block], second_up[:block], below3[:SPAN]), "z", 1)
+    z_above = shift(join(second_down[block:], second_up[block:], above3[SPAN:]), "z", -1)
     two_down = shift(join(first_down[: 3 * SPAN], second_down[:block]), "y", 1)
     two_up = shift(join(first_up[3 * SPAN :], second_up[block:]), "y", -1)
-    swapped[3] = swap(around[3])
-    two_down, two_up, z_below, z_above, around[2], swapped[3] = hold(
-        (two_down, two_up, z_below, z_above, around[2], swapped[3])
+    around[2] = shift(after(columns, below3), "x", 2)
+    swapped = [swap(around[0]), swap(around[1]), None, swap(around[3])]
+    two_down, two_up, z_below, z_above, around[2], swapped[0], swapped[1], swapped[3] = hold(
+        (two_down, two_up, z_below, z_above, around[2], swapped[0], swapped[1], swapped[3])
     )
 
     y_below, y_above = shift(z_below[:block], "y", 1), shift(z_above[block : 2 * block], "y", -1)
-    far_below = shift(join(z_below[:block], z_below[2 * block : 2 * block + SPAN]), "z", 1)
-    far_above = shift(join(z_above[block : 2 * block], z_above[2 * block + SPAN :]), "z", -1)
+    far_below, far_above = shift(z_below[:block], "z", 1), shift(z_above[block : 2 * block], "z", -1)
     rights = (first, first_down, first_up, second, second_down, second_up, two_down, two_up)
     total = group_call(near_runs, len(NEAR), place, rights, screens[:2], ())
     swapped[2] = swap(around[2])
@@ -563,12 +560,12 @@
         (y_below, y_above, far_below, far_above, total, swapped[2])
     )
 
-    across_low, across_high = shift(far_below[:SPAN], "y", 1), shift(far_above[SPAN : 2 * SPAN], "y", -1)
-    rights = (z_below, z_above, y_below, y_above)
+    across_low, across_high = shift(far_below[:SPAN], "y", 1), shift(far_above[SPAN:], "y", -1)
+    rights = (below3, above3, z_below, z_above, y_below, y_above)
     total = group_call(middle_runs, len(MIDDLE), place, rights, screens[2:4], (total,))
     left_high, left_low = left_call(place, around + swapped)
     across_low, across_high, total, left_high, left_low = hold((across_low, across_high, total, left_high, left_low))
-    rights = (far_below, far_above, across_low, across_high)
+    rights = (z_below, z_above, far_below, far_above, across_low, across_high)
     give, kern = pair_call(place, table, rights, screens[4:], total, left_high, left_low)
 
     parts = add_call(extract_call(place, table, kern), swap(give))

time: 156 us -> 151 us (0.968)
  waiting for transfers between devices: 47.9 us -> 40.8 us
  starting transfers between devices: 46.2 us -> 48.4 us
    ppermute x24 -> x26, waiting for transfers between devices: 33.9 us -> 25.2 us  [shards(): lax.ppermute(array, axis, ring(lax.axis_size(axis), by))]
    ppermute x24 -> x26, starting transfers between devices: 33.7 us -> 35.8 us  [shards(): lax.ppermute(array, axis, ring(lax.axis_size(axis), by))]
    ppermute x8, waiting for transfers between devices: 2.59 us -> 4.22 us  [shards(): swap = lambda array: lax.ppermute(array, 'core', SWAP)]
  transfers between devices with their start and end apart: 33 -> 35, of which waited for: 13 -> 17; matrix products, arithmetic and copies ran while one was open for 1% -> 1% of each run, Pallas kernels for 14% -> 14%
where the time goes in v2:
time: 151 us
  starting transfers between devices  48.4 us (32%)
  waiting for transfers between devices  40.8 us (27%)
  Pallas kernels  38.5 us (25%)
  blocking collectives  18.7 us (12%)
  local copies, waits for them, and re-layouts  2.99 us (2%)
    ppermute x26, starting transfers between devices, shards(): lax.ppermute(array, axis, ring(lax.axis_size(axis), by))  35.8 us
    ppermute x26, waiting for transfers between devices, shards(): lax.ppermute(array, axis, ring(lax.axis_size(axis), by))  25.2 us
    all_to_all x1, blocking collectives, shards(): parts = lax.all_to_all(parts, ('z', 'y'), 0, 0, tiled=True)  18.7 us
    all_to_all x1, starting transfers between devices, shards(): lax.all_to_all(pieces.reshape(32, 1, -1), ('z', 'y'), 0, 0, tiled=True)  11.6 us
    all_to_all x1, waiting for transfers between devices, shards(): lax.all_to_all(pieces.reshape(32, 1, -1), ('z', 'y'), 0, 0, tiled=True)  11.4 us
    pallas_call x1, Pallas kernels, pair_call(): pl.pallas_call(pair_kernel, out_shape=(jax.ShapeDtypeStruct((4, 8, ROOM *...  9.15 us
    pallas_call x2, Pallas kernels, group_call(): pl.pallas_call(functools.partial(group_kernel, runs, planes), out_shape=j...  7.55 us
    pallas_call x1, Pallas kernels, screen_call(): pl.pallas_call(screen_kernel, out_shape=shapes, in_specs=[SMEM, VMEM, VME...  7.35 us
  transfers between devices with their start and end apart: 35, of which 17 were waited for; matrix products, arithmetic and copies ran while one was open for 1% of the time, Pallas kernels for 14%

profile of v2, /device:TPU:2, one launch (start us, length us, event | category | flops | bytes accessed | tf_op | source)
XLA Modules:
  0.0 150.5 jit_solution(18355921051285358268)
XLA Ops:
  2.0 2.2 %pack.1 = f32[640,128]{1,0:T(8,128)} custom-call(s32[4]{0:T(128)} %pad_add_fusion.place, f32[2,16,2560]{2,1,0:T(8,128)} %own_ref.1, f32[2,16,2560]{2,1,0:T(8,128)} %collective-permute-done.other_ref), custom_call_target="tpu_custom_call" | custom-call | tf_op jit(solution)/shard_map/pack/pallas_call | solution.py:424
  4.4 11.6 %all-to-all-start = ((f32[32,1,2560]{2,1,0:T(1,128)}), f32[32,1,2560]{2,1,0:T(1,128)}, u32[]{:S(2)}, u32[]{:S(2)}) async-start(f32[32,1,2560]{2,1,0:T(1,128)} %bitcast.12), calls=%async_computation | async-start | bytes 655360 | tf_op jit(solution)/shard_map/all_to_all | solution.py:519
  19.4 11.4 %all-to-all-done = f32[32,1,2560]{2,1,0:T(1,128)} async-done(((f32[32,1,2560]{2,1,0:T(1,128)}), f32[32,1,2560]{2,1,0:T(1,128)}, u32[]{:S(2)}, u32[]{:S(2)}) %all-to-all-start) | async-done | bytes 327712 | tf_op jit(solution)/shard_map/all_to_all | solution.py:519
  31.4 2.5 %unpack.1 = (f32[80,1024]{1,0:T(8,128)S(1)}, f32[80,256]{1,0:T(8,128)S(1)}, f32[80,256]{1,0:T(8,128)S(1)}) custom-call(s32[4]{0:T(128)S(1)} %copy-done.2, s32[16,256]{1,0:T(8,128)S(1)} %plan.1.table, f32[640,128]{1,0:T(8,128)} %bitcast.6.in_ref), custom_call_target="tpu_custom_call" | custom-call | tf_op jit(solution)/shard_map/unpack/pallas_call | solution.py:473
  36.2 1.8 %collective-permute-start.3 = (f32[160,256]{1,0:T(8,128)S(1)}, f32[160,256]{1,0:T(8,128)S(1)}, u32[]{:S(2)}, u32[]{:S(2)}) collective-permute-start(f32[160,256]{1,0:T(8,128)S(1)} %shard.1), channel_id=1, source_target_pairs={{0,32},{32,64},{64,96},{96,128},{128,160},{160,192},{192,224},{224... | collective-permute-start | bytes 491528 | tf_op jit(solution)/shard_map/ppermute | solution.py:512
  38.9 2.0 %collective-permute-start.8 = (f32[160,256]{1,0:T(8,128)S(1)}, f32[160,256]{1,0:T(8,128)S(1)}, u32[]{:S(2)}, u32[]{:S(2)}) collective-permute-start(f32[160,256]{1,0:T(8,128)S(1)} %shard.1), channel_id=1, source_target_pairs={{0,64},{32,96},{64,128},{96,160},{128,192},{160,224},{192,0},{224,... | collective-permute-start | bytes 491528 | tf_op jit(solution)/shard_map/ppermute | solution.py:512
  40.9 2.6 %collective-permute-done.4 = f32[160,256]{1,0:T(8,128)S(1)} collective-permute-done((f32[160,256]{1,0:T(8,128)S(1)}, f32[160,256]{1,0:T(8,128)S(1)}, u32[]{:S(2)}, u32[]{:S(2)}) %collective-permute-start.4) | collective-permute-done | bytes 163872 | tf_op jit(solution)/shard_map/ppermute | solution.py:512
  43.5 3.5 %collective-permute-done.3 = f32[160,256]{1,0:T(8,128)S(1)} collective-permute-done((f32[160,256]{1,0:T(8,128)S(1)}, f32[160,256]{1,0:T(8,128)S(1)}, u32[]{:S(2)}, u32[]{:S(2)}) %collective-permute-start.3) | collective-permute-done | bytes 163872 | tf_op jit(solution)/shard_map/ppermute | solution.py:512
  47.2 2.0 %collective-permute-start.5 = (f32[480,256]{1,0:T(8,128)S(1)}, f32[480,256]{1,0:T(8,128)S(1)}, u32[]{:S(2)}, u32[]{:S(2)}) collective-permute-start(f32[480,256]{1,0:T(8,128)S(1)} %pad_maximum_fusion.refs_0_), channel_id=1, source_target_pairs={{0,8},{8,16},{16,24},{24,0},{1,9},{9,17},{17,25},{25,1},{2,10},{10... | collective-permute-start | bytes 1474568 | tf_op jit(solution)/shard_map/ppermute | solution.py:512
  52.8 3.4 %collective-permute-done.7.refs_1_ = f32[80,1024]{1,0:T(8,128)S(1)} collective-permute-done((f32[80,1024]{1,0:T(8,128)S(1)}, f32[80,1024]{1,0:T(8,128)S(1)}, u32[]{:S(2)}, u32[]{:S(2)}) %collective-permute-start.7) | collective-permute-done | bytes 327712 | tf_op jit(solution)/shard_map/ppermute | solution.py:512
  56.2 1.7 %collective-permute-start.14 = (f32[80,1024]{1,0:T(8,128)S(1)}, f32[80,1024]{1,0:T(8,128)S(1)}, u32[]{:S(2)}, u32[]{:S(2)}) collective-permute-start(f32[80,1024]{1,0:T(8,128)S(1)} %get-tuple-element.98.refs_0_), channel_id=1, source_target_pairs={{0,3},{1,0},{2,1},{3,2},{4,7},{5,4},{6,5},{7,6},{8,11},{9,8},{10,9... | collective-permute-start | bytes 983048 | tf_op jit(solution)/shard_map/ppermute | solution.py:512
  58.0 7.3 %screen.1 = (bf16[640,1664]{1,0:T(8,128)(2,1)S(1)}, bf16[640,1664]{1,0:T(8,128)(2,1)S(1)}, bf16[640,640]{1,0:T(8,128)(2,1)S(1)}, bf16[640,640]{1,0:T(8,128)(2,1)...) custom-call(s32[4]{0:T(128)S(1)} %copy-done.3, f32[320,2560]{1,0:T(8,128)S(1)} %bitcast.10, ...), custom_call_target="tpu_custom_call" | custom-call | tf_op jit(solution)/shard_map/screen/pallas_call | solution.py:153
  65.6 3.2 %collective-permute-start.11 = (f32[160,256]{1,0:T(8,128)S(1)}, f32[160,256]{1,0:T(8,128)S(1)}, u32[]{:S(2)}, u32[]{:S(2)}) collective-permute-start(f32[160,256]{1,0:T(8,128)S(1)} %collective-permute-done.9), channel_id=1, source_target_pairs={{0,224},{32,0},{64,32},{96,64},{128,96},{160,128},{192,160},{224,1... | collective-permute-start | bytes 491528 | tf_op jit(solution)/shard_map/ppermute | solution.py:512
  69.5 2.6 %collective-permute-done.10.refs_0_ = f32[160,256]{1,0:T(8,128)S(1)} collective-permute-done((f32[160,256]{1,0:T(8,128)S(1)}, f32[160,256]{1,0:T(8,128)S(1)}, u32[]{:S(2)}, u32[]{:S(2)}) %collective-permute-start.10) | collective-permute-done | bytes 163872 | tf_op jit(solution)/shard_map/ppermute | solution.py:512
  73.6 3.3 %collective-permute-start.18 = (f32[400,256]{1,0:T(8,128)S(1)}, f32[400,256]{1,0:T(8,128)S(1)}, u32[]{:S(2)}, u32[]{:S(2)}) collective-permute-start(f32[400,256]{1,0:T(8,128)S(1)} %get-tuple-element.139), channel_id=1, source_target_pairs={{0,224},{32,0},{64,32},{96,64},{128,96},{160,128},{192,160},{224,1... | collective-permute-start | bytes 1228808 | tf_op jit(solution)/shard_map/ppermute | solution.py:512
  79.2 1.7 %collective-permute-done.19.refs_2_ = f32[80,1024]{1,0:T(8,128)S(1)} collective-permute-done((f32[80,1024]{1,0:T(8,128)S(1)}, f32[80,1024]{1,0:T(8,128)S(1)}, u32[]{:S(2)}, u32[]{:S(2)}) %collective-permute-start.19) | collective-permute-done | bytes 327712 | tf_op jit(solution)/shard_map/ppermute | solution.py:512
  80.9 1.6 %collective-permute-done.22.refs_7_ = f32[80,1024]{1,0:T(8,128)S(1)} collective-permute-done((f32[80,1024]{1,0:T(8,128)S(1)}, f32[80,1024]{1,0:T(8,128)S(1)}, u32[]{:S(2)}, u32[]{:S(2)}) %collective-permute-start.22) | collective-permute-done | bytes 327712 | tf_op jit(solution)/shard_map/ppermute | solution.py:513
  82.5 2.4 %collective-permute-done.16.refs_7_ = f32[400,256]{1,0:T(8,128)S(1)} collective-permute-done((f32[400,256]{1,0:T(8,128)S(1)}, f32[400,256]{1,0:T(8,128)S(1)}, u32[]{:S(2)}, u32[]{:S(2)}) %collective-permute-start.16) | collective-permute-done | bytes 409632 | tf_op jit(solution)/shard_map/ppermute | solution.py:512
  84.9 2.7 %collective-permute-done.17.refs_2_.refs_0_ = f32[400,256]{1,0:T(8,128)S(1)} collective-permute-done((f32[400,256]{1,0:T(8,128)S(1)}, f32[400,256]{1,0:T(8,128)S(1)}, u32[]{:S(2)}, u32[]{:S(2)}) %collective-permute-start.17) | collective-permute-done | bytes 409632 | tf_op jit(solution)/shard_map/ppermute | solution.py:512
  87.7 3.2 %collective-permute-start.26 = (f32[160,256]{1,0:T(8,128)S(1)}, f32[160,256]{1,0:T(8,128)S(1)}, u32[]{:S(2)}, u32[]{:S(2)}) collective-permute-start(f32[160,256]{1,0:T(8,128)S(1)} %slice.49), channel_id=1, source_target_pairs={{0,224},{32,0},{64,32},{96,64},{128,96},{160,128},{192,160},{224,1... | collective-permute-start | bytes 491528 | tf_op jit(solution)/shard_map/ppermute | solution.py:512
  91.3 1.8 %collective-permute-start.23 = (f32[160,256]{1,0:T(8,128)S(1)}, f32[160,256]{1,0:T(8,128)S(1)}, u32[]{:S(2)}, u32[]{:S(2)}) collective-permute-start(f32[160,256]{1,0:T(8,128)S(1)} %slice.48), channel_id=1, source_target_pairs={{0,8},{8,16},{16,24},{24,0},{1,9},{9,17},{17,25},{25,1},{2,10},{10... | collective-permute-start | bytes 491528 | tf_op jit(solution)/shard_map/ppermute | solution.py:512
  93.1 5.0 %group.2.refs_8_ = f32[640,512]{1,0:T(8,128)S(1)} custom-call(s32[4]{0:T(128)S(1)} %copy-done.3, f32[480,256]{1,0:T(8,128)S(1)} %pad_maximum_fusion.refs_0_, f32[480,256]{1,0:T(8,128)S(1)} %collective-permute-done.5.refs_1_, f32[480,256]{1,0:T(8,128)S(1)} %collective-permute-done.6.refs_2_, f32[320,256]{1,0:T(8,128)S(1)} %constant_dynamic-update-slice_fusion.refs_3_, ...), custom_call_target="tpu_custom_call" | custom-call | tf_op jit(solution)/shard_map/group/pallas_call | solution.py:252
  101.0 2.1 %left.1 = (bf16[1024,640]{1,0:T(8,128)(2,1)S(1)}, bf16[1024,640]{1,0:T(8,128)(2,1)S(1)}) custom-call(s32[4]{0:T(128)S(1)} %copy-done.3, f32[80,1024]{1,0:T(8,128)S(1)} %get-tuple-element.98.refs_0_, f32[80,1024]{1,0:T(8,128)S(1)} %collective-permute-done.7.refs_1_, f32[80,1024]{1,0:T(8,128)S(1)} %collective-permute-done.19.refs_2_, ...), custom_call_target="tpu_custom_call" | custom-call | tf_op jit(solution)/shard_map/left/pallas_call | solution.py:185
  103.1 2.5 %group.3.refs_8_ = f32[640,512]{1,0:T(8,128)S(1)} custom-call(s32[4]{0:T(128)S(1)} %copy-done.3, f32[160,256]{1,0:T(8,128)S(1)} %collective-permute-done.10.refs_0_, f32[160,256]{1,0:T(8,128)S(1)} %collective-permute-done.11.refs_1_, f32[400,256]{1,0:T(8,128)S(1)} %collective-permute-done.17.refs_2_.refs_0_, ...), custom_call_target="tpu_custom_call" | custom-call | tf_op jit(solution)/shard_map/group/pallas_call | solution.py:252
  105.7 9.2 %pair.1 = (f32[4,8,3584]{2,1,0:T(8,128)S(1)}, f32[1024,512]{1,0:T(8,128)S(1)}) custom-call(s32[4]{0:T(128)S(1)} %copy-done.3, s32[16,256]{1,0:T(8,128)S(1)} %plan.1.table, f32[400,256]{1,0:T(8,128)S(1)} %collective-permute-done.17.refs_2_.refs_0_, f32[400,256]{1,0:T(8,128)S(1)} %collective-permute-done.18.refs_3_.refs_1_, ...), custom_call_target="tpu_custom_call" | custom-call | tf_op jit(solution)/shard_map/pair/pallas_call | solution.py:310
  114.9 3.0 %extract.1.one_ref = f32[4,8,3584]{2,1,0:T(8,128)S(1)} custom-call(s32[4]{0:T(128)S(1)} %copy-done.3, s32[16,256]{1,0:T(8,128)S(1)} %plan.1.table, f32[1024,512]{1,0:T(8,128)S(1)} %get-tuple-element.129.kern), custom_call_target="tpu_custom_call" | custom-call | tf_op jit(solution)/shard_map/extract/pallas_call | solution.py:329
  118.0 2.7 %collective-permute-start.31 = (f32[8,3584]{1,0:T(8,128)S(1)}, f32[8,3584]{1,0:T(8,128)S(1)}, u32[]{:S(2)}, u32[]{:S(2)}) collective-permute-start(f32[8,3584]{1,0:T(8,128)S(1)} %get-tuple-element.132), channel_id=1, source_target_pairs={{0,1},{1,2},{2,3},{3,0},{4,5},{5,6},{6,7},{7,4},{8,9},{9,10},{10,1... | collective-permute-start | bytes 344072 | tf_op jit(solution)/shard_map/ppermute | solution.py:512
  121.3 2.1 %collective-permute-start.33 = (f32[8,3584]{1,0:T(8,128)S(1)}, f32[8,3584]{1,0:T(8,128)S(1)}, u32[]{:S(2)}, u32[]{:S(2)}) collective-permute-start(f32[8,3584]{1,0:T(8,128)S(1)} %get-tuple-element.134), channel_id=1, source_target_pairs={{0,3},{1,0},{2,1},{3,2},{4,7},{5,4},{6,5},{7,6},{8,11},{9,8},{10,9... | collective-permute-start | bytes 344072 | tf_op jit(solution)/shard_map/ppermute | solution.py:512
  123.4 3.1 %collective-permute-done.31.two_ref = f32[8,3584]{1,0:T(8,128)S(1)} collective-permute-done((f32[8,3584]{1,0:T(8,128)S(1)}, f32[8,3584]{1,0:T(8,128)S(1)}, u32[]{:S(2)}, u32[]{:S(2)}) %collective-permute-start.31) | collective-permute-done | bytes 114720 | tf_op jit(solution)/shard_map/ppermute | solution.py:512
  126.5 1.7 %collective-permute-done.32.three_ref = f32[8,3584]{1,0:T(8,128)S(1)} collective-permute-done((f32[8,3584]{1,0:T(8,128)S(1)}, f32[8,3584]{1,0:T(8,128)S(1)}, u32[]{:S(2)}, u32[]{:S(2)}) %collective-permute-start.32) | collective-permute-done | bytes 114720 | tf_op jit(solution)/shard_map/ppermute | solution.py:512
  130.2 18.7 %all_to_all.10.parts_ref = f32[32,8,256]{2,1,0:T(8,128)S(1)} all-to-all(f32[32,8,256]{2,1,0:T(8,128)S(1)} %owner.1), channel_id=1, replica_groups=mesh['z'=8,'y'=4,'core'=2,'x'=4] {'z','y'}, dimensions={0} | all-to-all | bytes 524288 | tf_op jit(solution)/shard_map/all_to_all | solution.py:574
  149.0 1.5 %last.1 = f32[12,8,16]{2,1,0:T(8,128)} custom-call(s32[4]{0:T(128)S(1)} %copy-done.3, s32[16,256]{1,0:T(8,128)S(1)} %plan.1.table, f32[32,8,256]{2,1,0:T(8,128)S(1)} %all_to_all.10.parts_ref), custom_call_target="tpu_custom_call" | custom-call | tf_op jit(solution)/shard_map/last/pallas_call | solution.py:391
  (78 shorter events, 23.9 us)
Async XLA Ops:
  4.2 26.6 %collective-permute-start.1 = (f32[320,2560]{1,0:T(8,128)}, f32[320,2560]{1,0:T(8,128)}, u32[]{:S(2)}, u32[]{:S(2)}) collective-permute-start(f32[320,2560]{1,0:T(8,128)} %bitcast.9), channel_id=1, source_target_pairs={{0,4},{4,0},{1,5},{5,1},{2,6},{6,2},{3,7},{7,3},{8,12},{12,8},{9,1... | collective-permute-start | bytes 9830408 | tf_op jit(solution)/shard_map/ppermute | solution.py:513
  4.4 26.4 %all-to-all-start = ((f32[32,1,2560]{2,1,0:T(1,128)}), f32[32,1,2560]{2,1,0:T(1,128)}, u32[]{:S(2)}, u32[]{:S(2)}) async-start(f32[32,1,2560]{2,1,0:T(1,128)} %bitcast.12), calls=%async_computation | async-start | bytes 655360 | tf_op jit(solution)/shard_map/all_to_all | solution.py:519
  35.9 7.6 %collective-permute-start.4 = (f32[160,256]{1,0:T(8,128)S(1)}, f32[160,256]{1,0:T(8,128)S(1)}, u32[]{:S(2)}, u32[]{:S(2)}) collective-permute-start(f32[160,256]{1,0:T(8,128)S(1)} %shard.1), channel_id=1, source_target_pairs={{0,224},{32,0},{64,32},{96,64},{128,96},{160,128},{192,160},{224,1... | collective-permute-start | bytes 491528 | tf_op jit(solution)/shard_map/ppermute | solution.py:512
  36.2 10.9 %collective-permute-start.3 = (f32[160,256]{1,0:T(8,128)S(1)}, f32[160,256]{1,0:T(8,128)S(1)}, u32[]{:S(2)}, u32[]{:S(2)}) collective-permute-start(f32[160,256]{1,0:T(8,128)S(1)} %shard.1), channel_id=1, source_target_pairs={{0,32},{32,64},{64,96},{96,128},{128,160},{160,192},{192,224},{224... | collective-permute-start | bytes 491528 | tf_op jit(solution)/shard_map/ppermute | solution.py:512
  38.0 12.7 %collective-permute-start.9 = (f32[160,256]{1,0:T(8,128)S(1)}, f32[160,256]{1,0:T(8,128)S(1)}, u32[]{:S(2)}, u32[]{:S(2)}) collective-permute-start(f32[160,256]{1,0:T(8,128)S(1)} %shard.1), channel_id=1, source_target_pairs={{0,192},{32,224},{64,0},{96,32},{128,64},{160,96},{192,128},{224,1... | collective-permute-start | bytes 491528 | tf_op jit(solution)/shard_map/ppermute | solution.py:512
  38.9 11.7 %collective-permute-start.8 = (f32[160,256]{1,0:T(8,128)S(1)}, f32[160,256]{1,0:T(8,128)S(1)}, u32[]{:S(2)}, u32[]{:S(2)}) collective-permute-start(f32[160,256]{1,0:T(8,128)S(1)} %shard.1), channel_id=1, source_target_pairs={{0,64},{32,96},{64,128},{96,160},{128,192},{160,224},{192,0},{224,... | collective-permute-start | bytes 491528 | tf_op jit(solution)/shard_map/ppermute | solution.py:512
  47.1 18.3 %collective-permute-start.6 = (f32[480,256]{1,0:T(8,128)S(1)}, f32[480,256]{1,0:T(8,128)S(1)}, u32[]{:S(2)}, u32[]{:S(2)}) collective-permute-start(f32[480,256]{1,0:T(8,128)S(1)} %pad_maximum_fusion.refs_0_), channel_id=1, source_target_pairs={{0,24},{8,0},{16,8},{24,16},{1,25},{9,1},{17,9},{25,17},{2,26},{10... | collective-permute-start | bytes 1474568 | tf_op jit(solution)/shard_map/ppermute | solution.py:512
  47.2 18.2 %collective-permute-start.5 = (f32[480,256]{1,0:T(8,128)S(1)}, f32[480,256]{1,0:T(8,128)S(1)}, u32[]{:S(2)}, u32[]{:S(2)}) collective-permute-start(f32[480,256]{1,0:T(8,128)S(1)} %pad_maximum_fusion.refs_0_), channel_id=1, source_target_pairs={{0,8},{8,16},{16,24},{24,0},{1,9},{9,17},{17,25},{25,1},{2,10},{10... | collective-permute-start | bytes 1474568 | tf_op jit(solution)/shard_map/ppermute | solution.py:512
  49.2 7.1 %collective-permute-start.7 = (f32[80,1024]{1,0:T(8,128)S(1)}, f32[80,1024]{1,0:T(8,128)S(1)}, u32[]{:S(2)}, u32[]{:S(2)}) collective-permute-start(f32[80,1024]{1,0:T(8,128)S(1)} %get-tuple-element.98.refs_0_), channel_id=1, source_target_pairs={{0,1},{1,2},{2,3},{3,0},{4,5},{5,6},{6,7},{7,4},{8,9},{9,10},{10,1... | collective-permute-start | bytes 983048 | tf_op jit(solution)/shard_map/ppermute | solution.py:512
  50.7 18.2 %collective-permute-start.13 = (f32[320,256]{1,0:T(8,128)S(1)}, f32[320,256]{1,0:T(8,128)S(1)}, u32[]{:S(2)}, u32[]{:S(2)}) collective-permute-start(f32[320,256]{1,0:T(8,128)S(1)} %constant_dynamic-update-slice_fusion.refs_3_), channel_id=1, source_target_pairs={{0,24},{8,0},{16,8},{24,16},{1,25},{9,1},{17,9},{25,17},{2,26},{10... | collective-permute-start | bytes 983048 | tf_op jit(solution)/shard_map/ppermute | solution.py:512
  52.1 16.9 %collective-permute-start.12 = (f32[320,256]{1,0:T(8,128)S(1)}, f32[320,256]{1,0:T(8,128)S(1)}, u32[]{:S(2)}, u32[]{:S(2)}) collective-permute-start(f32[320,256]{1,0:T(8,128)S(1)} %constant_dynamic-update-slice_fusion.refs_3_), channel_id=1, source_target_pairs={{0,8},{8,16},{16,24},{24,0},{1,9},{9,17},{17,25},{25,1},{2,10},{10... | collective-permute-start | bytes 983048 | tf_op jit(solution)/shard_map/ppermute | solution.py:512
  56.2 13.3 %collective-permute-start.14 = (f32[80,1024]{1,0:T(8,128)S(1)}, f32[80,1024]{1,0:T(8,128)S(1)}, u32[]{:S(2)}, u32[]{:S(2)}) collective-permute-start(f32[80,1024]{1,0:T(8,128)S(1)} %get-tuple-element.98.refs_0_), channel_id=1, source_target_pairs={{0,3},{1,0},{2,1},{3,2},{4,7},{5,4},{6,5},{7,6},{8,11},{9,8},{10,9... | collective-permute-start | bytes 983048 | tf_op jit(solution)/shard_map/ppermute | solution.py:512
  65.4 6.8 %collective-permute-start.10 = (f32[160,256]{1,0:T(8,128)S(1)}, f32[160,256]{1,0:T(8,128)S(1)}, u32[]{:S(2)}, u32[]{:S(2)}) collective-permute-start(f32[160,256]{1,0:T(8,128)S(1)} %collective-permute-done.8), channel_id=1, source_target_pairs={{0,32},{32,64},{64,96},{96,128},{128,160},{160,192},{192,224},{224... | collective-permute-start | bytes 491528 | tf_op jit(solution)/shard_map/ppermute | solution.py:512
  65.6 6.5 %collective-permute-start.11 = (f32[160,256]{1,0:T(8,128)S(1)}, f32[160,256]{1,0:T(8,128)S(1)}, u32[]{:S(2)}, u32[]{:S(2)}) collective-permute-start(f32[160,256]{1,0:T(8,128)S(1)} %collective-permute-done.9), channel_id=1, source_target_pairs={{0,224},{32,0},{64,32},{96,64},{128,96},{160,128},{192,160},{224,1... | collective-permute-start | bytes 491528 | tf_op jit(solution)/shard_map/ppermute | solution.py:512
  68.9 9.4 %collective-permute-start.20 = (f32[80,1024]{1,0:T(8,128)S(1)}, f32[80,1024]{1,0:T(8,128)S(1)}, u32[]{:S(2)}, u32[]{:S(2)}) collective-permute-start(f32[80,1024]{1,0:T(8,128)S(1)} %get-tuple-element.98.refs_0_), channel_id=1, source_target_pairs={{0,4},{4,0},{1,5},{5,1},{2,6},{6,2},{3,7},{7,3},{8,12},{12,8},{9,1... | collective-permute-start | bytes 983048 | tf_op jit(solution)/shard_map/ppermute | solution.py:513
  69.0 9.4 %collective-permute-start.21 = (f32[80,1024]{1,0:T(8,128)S(1)}, f32[80,1024]{1,0:T(8,128)S(1)}, u32[]{:S(2)}, u32[]{:S(2)}) collective-permute-start(f32[80,1024]{1,0:T(8,128)S(1)} %collective-permute-done.7.refs_1_), channel_id=1, source_target_pairs={{0,4},{4,0},{1,5},{5,1},{2,6},{6,2},{3,7},{7,3},{8,12},{12,8},{9,1... | collective-permute-start | bytes 983048 | tf_op jit(solution)/shard_map/ppermute | solution.py:513
  72.2 8.7 %collective-permute-start.19 = (f32[80,1024]{1,0:T(8,128)S(1)}, f32[80,1024]{1,0:T(8,128)S(1)}, u32[]{:S(2)}, u32[]{:S(2)}) collective-permute-start(f32[80,1024]{1,0:T(8,128)S(1)} %get-tuple-element.98.refs_0_), channel_id=1, source_target_pairs={{0,2},{1,3},{2,0},{3,1},{4,6},{5,7},{6,4},{7,5},{8,10},{9,11},{10,... | collective-permute-start | bytes 983048 | tf_op jit(solution)/shard_map/ppermute | solution.py:512
  73.6 8.9 %collective-permute-start.18 = (f32[400,256]{1,0:T(8,128)S(1)}, f32[400,256]{1,0:T(8,128)S(1)}, u32[]{:S(2)}, u32[]{:S(2)}) collective-permute-start(f32[400,256]{1,0:T(8,128)S(1)} %get-tuple-element.139), channel_id=1, source_target_pairs={{0,224},{32,0},{64,32},{96,64},{128,96},{160,128},{192,160},{224,1... | collective-permute-start | bytes 1228808 | tf_op jit(solution)/shard_map/ppermute | solution.py:512
  76.9 8.0 %collective-permute-start.16 = (f32[400,256]{1,0:T(8,128)S(1)}, f32[400,256]{1,0:T(8,128)S(1)}, u32[]{:S(2)}, u32[]{:S(2)}) collective-permute-start(f32[400,256]{1,0:T(8,128)S(1)} %get-tuple-element.140), channel_id=1, source_target_pairs={{0,24},{8,0},{16,8},{24,16},{1,25},{9,1},{17,9},{25,17},{2,26},{10... | collective-permute-start | bytes 1228808 | tf_op jit(solution)/shard_map/ppermute | solution.py:512
  78.3 9.2 %collective-permute-start.17 = (f32[400,256]{1,0:T(8,128)S(1)}, f32[400,256]{1,0:T(8,128)S(1)}, u32[]{:S(2)}, u32[]{:S(2)}) collective-permute-start(f32[400,256]{1,0:T(8,128)S(1)} %get-tuple-element.141), channel_id=1, source_target_pairs={{0,32},{32,64},{64,96},{96,128},{128,160},{160,192},{192,224},{224... | collective-permute-start | bytes 1228808 | tf_op jit(solution)/shard_map/ppermute | solution.py:512
  78.4 9.2 %collective-permute-start.15 = (f32[400,256]{1,0:T(8,128)S(1)}, f32[400,256]{1,0:T(8,128)S(1)}, u32[]{:S(2)}, u32[]{:S(2)}) collective-permute-start(f32[400,256]{1,0:T(8,128)S(1)} %get-tuple-element.142), channel_id=1, source_target_pairs={{0,8},{8,16},{16,24},{24,0},{1,9},{9,17},{17,25},{25,1},{2,10},{10... | collective-permute-start | bytes 1228808 | tf_op jit(solution)/shard_map/ppermute | solution.py:512
  87.6 11.0 %collective-permute-start.27 = (f32[80,1024]{1,0:T(8,128)S(1)}, f32[80,1024]{1,0:T(8,128)S(1)}, u32[]{:S(2)}, u32[]{:S(2)}) collective-permute-start(f32[80,1024]{1,0:T(8,128)S(1)} %collective-permute-done.19.refs_2_), channel_id=1, source_target_pairs={{0,4},{4,0},{1,5},{5,1},{2,6},{6,2},{3,7},{7,3},{8,12},{12,8},{9,1... | collective-permute-start | bytes 983048 | tf_op jit(solution)/shard_map/ppermute | solution.py:513
  87.7 10.4 %collective-permute-start.26 = (f32[160,256]{1,0:T(8,128)S(1)}, f32[160,256]{1,0:T(8,128)S(1)}, u32[]{:S(2)}, u32[]{:S(2)}) collective-permute-start(f32[160,256]{1,0:T(8,128)S(1)} %slice.49), channel_id=1, source_target_pairs={{0,224},{32,0},{64,32},{96,64},{128,96},{160,128},{192,160},{224,1... | collective-permute-start | bytes 491528 | tf_op jit(solution)/shard_map/ppermute | solution.py:512
  90.9 7.2 %collective-permute-start.24 = (f32[160,256]{1,0:T(8,128)S(1)}, f32[160,256]{1,0:T(8,128)S(1)}, u32[]{:S(2)}, u32[]{:S(2)}) collective-permute-start(f32[160,256]{1,0:T(8,128)S(1)} %slice.49), channel_id=1, source_target_pairs={{0,24},{8,0},{16,8},{24,16},{1,25},{9,1},{17,9},{25,17},{2,26},{10... | collective-permute-start | bytes 491528 | tf_op jit(solution)/shard_map/ppermute | solution.py:512
  91.2 7.3 %collective-permute-start.25 = (f32[160,256]{1,0:T(8,128)S(1)}, f32[160,256]{1,0:T(8,128)S(1)}, u32[]{:S(2)}, u32[]{:S(2)}) collective-permute-start(f32[160,256]{1,0:T(8,128)S(1)} %slice.48), channel_id=1, source_target_pairs={{0,32},{32,64},{64,96},{96,128},{128,160},{160,192},{192,224},{224... | collective-permute-start | bytes 491528 | tf_op jit(solution)/shard_map/ppermute | solution.py:512
  91.3 7.3 %collective-permute-start.23 = (f32[160,256]{1,0:T(8,128)S(1)}, f32[160,256]{1,0:T(8,128)S(1)}, u32[]{:S(2)}, u32[]{:S(2)}) collective-permute-start(f32[160,256]{1,0:T(8,128)S(1)} %slice.48), channel_id=1, source_target_pairs={{0,8},{8,16},{16,24},{24,0},{1,9},{9,17},{17,25},{25,1},{2,10},{10... | collective-permute-start | bytes 491528 | tf_op jit(solution)/shard_map/ppermute | solution.py:512
  98.7 7.0 %collective-permute-start.29 = (f32[80,256]{1,0:T(8,128)S(1)}, f32[80,256]{1,0:T(8,128)S(1)}, u32[]{:S(2)}, u32[]{:S(2)}) collective-permute-start(f32[80,256]{1,0:T(8,128)S(1)} %slice.51), channel_id=1, source_target_pairs={{0,24},{8,0},{16,8},{24,16},{1,25},{9,1},{17,9},{25,17},{2,26},{10... | collective-permute-start | bytes 245768 | tf_op jit(solution)/shard_map/ppermute | solution.py:512
  100.0 5.7 %collective-permute-start.28 = (f32[80,256]{1,0:T(8,128)S(1)}, f32[80,256]{1,0:T(8,128)S(1)}, u32[]{:S(2)}, u32[]{:S(2)}) collective-permute-start(f32[80,256]{1,0:T(8,128)S(1)} %slice.50), channel_id=1, source_target_pairs={{0,8},{8,16},{16,24},{24,0},{1,9},{9,17},{17,25},{25,1},{2,10},{10... | collective-permute-start | bytes 245768 | tf_op jit(solution)/shard_map/ppermute | solution.py:512
  114.8 3.1 %collective-permute-start.30 = (f32[4,8,3584]{2,1,0:T(8,128)S(1)}, f32[4,8,3584]{2,1,0:T(8,128)S(1)}, u32[]{:S(2)}, u32[]{:S(2)}) collective-permute-start(f32[4,8,3584]{2,1,0:T(8,128)S(1)} %get-tuple-element.130), channel_id=1, source_target_pairs={{0,4},{4,0},{1,5},{5,1},{2,6},{6,2},{3,7},{7,3},{8,12},{12,8},{9,1... | collective-permute-start | bytes 1376264 | tf_op jit(solution)/shard_map/ppermute | solution.py:513
  118.0 8.5 %collective-permute-start.31 = (f32[8,3584]{1,0:T(8,128)S(1)}, f32[8,3584]{1,0:T(8,128)S(1)}, u32[]{:S(2)}, u32[]{:S(2)}) collective-permute-start(f32[8,3584]{1,0:T(8,128)S(1)} %get-tuple-element.132), channel_id=1, source_target_pairs={{0,1},{1,2},{2,3},{3,0},{4,5},{5,6},{6,7},{7,4},{8,9},{9,10},{10,1... | collective-permute-start | bytes 344072 | tf_op jit(solution)/shard_map/ppermute | solution.py:512
  120.7 7.5 %collective-permute-start.32 = (f32[8,3584]{1,0:T(8,128)S(1)}, f32[8,3584]{1,0:T(8,128)S(1)}, u32[]{:S(2)}, u32[]{:S(2)}) collective-permute-start(f32[8,3584]{1,0:T(8,128)S(1)} %get-tuple-element.133), channel_id=1, source_target_pairs={{0,2},{1,3},{2,0},{3,1},{4,6},{5,7},{6,4},{7,5},{8,10},{9,11},{10,... | collective-permute-start | bytes 344072 | tf_op jit(solution)/shard_map/ppermute | solution.py:512
  121.3 7.7 %collective-permute-start.33 = (f32[8,3584]{1,0:T(8,128)S(1)}, f32[8,3584]{1,0:T(8,128)S(1)}, u32[]{:S(2)}, u32[]{:S(2)}) collective-permute-start(f32[8,3584]{1,0:T(8,128)S(1)} %get-tuple-element.134), channel_id=1, source_target_pairs={{0,3},{1,0},{2,1},{3,2},{4,7},{5,4},{6,5},{7,6},{8,11},{9,8},{10,9... | collective-permute-start | bytes 344072 | tf_op jit(solution)/shard_map/ppermute | solution.py:512
  (8 other events, 90.9 us)

commit v3 on v0

--- a/solution.py
+++ b/solution.py
@@ -538,19 +538,16 @@
     first_down, first_up, around[1], below2, above2, *screens = hold(
         (first_down, first_up, around[1], below2, above2, *screens)
     )
-    around[2] = shift(after(columns, first_down), "x", 2)
-    swapped = [swap(columns), swap(around[1]), None, None]
-    second_down, second_up, first_down, swapped[0], swapped[1] = hold(
-        (second_down, second_up, first_down, swapped[0], swapped[1])
-    )
+    second_down, second_up, first_down, around[3] = hold((second_down, second_up, first_down, around[3]))
 
     z_below = shift(join(second_down[:block], second_up[:block], second[:block]), "z", 1)
     z_above = shift(join(second_down[block:], second_up[block:], second[block:]), "z", -1)
     two_down = shift(join(first_down[: 3 * SPAN], second_down[:block]), "y", 1)
     two_up = shift(join(first_up[3 * SPAN :], second_up[block:]), "y", -1)
-    swapped[3] = swap(around[3])
-    two_down, two_up, z_below, z_above, around[2], swapped[3] = hold(
-        (two_down, two_up, z_below, z_above, around[2], swapped[3])
+    around[2] = shift(after(columns, second_down), "x", 2)
+    swapped = [swap(columns), swap(around[1]), None, None]
+    two_down, two_up, z_below, z_above, around[2], swapped[0], swapped[1] = hold(
+        (two_down, two_up, z_below, z_above, around[2], swapped[0], swapped[1])
     )
 
     y_below, y_above = shift(z_below[:block], "y", 1), shift(z_above[block : 2 * block], "y", -1)
@@ -558,9 +555,9 @@
     far_above = shift(join(z_above[block : 2 * block], z_above[2 * block + SPAN :]), "z", -1)
     rights = (first, first_down, first_up, second, second_down, second_up, two_down, two_up)
     total = group_call(near_runs, len(NEAR), place, rights, screens[:2], ())
-    swapped[2] = swap(around[2])
-    y_below, y_above, far_below, far_above, total, swapped[2] = hold(
-        (y_below, y_above, far_below, far_above, total, swapped[2])
+    swapped[2:] = [swap(array) for array in around[2:]]
+    y_below, y_above, far_below, far_above, total, *swapped[2:] = hold(
+        (y_below, y_above, far_below, far_above, total, *swapped[2:])
     )
 
     across_low, across_high = shift(far_below[:SPAN], "y", 1), shift(far_above[SPAN : 2 * SPAN], "y", -1)

time: 156 us -> 145 us (0.929)
  waiting for transfers between devices: 47.9 us -> 37 us
  blocking collectives: 19.4 us -> 16.3 us
  starting transfers between devices: 46.2 us -> 49.1 us
    ppermute x24, waiting for transfers between devices: 33.9 us -> 21.5 us  [shards(): lax.ppermute(array, axis, ring(lax.axis_size(axis), by))]
    all_to_all x1, blocking collectives: 19.4 us -> 16.3 us  [shards(): parts = lax.all_to_all(parts, ('z', 'y'), 0, 0, tiled=True)]
    ppermute x24, starting transfers between devices: 33.7 us -> 36.7 us  [shards(): lax.ppermute(array, axis, ring(lax.axis_size(axis), by))]
    ppermute x8, waiting for transfers between devices: 2.59 us -> 4.21 us  [shards(): swap = lambda array: lax.ppermute(array, 'core', SWAP)]
  transfers between devices with their start and end apart: 33 -> 33, of which waited for: 13 -> 16; matrix products, arithmetic and copies ran while one was open for 1% -> 1% of each run, Pallas kernels for 14% -> 15%
where the time goes in v3:
time: 145 us
  starting transfers between devices  49.1 us (34%)
  Pallas kernels  38.5 us (27%)
  waiting for transfers between devices  37 us (26%)
  blocking collectives  16.3 us (11%)
  local copies, waits for them, and re-layouts  2.98 us (2%)
    ppermute x24, starting transfers between devices, shards(): lax.ppermute(array, axis, ring(lax.axis_size(axis), by))  36.7 us
    ppermute x24, waiting for transfers between devices, shards(): lax.ppermute(array, axis, ring(lax.axis_size(axis), by))  21.5 us
    all_to_all x1, blocking collectives, shards(): parts = lax.all_to_all(parts, ('z', 'y'), 0, 0, tiled=True)  16.3 us
    all_to_all x1, starting transfers between devices, shards(): lax.all_to_all(pieces.reshape(32, 1, -1), ('z', 'y'), 0, 0, tiled=True)  11.6 us
    all_to_all x1, waiting for transfers between devices, shards(): lax.all_to_all(pieces.reshape(32, 1, -1), ('z', 'y'), 0, 0, tiled=True)  11.4 us
    pallas_call x1, Pallas kernels, pair_call(): pl.pallas_call(pair_kernel, out_shape=(jax.ShapeDtypeStruct((4, 8, ROOM *...  8.88 us
    pallas_call x2, Pallas kernels, group_call(): pl.pallas_call(functools.partial(group_kernel, runs, planes), out_shape=j...  7.55 us
    pallas_call x1, Pallas kernels, screen_call(): pl.pallas_call(screen_kernel, out_shape=shapes, in_specs=[SMEM, VMEM, VME...  7.35 us
  transfers between devices with their start and end apart: 33, of which 16 were waited for; matrix products, arithmetic and copies ran while one was open for 1% of the time, Pallas kernels for 15%

profile of v3, /device:TPU:2, one launch (start us, length us, event | category | flops | bytes accessed | tf_op | source)
XLA Modules:
  0.0 145.1 jit_solution(5263558394809960735)
XLA Ops:
  2.0 2.2 %pack.1 = f32[640,128]{1,0:T(8,128)} custom-call(s32[4]{0:T(128)} %pad_add_fusion.place, f32[2,16,2560]{2,1,0:T(8,128)} %own_ref.1, f32[2,16,2560]{2,1,0:T(8,128)} %collective-permute-done.other_ref), custom_call_target="tpu_custom_call" | custom-call | tf_op jit(solution)/shard_map/pack/pallas_call | solution.py:424
  4.4 11.6 %all-to-all-start = ((f32[32,1,2560]{2,1,0:T(1,128)}), f32[32,1,2560]{2,1,0:T(1,128)}, u32[]{:S(2)}, u32[]{:S(2)}) async-start(f32[32,1,2560]{2,1,0:T(1,128)} %bitcast.12), calls=%async_computation | async-start | bytes 655360 | tf_op jit(solution)/shard_map/all_to_all | solution.py:519
  19.4 11.4 %all-to-all-done = f32[32,1,2560]{2,1,0:T(1,128)} async-done(((f32[32,1,2560]{2,1,0:T(1,128)}), f32[32,1,2560]{2,1,0:T(1,128)}, u32[]{:S(2)}, u32[]{:S(2)}) %all-to-all-start) | async-done | bytes 327712 | tf_op jit(solution)/shard_map/all_to_all | solution.py:519
  31.5 2.5 %unpack.1 = (f32[80,1024]{1,0:T(8,128)S(1)}, f32[80,256]{1,0:T(8,128)S(1)}, f32[80,256]{1,0:T(8,128)S(1)}) custom-call(s32[4]{0:T(128)S(1)} %copy-done.2, s32[16,256]{1,0:T(8,128)S(1)} %plan.1.table, f32[640,128]{1,0:T(8,128)} %bitcast.6.in_ref), custom_call_target="tpu_custom_call" | custom-call | tf_op jit(solution)/shard_map/unpack/pallas_call | solution.py:473
  36.9 2.3 %collective-permute-start.6 = (f32[160,256]{1,0:T(8,128)S(1)}, f32[160,256]{1,0:T(8,128)S(1)}, u32[]{:S(2)}, u32[]{:S(2)}) collective-permute-start(f32[160,256]{1,0:T(8,128)S(1)} %shard.1), channel_id=1, source_target_pairs={{0,224},{32,0},{64,32},{96,64},{128,96},{160,128},{192,160},{224,1... | collective-permute-start | bytes 491528 | tf_op jit(solution)/shard_map/ppermute | solution.py:512
  39.2 4.1 %collective-permute-start.4 = (f32[160,256]{1,0:T(8,128)S(1)}, f32[160,256]{1,0:T(8,128)S(1)}, u32[]{:S(2)}, u32[]{:S(2)}) collective-permute-start(f32[160,256]{1,0:T(8,128)S(1)} %shard.1), channel_id=1, source_target_pairs={{0,192},{32,224},{64,0},{96,32},{128,64},{160,96},{192,128},{224,1... | collective-permute-start | bytes 491528 | tf_op jit(solution)/shard_map/ppermute | solution.py:512
  43.4 2.6 %collective-permute-done.5 = f32[160,256]{1,0:T(8,128)S(1)} collective-permute-done((f32[160,256]{1,0:T(8,128)S(1)}, f32[160,256]{1,0:T(8,128)S(1)}, u32[]{:S(2)}, u32[]{:S(2)}) %collective-permute-start.5) | collective-permute-done | bytes 163872 | tf_op jit(solution)/shard_map/ppermute | solution.py:512
  46.5 1.5 %collective-permute-start.11 = (f32[80,1024]{1,0:T(8,128)S(1)}, f32[80,1024]{1,0:T(8,128)S(1)}, u32[]{:S(2)}, u32[]{:S(2)}) collective-permute-start(f32[80,1024]{1,0:T(8,128)S(1)} %get-tuple-element.92.refs_0_), channel_id=1, source_target_pairs={{0,1},{1,2},{2,3},{3,0},{4,5},{5,6},{6,7},{7,4},{8,9},{9,10},{10,1... | collective-permute-start | bytes 983048 | tf_op jit(solution)/shard_map/ppermute | solution.py:512
  48.1 1.6 %collective-permute-start.10 = (f32[480,256]{1,0:T(8,128)S(1)}, f32[480,256]{1,0:T(8,128)S(1)}, u32[]{:S(2)}, u32[]{:S(2)}) collective-permute-start(f32[480,256]{1,0:T(8,128)S(1)} %pad_maximum_fusion.refs_0_), channel_id=1, source_target_pairs={{0,24},{8,0},{16,8},{24,16},{1,25},{9,1},{17,9},{25,17},{2,26},{10... | collective-permute-start | bytes 1474568 | tf_op jit(solution)/shard_map/ppermute | solution.py:512
  50.7 3.0 %collective-permute-start.8 = (f32[320,256]{1,0:T(8,128)S(1)}, f32[320,256]{1,0:T(8,128)S(1)}, u32[]{:S(2)}, u32[]{:S(2)}) collective-permute-start(f32[320,256]{1,0:T(8,128)S(1)} %constant_dynamic-update-slice_fusion.refs_3_), channel_id=1, source_target_pairs={{0,24},{8,0},{16,8},{24,16},{1,25},{9,1},{17,9},{25,17},{2,26},{10... | collective-permute-start | bytes 983048 | tf_op jit(solution)/shard_map/ppermute | solution.py:512
  53.7 1.7 %collective-permute-start.12 = (f32[80,1024]{1,0:T(8,128)S(1)}, f32[80,1024]{1,0:T(8,128)S(1)}, u32[]{:S(2)}, u32[]{:S(2)}) collective-permute-start(f32[80,1024]{1,0:T(8,128)S(1)} %get-tuple-element.92.refs_0_), channel_id=1, source_target_pairs={{0,3},{1,0},{2,1},{3,2},{4,7},{5,4},{6,5},{7,6},{8,11},{9,8},{10,9... | collective-permute-start | bytes 983048 | tf_op jit(solution)/shard_map/ppermute | solution.py:512
  55.4 7.3 %screen.1 = (bf16[640,1664]{1,0:T(8,128)(2,1)S(1)}, bf16[640,1664]{1,0:T(8,128)(2,1)S(1)}, bf16[640,640]{1,0:T(8,128)(2,1)S(1)}, bf16[640,640]{1,0:T(8,128)(2,1)...) custom-call(s32[4]{0:T(128)S(1)} %copy-done.3, f32[320,2560]{1,0:T(8,128)S(1)} %bitcast.10, ...), custom_call_target="tpu_custom_call" | custom-call | tf_op jit(solution)/shard_map/screen/pallas_call | solution.py:153
  63.0 3.5 %collective-permute-done.7.refs_4_ = f32[320,256]{1,0:T(8,128)S(1)} collective-permute-done((f32[320,256]{1,0:T(8,128)S(1)}, f32[320,256]{1,0:T(8,128)S(1)}, u32[]{:S(2)}, u32[]{:S(2)}) %collective-permute-start.7) | collective-permute-done | bytes 327712 | tf_op jit(solution)/shard_map/ppermute | solution.py:512
  67.9 2.6 %collective-permute-start.16 = (f32[480,256]{1,0:T(8,128)S(1)}, f32[480,256]{1,0:T(8,128)S(1)}, u32[]{:S(2)}, u32[]{:S(2)}) collective-permute-start(f32[480,256]{1,0:T(8,128)S(1)} %pad_maximum_fusion.2), channel_id=1, source_target_pairs={{0,224},{32,0},{64,32},{96,64},{128,96},{160,128},{192,160},{224,1... | collective-permute-start | bytes 1474568 | tf_op jit(solution)/shard_map/ppermute | solution.py:512
  71.5 1.4 collective-permute-start.13
  73.0 2.3 %collective-permute-done.17.refs_2_ = f32[80,1024]{1,0:T(8,128)S(1)} collective-permute-done((f32[80,1024]{1,0:T(8,128)S(1)}, f32[80,1024]{1,0:T(8,128)S(1)}, u32[]{:S(2)}, u32[]{:S(2)}) %collective-permute-start.17) | collective-permute-done | bytes 327712 | tf_op jit(solution)/shard_map/ppermute | solution.py:512
  75.2 1.6 %collective-permute-done.19.refs_5_ = f32[80,1024]{1,0:T(8,128)S(1)} collective-permute-done((f32[80,1024]{1,0:T(8,128)S(1)}, f32[80,1024]{1,0:T(8,128)S(1)}, u32[]{:S(2)}, u32[]{:S(2)}) %collective-permute-start.19) | collective-permute-done | bytes 327712 | tf_op jit(solution)/shard_map/ppermute | solution.py:513
  77.0 2.9 %collective-permute-done.14.refs_7_ = f32[400,256]{1,0:T(8,128)S(1)} collective-permute-done((f32[400,256]{1,0:T(8,128)S(1)}, f32[400,256]{1,0:T(8,128)S(1)}, u32[]{:S(2)}, u32[]{:S(2)}) %collective-permute-start.14) | collective-permute-done | bytes 409632 | tf_op jit(solution)/shard_map/ppermute | solution.py:512
  79.9 2.5 %collective-permute-done.13.refs_6_ = f32[400,256]{1,0:T(8,128)S(1)} collective-permute-done((f32[400,256]{1,0:T(8,128)S(1)}, f32[400,256]{1,0:T(8,128)S(1)}, u32[]{:S(2)}, u32[]{:S(2)}) %collective-permute-start.13) | collective-permute-done | bytes 409632 | tf_op jit(solution)/shard_map/ppermute | solution.py:512
  82.8 2.8 %collective-permute-start.23 = (f32[240,256]{1,0:T(8,128)S(1)}, f32[240,256]{1,0:T(8,128)S(1)}, u32[]{:S(2)}, u32[]{:S(2)}) collective-permute-start(f32[240,256]{1,0:T(8,128)S(1)} %pad_maximum_fusion.6), channel_id=1, source_target_pairs={{0,224},{32,0},{64,32},{96,64},{128,96},{160,128},{192,160},{224,1... | collective-permute-start | bytes 737288 | tf_op jit(solution)/shard_map/ppermute | solution.py:512
  85.8 3.2 %collective-permute-start.21 = (f32[160,256]{1,0:T(8,128)S(1)}, f32[160,256]{1,0:T(8,128)S(1)}, u32[]{:S(2)}, u32[]{:S(2)}) collective-permute-start(f32[160,256]{1,0:T(8,128)S(1)} %slice.47), channel_id=1, source_target_pairs={{0,24},{8,0},{16,8},{24,16},{1,25},{9,1},{17,9},{25,17},{2,26},{10... | collective-permute-start | bytes 491528 | tf_op jit(solution)/shard_map/ppermute | solution.py:512
  89.0 5.0 %group.2.refs_6_ = f32[640,512]{1,0:T(8,128)S(1)} custom-call(s32[4]{0:T(128)S(1)} %copy-done.3, f32[480,256]{1,0:T(8,128)S(1)} %pad_maximum_fusion.refs_0_, f32[480,256]{1,0:T(8,128)S(1)} %collective-permute-done.9.refs_1_, f32[480,256]{1,0:T(8,128)S(1)} %collective-permute-done.10.refs_2_, f32[320,256]{1,0:T(8,128)S(1)} %constant_dynamic-update-slice_fusion.refs_3_, ...), custom_call_target="tpu_custom_call" | custom-call | tf_op jit(solution)/shard_map/group/pallas_call | solution.py:252
  95.4 3.2 %collective-permute-start.27 = (f32[80,256]{1,0:T(8,128)S(1)}, f32[80,256]{1,0:T(8,128)S(1)}, u32[]{:S(2)}, u32[]{:S(2)}) collective-permute-start(f32[80,256]{1,0:T(8,128)S(1)} %slice.51), channel_id=1, source_target_pairs={{0,24},{8,0},{16,8},{24,16},{1,25},{9,1},{17,9},{25,17},{2,26},{10... | collective-permute-start | bytes 245768 | tf_op jit(solution)/shard_map/ppermute | solution.py:512
  98.6 2.1 %left.1 = (bf16[1024,640]{1,0:T(8,128)(2,1)S(1)}, bf16[1024,640]{1,0:T(8,128)(2,1)S(1)}) custom-call(s32[4]{0:T(128)S(1)} %copy-done.3, f32[80,1024]{1,0:T(8,128)S(1)} %get-tuple-element.92.refs_0_, f32[80,1024]{1,0:T(8,128)S(1)} %collective-permute-done.11.refs_1_, f32[80,1024]{1,0:T(8,128)S(1)} %collective-permute-done.17.refs_2_, ...), custom_call_target="tpu_custom_call" | custom-call | tf_op jit(solution)/shard_map/left/pallas_call | solution.py:185
  100.7 2.5 %group.3.refs_6_ = f32[640,512]{1,0:T(8,128)S(1)} custom-call(s32[4]{0:T(128)S(1)} %copy-done.3, f32[480,256]{1,0:T(8,128)S(1)} %collective-permute-done.15.refs_0_, f32[480,256]{1,0:T(8,128)S(1)} %collective-permute-done.16.refs_1_, f32[160,256]{1,0:T(8,128)S(1)} %collective-permute-done.20.refs_2_, f32[160,256]{1,0:T(8,128)S(1)} %collective-permute-done.21.refs_3_, ...), custom_call_target="tpu_custom_call" | custom-call | tf_op jit(solution)/shard_map/group/pallas_call | solution.py:252
  103.3 8.9 %pair.1 = (f32[4,8,3584]{2,1,0:T(8,128)S(1)}, f32[1024,512]{1,0:T(8,128)S(1)}) custom-call(s32[4]{0:T(128)S(1)} %copy-done.3, s32[16,256]{1,0:T(8,128)S(1)} %plan.1.table, f32[240,256]{1,0:T(8,128)S(1)} %collective-permute-done.22.refs_0_, f32[240,256]{1,0:T(8,128)S(1)} %collective-permute-done.23.refs_1_, f32[80,256]{1,0:T(8,128)S(1)} %collective-permute-done.26.refs_2_, ...), custom_call_target="tpu_custom_call" | custom-call | tf_op jit(solution)/shard_map/pair/pallas_call | solution.py:310
  112.3 3.2 %extract.1.one_ref = f32[4,8,3584]{2,1,0:T(8,128)S(1)} custom-call(s32[4]{0:T(128)S(1)} %copy-done.3, s32[16,256]{1,0:T(8,128)S(1)} %plan.1.table, f32[1024,512]{1,0:T(8,128)S(1)} %get-tuple-element.123.kern), custom_call_target="tpu_custom_call" | custom-call | tf_op jit(solution)/shard_map/extract/pallas_call | solution.py:329
  115.6 1.9 %collective-permute-start.29 = (f32[8,3584]{1,0:T(8,128)S(1)}, f32[8,3584]{1,0:T(8,128)S(1)}, u32[]{:S(2)}, u32[]{:S(2)}) collective-permute-start(f32[8,3584]{1,0:T(8,128)S(1)} %get-tuple-element.126), channel_id=1, source_target_pairs={{0,1},{1,2},{2,3},{3,0},{4,5},{5,6},{6,7},{7,4},{8,9},{9,10},{10,1... | collective-permute-start | bytes 344072 | tf_op jit(solution)/shard_map/ppermute | solution.py:512
  118.9 1.7 %collective-permute-start.31 = (f32[8,3584]{1,0:T(8,128)S(1)}, f32[8,3584]{1,0:T(8,128)S(1)}, u32[]{:S(2)}, u32[]{:S(2)}) collective-permute-start(f32[8,3584]{1,0:T(8,128)S(1)} %get-tuple-element.128), channel_id=1, source_target_pairs={{0,3},{1,0},{2,1},{3,2},{4,7},{5,4},{6,5},{7,6},{8,11},{9,8},{10,9... | collective-permute-start | bytes 344072 | tf_op jit(solution)/shard_map/ppermute | solution.py:512
  120.9 4.0 %collective-permute-done.30.three_ref = f32[8,3584]{1,0:T(8,128)S(1)} collective-permute-done((f32[8,3584]{1,0:T(8,128)S(1)}, f32[8,3584]{1,0:T(8,128)S(1)}, u32[]{:S(2)}, u32[]{:S(2)}) %collective-permute-start.30) | collective-permute-done | bytes 114720 | tf_op jit(solution)/shard_map/ppermute | solution.py:512
  127.3 16.3 %all_to_all.10.parts_ref = f32[32,8,256]{2,1,0:T(8,128)S(1)} all-to-all(f32[32,8,256]{2,1,0:T(8,128)S(1)} %owner.1), channel_id=1, replica_groups=mesh['z'=8,'y'=4,'core'=2,'x'=4] {'z','y'}, dimensions={0} | all-to-all | bytes 524288 | tf_op jit(solution)/shard_map/all_to_all | solution.py:574
  143.6 1.5 %last.1 = f32[12,8,16]{2,1,0:T(8,128)} custom-call(s32[4]{0:T(128)S(1)} %copy-done.3, s32[16,256]{1,0:T(8,128)S(1)} %plan.1.table, f32[32,8,256]{2,1,0:T(8,128)S(1)} %all_to_all.10.parts_ref), custom_call_target="tpu_custom_call" | custom-call | tf_op jit(solution)/shard_map/last/pallas_call | solution.py:391
  (79 shorter events, 19.5 us)
Async XLA Ops:
  0.0 2.0 %collective-permute-start = (f32[2,16,2560]{2,1,0:T(8,128)}, f32[2,16,2560]{2,1,0:T(8,128)}, u32[]{:S(2)}, u32[]{:S(2)}) collective-permute-start(f32[2,16,2560]{2,1,0:T(8,128)} %own_ref.1), channel_id=1, source_target_pairs={{0,4},{4,0},{1,5},{5,1},{2,6},{6,2},{3,7},{7,3},{8,12},{12,8},{9,1... | collective-permute-start | bytes 983048 | tf_op jit(solution)/shard_map/ppermute | solution.py:513
  4.2 26.6 %collective-permute-start.1 = (f32[320,2560]{1,0:T(8,128)}, f32[320,2560]{1,0:T(8,128)}, u32[]{:S(2)}, u32[]{:S(2)}) collective-permute-start(f32[320,2560]{1,0:T(8,128)} %bitcast.9), channel_id=1, source_target_pairs={{0,4},{4,0},{1,5},{5,1},{2,6},{6,2},{3,7},{7,3},{8,12},{12,8},{9,1... | collective-permute-start | bytes 9830408 | tf_op jit(solution)/shard_map/ppermute | solution.py:513
  4.4 26.4 %all-to-all-start = ((f32[32,1,2560]{2,1,0:T(1,128)}), f32[32,1,2560]{2,1,0:T(1,128)}, u32[]{:S(2)}, u32[]{:S(2)}) async-start(f32[32,1,2560]{2,1,0:T(1,128)} %bitcast.12), calls=%async_computation | async-start | bytes 655360 | tf_op jit(solution)/shard_map/all_to_all | solution.py:519
  35.9 10.1 %collective-permute-start.5 = (f32[160,256]{1,0:T(8,128)S(1)}, f32[160,256]{1,0:T(8,128)S(1)}, u32[]{:S(2)}, u32[]{:S(2)}) collective-permute-start(f32[160,256]{1,0:T(8,128)S(1)} %shard.1), channel_id=1, source_target_pairs={{0,32},{32,64},{64,96},{96,128},{128,160},{160,192},{192,224},{224... | collective-permute-start | bytes 491528 | tf_op jit(solution)/shard_map/ppermute | solution.py:512
  36.9 9.7 %collective-permute-start.6 = (f32[160,256]{1,0:T(8,128)S(1)}, f32[160,256]{1,0:T(8,128)S(1)}, u32[]{:S(2)}, u32[]{:S(2)}) collective-permute-start(f32[160,256]{1,0:T(8,128)S(1)} %shard.1), channel_id=1, source_target_pairs={{0,224},{32,0},{64,32},{96,64},{128,96},{160,128},{192,160},{224,1... | collective-permute-start | bytes 491528 | tf_op jit(solution)/shard_map/ppermute | solution.py:512
  39.2 11.1 %collective-permute-start.3 = (f32[160,256]{1,0:T(8,128)S(1)}, f32[160,256]{1,0:T(8,128)S(1)}, u32[]{:S(2)}, u32[]{:S(2)}) collective-permute-start(f32[160,256]{1,0:T(8,128)S(1)} %shard.1), channel_id=1, source_target_pairs={{0,64},{32,96},{64,128},{96,160},{128,192},{160,224},{192,0},{224,... | collective-permute-start | bytes 491528 | tf_op jit(solution)/shard_map/ppermute | solution.py:512
  39.2 11.1 %collective-permute-start.4 = (f32[160,256]{1,0:T(8,128)S(1)}, f32[160,256]{1,0:T(8,128)S(1)}, u32[]{:S(2)}, u32[]{:S(2)}) collective-permute-start(f32[160,256]{1,0:T(8,128)S(1)} %shard.1), channel_id=1, source_target_pairs={{0,192},{32,224},{64,0},{96,32},{128,64},{160,96},{192,128},{224,1... | collective-permute-start | bytes 491528 | tf_op jit(solution)/shard_map/ppermute | solution.py:512
  46.5 7.1 %collective-permute-start.11 = (f32[80,1024]{1,0:T(8,128)S(1)}, f32[80,1024]{1,0:T(8,128)S(1)}, u32[]{:S(2)}, u32[]{:S(2)}) collective-permute-start(f32[80,1024]{1,0:T(8,128)S(1)} %get-tuple-element.92.refs_0_), channel_id=1, source_target_pairs={{0,1},{1,2},{2,3},{3,0},{4,5},{5,6},{6,7},{7,4},{8,9},{9,10},{10,1... | collective-permute-start | bytes 983048 | tf_op jit(solution)/shard_map/ppermute | solution.py:512
  48.1 14.7 %collective-permute-start.10 = (f32[480,256]{1,0:T(8,128)S(1)}, f32[480,256]{1,0:T(8,128)S(1)}, u32[]{:S(2)}, u32[]{:S(2)}) collective-permute-start(f32[480,256]{1,0:T(8,128)S(1)} %pad_maximum_fusion.refs_0_), channel_id=1, source_target_pairs={{0,24},{8,0},{16,8},{24,16},{1,25},{9,1},{17,9},{25,17},{2,26},{10... | collective-permute-start | bytes 1474568 | tf_op jit(solution)/shard_map/ppermute | solution.py:512
  49.6 13.4 %collective-permute-start.9 = (f32[480,256]{1,0:T(8,128)S(1)}, f32[480,256]{1,0:T(8,128)S(1)}, u32[]{:S(2)}, u32[]{:S(2)}) collective-permute-start(f32[480,256]{1,0:T(8,128)S(1)} %pad_maximum_fusion.refs_0_), channel_id=1, source_target_pairs={{0,8},{8,16},{16,24},{24,0},{1,9},{9,17},{17,25},{25,1},{2,10},{10... | collective-permute-start | bytes 1474568 | tf_op jit(solution)/shard_map/ppermute | solution.py:512
  50.3 16.2 %collective-permute-start.7 = (f32[320,256]{1,0:T(8,128)S(1)}, f32[320,256]{1,0:T(8,128)S(1)}, u32[]{:S(2)}, u32[]{:S(2)}) collective-permute-start(f32[320,256]{1,0:T(8,128)S(1)} %constant_dynamic-update-slice_fusion.refs_3_), channel_id=1, source_target_pairs={{0,8},{8,16},{16,24},{24,0},{1,9},{9,17},{17,25},{25,1},{2,10},{10... | collective-permute-start | bytes 983048 | tf_op jit(solution)/shard_map/ppermute | solution.py:512
  50.7 15.9 %collective-permute-start.8 = (f32[320,256]{1,0:T(8,128)S(1)}, f32[320,256]{1,0:T(8,128)S(1)}, u32[]{:S(2)}, u32[]{:S(2)}) collective-permute-start(f32[320,256]{1,0:T(8,128)S(1)} %constant_dynamic-update-slice_fusion.refs_3_), channel_id=1, source_target_pairs={{0,24},{8,0},{16,8},{24,16},{1,25},{9,1},{17,9},{25,17},{2,26},{10... | collective-permute-start | bytes 983048 | tf_op jit(solution)/shard_map/ppermute | solution.py:512
  53.7 12.9 %collective-permute-start.12 = (f32[80,1024]{1,0:T(8,128)S(1)}, f32[80,1024]{1,0:T(8,128)S(1)}, u32[]{:S(2)}, u32[]{:S(2)}) collective-permute-start(f32[80,1024]{1,0:T(8,128)S(1)} %get-tuple-element.92.refs_0_), channel_id=1, source_target_pairs={{0,3},{1,0},{2,1},{3,2},{4,7},{5,4},{6,5},{7,6},{8,11},{9,8},{10,9... | collective-permute-start | bytes 983048 | tf_op jit(solution)/shard_map/ppermute | solution.py:512
  62.7 8.8 %collective-permute-start.18 = (f32[80,1024]{1,0:T(8,128)S(1)}, f32[80,1024]{1,0:T(8,128)S(1)}, u32[]{:S(2)}, u32[]{:S(2)}) collective-permute-start(f32[80,1024]{1,0:T(8,128)S(1)} %get-tuple-element.92.refs_0_), channel_id=1, source_target_pairs={{0,4},{4,0},{1,5},{5,1},{2,6},{6,2},{3,7},{7,3},{8,12},{12,8},{9,1... | collective-permute-start | bytes 983048 | tf_op jit(solution)/shard_map/ppermute | solution.py:513
  66.6 8.7 %collective-permute-start.17 = (f32[80,1024]{1,0:T(8,128)S(1)}, f32[80,1024]{1,0:T(8,128)S(1)}, u32[]{:S(2)}, u32[]{:S(2)}) collective-permute-start(f32[80,1024]{1,0:T(8,128)S(1)} %get-tuple-element.92.refs_0_), channel_id=1, source_target_pairs={{0,2},{1,3},{2,0},{3,1},{4,6},{5,7},{6,4},{7,5},{8,10},{9,11},{10,... | collective-permute-start | bytes 983048 | tf_op jit(solution)/shard_map/ppermute | solution.py:512
  67.9 14.6 %collective-permute-start.16 = (f32[480,256]{1,0:T(8,128)S(1)}, f32[480,256]{1,0:T(8,128)S(1)}, u32[]{:S(2)}, u32[]{:S(2)}) collective-permute-start(f32[480,256]{1,0:T(8,128)S(1)} %pad_maximum_fusion.2), channel_id=1, source_target_pairs={{0,224},{32,0},{64,32},{96,64},{128,96},{160,128},{192,160},{224,1... | collective-permute-start | bytes 1474568 | tf_op jit(solution)/shard_map/ppermute | solution.py:512
  70.6 12.2 %collective-permute-start.15 = (f32[480,256]{1,0:T(8,128)S(1)}, f32[480,256]{1,0:T(8,128)S(1)}, u32[]{:S(2)}, u32[]{:S(2)}) collective-permute-start(f32[480,256]{1,0:T(8,128)S(1)} %pad_maximum_fusion.1), channel_id=1, source_target_pairs={{0,32},{32,64},{64,96},{96,128},{128,160},{160,192},{192,224},{224... | collective-permute-start | bytes 1474568 | tf_op jit(solution)/shard_map/ppermute | solution.py:512
  70.7 9.2 %collective-permute-start.14 = (f32[400,256]{1,0:T(8,128)S(1)}, f32[400,256]{1,0:T(8,128)S(1)}, u32[]{:S(2)}, u32[]{:S(2)}) collective-permute-start(f32[400,256]{1,0:T(8,128)S(1)} %pad_maximum_fusion.4), channel_id=1, source_target_pairs={{0,24},{8,0},{16,8},{24,16},{1,25},{9,1},{17,9},{25,17},{2,26},{10... | collective-permute-start | bytes 1228808 | tf_op jit(solution)/shard_map/ppermute | solution.py:512
  71.5 11.0 %collective-permute-start.13 = (f32[400,256]{1,0:T(8,128)S(1)}, f32[400,256]{1,0:T(8,128)S(1)}, u32[]{:S(2)}, u32[]{:S(2)}) collective-permute-start(f32[400,256]{1,0:T(8,128)S(1)} %pad_maximum_fusion.3), channel_id=1, source_target_pairs={{0,8},{8,16},{16,24},{24,0},{1,9},{9,17},{17,25},{25,1},{2,10},{10... | collective-permute-start | bytes 1228808 | tf_op jit(solution)/shard_map/ppermute | solution.py:512
  75.2 1.6 %collective-permute-start.19 = (f32[80,1024]{1,0:T(8,128)S(1)}, f32[80,1024]{1,0:T(8,128)S(1)}, u32[]{:S(2)}, u32[]{:S(2)}) collective-permute-start(f32[80,1024]{1,0:T(8,128)S(1)} %collective-permute-done.11.refs_1_), channel_id=1, source_target_pairs={{0,4},{4,0},{1,5},{5,1},{2,6},{6,2},{3,7},{7,3},{8,12},{12,8},{9,1... | collective-permute-start | bytes 983048 | tf_op jit(solution)/shard_map/ppermute | solution.py:513
  76.9 9.0 %collective-permute-start.25 = (f32[80,1024]{1,0:T(8,128)S(1)}, f32[80,1024]{1,0:T(8,128)S(1)}, u32[]{:S(2)}, u32[]{:S(2)}) collective-permute-start(f32[80,1024]{1,0:T(8,128)S(1)} %collective-permute-done.12.refs_3_), channel_id=1, source_target_pairs={{0,4},{4,0},{1,5},{5,1},{2,6},{6,2},{3,7},{7,3},{8,12},{12,8},{9,1... | collective-permute-start | bytes 983048 | tf_op jit(solution)/shard_map/ppermute | solution.py:513
  82.8 11.2 %collective-permute-start.23 = (f32[240,256]{1,0:T(8,128)S(1)}, f32[240,256]{1,0:T(8,128)S(1)}, u32[]{:S(2)}, u32[]{:S(2)}) collective-permute-start(f32[240,256]{1,0:T(8,128)S(1)} %pad_maximum_fusion.6), channel_id=1, source_target_pairs={{0,224},{32,0},{64,32},{96,64},{128,96},{160,128},{192,160},{224,1... | collective-permute-start | bytes 737288 | tf_op jit(solution)/shard_map/ppermute | solution.py:512
  85.6 9.7 %collective-permute-start.24 = (f32[80,1024]{1,0:T(8,128)S(1)}, f32[80,1024]{1,0:T(8,128)S(1)}, u32[]{:S(2)}, u32[]{:S(2)}) collective-permute-start(f32[80,1024]{1,0:T(8,128)S(1)} %collective-permute-done.17.refs_2_), channel_id=1, source_target_pairs={{0,4},{4,0},{1,5},{5,1},{2,6},{6,2},{3,7},{7,3},{8,12},{12,8},{9,1... | collective-permute-start | bytes 983048 | tf_op jit(solution)/shard_map/ppermute | solution.py:513
  85.6 9.7 %collective-permute-start.22 = (f32[240,256]{1,0:T(8,128)S(1)}, f32[240,256]{1,0:T(8,128)S(1)}, u32[]{:S(2)}, u32[]{:S(2)}) collective-permute-start(f32[240,256]{1,0:T(8,128)S(1)} %pad_maximum_fusion.5), channel_id=1, source_target_pairs={{0,32},{32,64},{64,96},{96,128},{128,160},{160,192},{192,224},{224... | collective-permute-start | bytes 737288 | tf_op jit(solution)/shard_map/ppermute | solution.py:512
  85.7 8.3 %collective-permute-start.20 = (f32[160,256]{1,0:T(8,128)S(1)}, f32[160,256]{1,0:T(8,128)S(1)}, u32[]{:S(2)}, u32[]{:S(2)}) collective-permute-start(f32[160,256]{1,0:T(8,128)S(1)} %slice.46), channel_id=1, source_target_pairs={{0,8},{8,16},{16,24},{24,0},{1,9},{9,17},{17,25},{25,1},{2,10},{10... | collective-permute-start | bytes 491528 | tf_op jit(solution)/shard_map/ppermute | solution.py:512
  85.8 8.2 %collective-permute-start.21 = (f32[160,256]{1,0:T(8,128)S(1)}, f32[160,256]{1,0:T(8,128)S(1)}, u32[]{:S(2)}, u32[]{:S(2)}) collective-permute-start(f32[160,256]{1,0:T(8,128)S(1)} %slice.47), channel_id=1, source_target_pairs={{0,24},{8,0},{16,8},{24,16},{1,25},{9,1},{17,9},{25,17},{2,26},{10... | collective-permute-start | bytes 491528 | tf_op jit(solution)/shard_map/ppermute | solution.py:512
  95.3 8.0 %collective-permute-start.26 = (f32[80,256]{1,0:T(8,128)S(1)}, f32[80,256]{1,0:T(8,128)S(1)}, u32[]{:S(2)}, u32[]{:S(2)}) collective-permute-start(f32[80,256]{1,0:T(8,128)S(1)} %slice.50), channel_id=1, source_target_pairs={{0,8},{8,16},{16,24},{24,0},{1,9},{9,17},{17,25},{25,1},{2,10},{10... | collective-permute-start | bytes 245768 | tf_op jit(solution)/shard_map/ppermute | solution.py:512
  95.4 7.9 %collective-permute-start.27 = (f32[80,256]{1,0:T(8,128)S(1)}, f32[80,256]{1,0:T(8,128)S(1)}, u32[]{:S(2)}, u32[]{:S(2)}) collective-permute-start(f32[80,256]{1,0:T(8,128)S(1)} %slice.51), channel_id=1, source_target_pairs={{0,24},{8,0},{16,8},{24,16},{1,25},{9,1},{17,9},{25,17},{2,26},{10... | collective-permute-start | bytes 245768 | tf_op jit(solution)/shard_map/ppermute | solution.py:512
  112.2 3.3 %collective-permute-start.28 = (f32[4,8,3584]{2,1,0:T(8,128)S(1)}, f32[4,8,3584]{2,1,0:T(8,128)S(1)}, u32[]{:S(2)}, u32[]{:S(2)}) collective-permute-start(f32[4,8,3584]{2,1,0:T(8,128)S(1)} %get-tuple-element.124), channel_id=1, source_target_pairs={{0,4},{4,0},{1,5},{5,1},{2,6},{6,2},{3,7},{7,3},{8,12},{12,8},{9,1... | collective-permute-start | bytes 1376264 | tf_op jit(solution)/shard_map/ppermute | solution.py:513
  115.6 5.4 %collective-permute-start.29 = (f32[8,3584]{1,0:T(8,128)S(1)}, f32[8,3584]{1,0:T(8,128)S(1)}, u32[]{:S(2)}, u32[]{:S(2)}) collective-permute-start(f32[8,3584]{1,0:T(8,128)S(1)} %get-tuple-element.126), channel_id=1, source_target_pairs={{0,1},{1,2},{2,3},{3,0},{4,5},{5,6},{6,7},{7,4},{8,9},{9,10},{10,1... | collective-permute-start | bytes 344072 | tf_op jit(solution)/shard_map/ppermute | solution.py:512
  117.5 7.5 %collective-permute-start.30 = (f32[8,3584]{1,0:T(8,128)S(1)}, f32[8,3584]{1,0:T(8,128)S(1)}, u32[]{:S(2)}, u32[]{:S(2)}) collective-permute-start(f32[8,3584]{1,0:T(8,128)S(1)} %get-tuple-element.127), channel_id=1, source_target_pairs={{0,2},{1,3},{2,0},{3,1},{4,6},{5,7},{6,4},{7,5},{8,10},{9,11},{10,... | collective-permute-start | bytes 344072 | tf_op jit(solution)/shard_map/ppermute | solution.py:512
  118.9 7.2 %collective-permute-start.31 = (f32[8,3584]{1,0:T(8,128)S(1)}, f32[8,3584]{1,0:T(8,128)S(1)}, u32[]{:S(2)}, u32[]{:S(2)}) collective-permute-start(f32[8,3584]{1,0:T(8,128)S(1)} %get-tuple-element.128), channel_id=1, source_target_pairs={{0,3},{1,0},{2,1},{3,2},{4,7},{5,4},{6,5},{7,6},{8,11},{9,8},{10,9... | collective-permute-start | bytes 344072 | tf_op jit(solution)/shard_map/ppermute | solution.py:512
  (6 other events, 82.0 us)

commit v4 on v3

--- a/solution.py
+++ b/solution.py
@@ -538,13 +538,13 @@
     first_down, first_up, around[1], below2, above2, *screens = hold(
         (first_down, first_up, around[1], below2, above2, *screens)
     )
+    around[2] = shift(after(columns, first_down), "x", 2)
     second_down, second_up, first_down, around[3] = hold((second_down, second_up, first_down, around[3]))
 
     z_below = shift(join(second_down[:block], second_up[:block], second[:block]), "z", 1)
     z_above = shift(join(second_down[block:], second_up[block:], second[block:]), "z", -1)
     two_down = shift(join(first_down[: 3 * SPAN], second_down[:block]), "y", 1)
     two_up = shift(join(first_up[3 * SPAN :], second_up[block:]), "y", -1)
-    around[2] = shift(after(columns, second_down), "x", 2)
     swapped = [swap(columns), swap(around[1]), None, None]
     two_down, two_up, z_below, z_above, around[2], swapped[0], swapped[1] = hold(
         (two_down, two_up, z_below, z_above, around[2], swapped[0], swapped[1])

time: 145 us -> 146 us (level)
  no operation moved by 1% of the time
where the time goes in v4:
time: 146 us
  starting transfers between devices  49.2 us (34%)
  Pallas kernels  38.5 us (26%)
  waiting for transfers between devices  37.4 us (26%)
  blocking collectives  16.4 us (11%)
  local copies, waits for them, and re-layouts  2.98 us (2%)
    ppermute x24, starting transfers between devices, shards(): lax.ppermute(array, axis, ring(lax.axis_size(axis), by))  36.8 us
    ppermute x24, waiting for transfers between devices, shards(): lax.ppermute(array, axis, ring(lax.axis_size(axis), by))  21.8 us
    all_to_all x1, blocking collectives, shards(): parts = lax.all_to_all(parts, ('z', 'y'), 0, 0, tiled=True)  16.4 us
    all_to_all x1, starting transfers between devices, shards(): lax.all_to_all(pieces.reshape(32, 1, -1), ('z', 'y'), 0, 0, tiled=True)  11.6 us
    all_to_all x1, waiting for transfers between devices, shards(): lax.all_to_all(pieces.reshape(32, 1, -1), ('z', 'y'), 0, 0, tiled=True)  11.4 us
    pallas_call x1, Pallas kernels, pair_call(): pl.pallas_call(pair_kernel, out_shape=(jax.ShapeDtypeStruct((4, 8, ROOM *...  9.15 us
    pallas_call x2, Pallas kernels, group_call(): pl.pallas_call(functools.partial(group_kernel, runs, planes), out_shape=j...  7.55 us
    pallas_call x1, Pallas kernels, screen_call(): pl.pallas_call(screen_kernel, out_shape=shapes, in_specs=[SMEM, VMEM, VME...  7.35 us
  transfers between devices with their start and end apart: 33, of which 16 were waited for; matrix products, arithmetic and copies ran while one was open for 1% of the time, Pallas kernels for 15%

profile of v4, /device:TPU:2, one launch (start us, length us, event | category | flops | bytes accessed | tf_op | source)
XLA Modules:
  0.0 145.7 jit_solution(657256988785853504)
XLA Ops:
  2.0 2.2 %pack.1 = f32[640,128]{1,0:T(8,128)} custom-call(s32[4]{0:T(128)} %pad_add_fusion.place, f32[2,16,2560]{2,1,0:T(8,128)} %own_ref.1, f32[2,16,2560]{2,1,0:T(8,128)} %collective-permute-done.other_ref), custom_call_target="tpu_custom_call" | custom-call | tf_op jit(solution)/shard_map/pack/pallas_call | solution.py:424
  4.4 11.6 %all-to-all-start = ((f32[32,1,2560]{2,1,0:T(1,128)}), f32[32,1,2560]{2,1,0:T(1,128)}, u32[]{:S(2)}, u32[]{:S(2)}) async-start(f32[32,1,2560]{2,1,0:T(1,128)} %bitcast.12), calls=%async_computation | async-start | bytes 655360 | tf_op jit(solution)/shard_map/all_to_all | solution.py:519
  19.4 11.4 %all-to-all-done = f32[32,1,2560]{2,1,0:T(1,128)} async-done(((f32[32,1,2560]{2,1,0:T(1,128)}), f32[32,1,2560]{2,1,0:T(1,128)}, u32[]{:S(2)}, u32[]{:S(2)}) %all-to-all-start) | async-done | bytes 327712 | tf_op jit(solution)/shard_map/all_to_all | solution.py:519
  31.5 2.5 %unpack.1 = (f32[80,1024]{1,0:T(8,128)S(1)}, f32[80,256]{1,0:T(8,128)S(1)}, f32[80,256]{1,0:T(8,128)S(1)}) custom-call(s32[4]{0:T(128)S(1)} %copy-done.2, s32[16,256]{1,0:T(8,128)S(1)} %plan.1.table, f32[640,128]{1,0:T(8,128)} %bitcast.6.in_ref), custom_call_target="tpu_custom_call" | custom-call | tf_op jit(solution)/shard_map/unpack/pallas_call | solution.py:473
  36.9 2.3 %collective-permute-start.6 = (f32[160,256]{1,0:T(8,128)S(1)}, f32[160,256]{1,0:T(8,128)S(1)}, u32[]{:S(2)}, u32[]{:S(2)}) collective-permute-start(f32[160,256]{1,0:T(8,128)S(1)} %shard.1), channel_id=1, source_target_pairs={{0,224},{32,0},{64,32},{96,64},{128,96},{160,128},{192,160},{224,1... | collective-permute-start | bytes 491528 | tf_op jit(solution)/shard_map/ppermute | solution.py:512
  39.2 4.1 %collective-permute-start.4 = (f32[160,256]{1,0:T(8,128)S(1)}, f32[160,256]{1,0:T(8,128)S(1)}, u32[]{:S(2)}, u32[]{:S(2)}) collective-permute-start(f32[160,256]{1,0:T(8,128)S(1)} %shard.1), channel_id=1, source_target_pairs={{0,192},{32,224},{64,0},{96,32},{128,64},{160,96},{192,128},{224,1... | collective-permute-start | bytes 491528 | tf_op jit(solution)/shard_map/ppermute | solution.py:512
  43.4 2.6 %collective-permute-done.5 = f32[160,256]{1,0:T(8,128)S(1)} collective-permute-done((f32[160,256]{1,0:T(8,128)S(1)}, f32[160,256]{1,0:T(8,128)S(1)}, u32[]{:S(2)}, u32[]{:S(2)}) %collective-permute-start.5) | collective-permute-done | bytes 163872 | tf_op jit(solution)/shard_map/ppermute | solution.py:512
  48.1 1.6 %collective-permute-start.10 = (f32[480,256]{1,0:T(8,128)S(1)}, f32[480,256]{1,0:T(8,128)S(1)}, u32[]{:S(2)}, u32[]{:S(2)}) collective-permute-start(f32[480,256]{1,0:T(8,128)S(1)} %pad_maximum_fusion.refs_0_), channel_id=1, source_target_pairs={{0,24},{8,0},{16,8},{24,16},{1,25},{9,1},{17,9},{25,17},{2,26},{10... | collective-permute-start | bytes 1474568 | tf_op jit(solution)/shard_map/ppermute | solution.py:512
  50.7 3.0 %collective-permute-start.8 = (f32[320,256]{1,0:T(8,128)S(1)}, f32[320,256]{1,0:T(8,128)S(1)}, u32[]{:S(2)}, u32[]{:S(2)}) collective-permute-start(f32[320,256]{1,0:T(8,128)S(1)} %constant_dynamic-update-slice_fusion.refs_3_), channel_id=1, source_target_pairs={{0,24},{8,0},{16,8},{24,16},{1,25},{9,1},{17,9},{25,17},{2,26},{10... | collective-permute-start | bytes 983048 | tf_op jit(solution)/shard_map/ppermute | solution.py:512
  53.7 1.7 %collective-permute-start.12 = (f32[80,1024]{1,0:T(8,128)S(1)}, f32[80,1024]{1,0:T(8,128)S(1)}, u32[]{:S(2)}, u32[]{:S(2)}) collective-permute-start(f32[80,1024]{1,0:T(8,128)S(1)} %get-tuple-element.92.refs_0_), channel_id=1, source_target_pairs={{0,3},{1,0},{2,1},{3,2},{4,7},{5,4},{6,5},{7,6},{8,11},{9,8},{10,9... | collective-permute-start | bytes 983048 | tf_op jit(solution)/shard_map/ppermute | solution.py:512
  55.4 7.3 %screen.1 = (bf16[640,1664]{1,0:T(8,128)(2,1)S(1)}, bf16[640,1664]{1,0:T(8,128)(2,1)S(1)}, bf16[640,640]{1,0:T(8,128)(2,1)S(1)}, bf16[640,640]{1,0:T(8,128)(2,1)...) custom-call(s32[4]{0:T(128)S(1)} %copy-done.3, f32[320,2560]{1,0:T(8,128)S(1)} %bitcast.10, ...), custom_call_target="tpu_custom_call" | custom-call | tf_op jit(solution)/shard_map/screen/pallas_call | solution.py:153
  64.4 2.2 %collective-permute-done.7.refs_4_ = f32[320,256]{1,0:T(8,128)S(1)} collective-permute-done((f32[320,256]{1,0:T(8,128)S(1)}, f32[320,256]{1,0:T(8,128)S(1)}, u32[]{:S(2)}, u32[]{:S(2)}) %collective-permute-start.7) | collective-permute-done | bytes 327712 | tf_op jit(solution)/shard_map/ppermute | solution.py:512
  66.6 2.7 %collective-permute-start.16 = (f32[480,256]{1,0:T(8,128)S(1)}, f32[480,256]{1,0:T(8,128)S(1)}, u32[]{:S(2)}, u32[]{:S(2)}) collective-permute-start(f32[480,256]{1,0:T(8,128)S(1)} %pad_maximum_fusion.2), channel_id=1, source_target_pairs={{0,224},{32,0},{64,32},{96,64},{128,96},{160,128},{192,160},{224,1... | collective-permute-start | bytes 1474568 | tf_op jit(solution)/shard_map/ppermute | solution.py:512
  70.2 1.6 %collective-permute-start.13 = (f32[400,256]{1,0:T(8,128)S(1)}, f32[400,256]{1,0:T(8,128)S(1)}, u32[]{:S(2)}, u32[]{:S(2)}) collective-permute-start(f32[400,256]{1,0:T(8,128)S(1)} %pad_maximum_fusion.3), channel_id=1, source_target_pairs={{0,8},{8,16},{16,24},{24,0},{1,9},{9,17},{17,25},{25,1},{2,10},{10... | collective-permute-start | bytes 1228808 | tf_op jit(solution)/shard_map/ppermute | solution.py:512
  71.8 2.9 %collective-permute-done.17.refs_2_ = f32[80,1024]{1,0:T(8,128)S(1)} collective-permute-done((f32[80,1024]{1,0:T(8,128)S(1)}, f32[80,1024]{1,0:T(8,128)S(1)}, u32[]{:S(2)}, u32[]{:S(2)}) %collective-permute-start.17) | collective-permute-done | bytes 327712 | tf_op jit(solution)/shard_map/ppermute | solution.py:512
  74.7 1.6 %collective-permute-done.19.refs_5_ = f32[80,1024]{1,0:T(8,128)S(1)} collective-permute-done((f32[80,1024]{1,0:T(8,128)S(1)}, f32[80,1024]{1,0:T(8,128)S(1)}, u32[]{:S(2)}, u32[]{:S(2)}) %collective-permute-start.19) | collective-permute-done | bytes 327712 | tf_op jit(solution)/shard_map/ppermute | solution.py:513
  76.4 3.4 %collective-permute-done.14.refs_7_ = f32[400,256]{1,0:T(8,128)S(1)} collective-permute-done((f32[400,256]{1,0:T(8,128)S(1)}, f32[400,256]{1,0:T(8,128)S(1)}, u32[]{:S(2)}, u32[]{:S(2)}) %collective-permute-start.14) | collective-permute-done | bytes 409632 | tf_op jit(solution)/shard_map/ppermute | solution.py:512
  79.9 2.5 %collective-permute-done.13.refs_6_ = f32[400,256]{1,0:T(8,128)S(1)} collective-permute-done((f32[400,256]{1,0:T(8,128)S(1)}, f32[400,256]{1,0:T(8,128)S(1)}, u32[]{:S(2)}, u32[]{:S(2)}) %collective-permute-start.13) | collective-permute-done | bytes 409632 | tf_op jit(solution)/shard_map/ppermute | solution.py:512
  82.8 2.8 %collective-permute-start.23 = (f32[240,256]{1,0:T(8,128)S(1)}, f32[240,256]{1,0:T(8,128)S(1)}, u32[]{:S(2)}, u32[]{:S(2)}) collective-permute-start(f32[240,256]{1,0:T(8,128)S(1)} %pad_maximum_fusion.6), channel_id=1, source_target_pairs={{0,224},{32,0},{64,32},{96,64},{128,96},{160,128},{192,160},{224,1... | collective-permute-start | bytes 737288 | tf_op jit(solution)/shard_map/ppermute | solution.py:512
  85.8 3.2 %collective-permute-start.21 = (f32[160,256]{1,0:T(8,128)S(1)}, f32[160,256]{1,0:T(8,128)S(1)}, u32[]{:S(2)}, u32[]{:S(2)}) collective-permute-start(f32[160,256]{1,0:T(8,128)S(1)} %slice.47), channel_id=1, source_target_pairs={{0,24},{8,0},{16,8},{24,16},{1,25},{9,1},{17,9},{25,17},{2,26},{10... | collective-permute-start | bytes 491528 | tf_op jit(solution)/shard_map/ppermute | solution.py:512
  89.0 5.0 %group.2.refs_6_ = f32[640,512]{1,0:T(8,128)S(1)} custom-call(s32[4]{0:T(128)S(1)} %copy-done.3, f32[480,256]{1,0:T(8,128)S(1)} %pad_maximum_fusion.refs_0_, f32[480,256]{1,0:T(8,128)S(1)} %collective-permute-done.9.refs_1_, f32[480,256]{1,0:T(8,128)S(1)} %collective-permute-done.10.refs_2_, f32[320,256]{1,0:T(8,128)S(1)} %constant_dynamic-update-slice_fusion.refs_3_, ...), custom_call_target="tpu_custom_call" | custom-call | tf_op jit(solution)/shard_map/group/pallas_call | solution.py:252
  95.3 3.2 %collective-permute-start.27 = (f32[80,256]{1,0:T(8,128)S(1)}, f32[80,256]{1,0:T(8,128)S(1)}, u32[]{:S(2)}, u32[]{:S(2)}) collective-permute-start(f32[80,256]{1,0:T(8,128)S(1)} %slice.51), channel_id=1, source_target_pairs={{0,24},{8,0},{16,8},{24,16},{1,25},{9,1},{17,9},{25,17},{2,26},{10... | collective-permute-start | bytes 245768 | tf_op jit(solution)/shard_map/ppermute | solution.py:512
  98.6 2.1 %left.1 = (bf16[1024,640]{1,0:T(8,128)(2,1)S(1)}, bf16[1024,640]{1,0:T(8,128)(2,1)S(1)}) custom-call(s32[4]{0:T(128)S(1)} %copy-done.3, f32[80,1024]{1,0:T(8,128)S(1)} %get-tuple-element.92.refs_0_, f32[80,1024]{1,0:T(8,128)S(1)} %collective-permute-done.11.refs_1_, f32[80,1024]{1,0:T(8,128)S(1)} %collective-permute-done.17.refs_2_, ...), custom_call_target="tpu_custom_call" | custom-call | tf_op jit(solution)/shard_map/left/pallas_call | solution.py:185
  100.7 2.5 %group.3.refs_6_ = f32[640,512]{1,0:T(8,128)S(1)} custom-call(s32[4]{0:T(128)S(1)} %copy-done.3, f32[480,256]{1,0:T(8,128)S(1)} %collective-permute-done.15.refs_0_, f32[480,256]{1,0:T(8,128)S(1)} %collective-permute-done.16.refs_1_, f32[160,256]{1,0:T(8,128)S(1)} %collective-permute-done.20.refs_2_, f32[160,256]{1,0:T(8,128)S(1)} %collective-permute-done.21.refs_3_, ...), custom_call_target="tpu_custom_call" | custom-call | tf_op jit(solution)/shard_map/group/pallas_call | solution.py:252
  103.2 9.1 %pair.1 = (f32[4,8,3584]{2,1,0:T(8,128)S(1)}, f32[1024,512]{1,0:T(8,128)S(1)}) custom-call(s32[4]{0:T(128)S(1)} %copy-done.3, s32[16,256]{1,0:T(8,128)S(1)} %plan.1.table, f32[240,256]{1,0:T(8,128)S(1)} %collective-permute-done.22.refs_0_, f32[240,256]{1,0:T(8,128)S(1)} %collective-permute-done.23.refs_1_, f32[80,256]{1,0:T(8,128)S(1)} %collective-permute-done.26.refs_2_, ...), custom_call_target="tpu_custom_call" | custom-call | tf_op jit(solution)/shard_map/pair/pallas_call | solution.py:310
  112.5 3.0 %extract.1.one_ref = f32[4,8,3584]{2,1,0:T(8,128)S(1)} custom-call(s32[4]{0:T(128)S(1)} %copy-done.3, s32[16,256]{1,0:T(8,128)S(1)} %plan.1.table, f32[1024,512]{1,0:T(8,128)S(1)} %get-tuple-element.123.kern), custom_call_target="tpu_custom_call" | custom-call | tf_op jit(solution)/shard_map/extract/pallas_call | solution.py:329
  115.5 1.9 %collective-permute-start.29 = (f32[8,3584]{1,0:T(8,128)S(1)}, f32[8,3584]{1,0:T(8,128)S(1)}, u32[]{:S(2)}, u32[]{:S(2)}) collective-permute-start(f32[8,3584]{1,0:T(8,128)S(1)} %get-tuple-element.126), channel_id=1, source_target_pairs={{0,1},{1,2},{2,3},{3,0},{4,5},{5,6},{6,7},{7,4},{8,9},{9,10},{10,1... | collective-permute-start | bytes 344072 | tf_op jit(solution)/shard_map/ppermute | solution.py:512
  118.8 1.7 %collective-permute-start.31 = (f32[8,3584]{1,0:T(8,128)S(1)}, f32[8,3584]{1,0:T(8,128)S(1)}, u32[]{:S(2)}, u32[]{:S(2)}) collective-permute-start(f32[8,3584]{1,0:T(8,128)S(1)} %get-tuple-element.128), channel_id=1, source_target_pairs={{0,3},{1,0},{2,1},{3,2},{4,7},{5,4},{6,5},{7,6},{8,11},{9,8},{10,9... | collective-permute-start | bytes 344072 | tf_op jit(solution)/shard_map/ppermute | solution.py:512
  121.4 3.5 %collective-permute-done.30.three_ref = f32[8,3584]{1,0:T(8,128)S(1)} collective-permute-done((f32[8,3584]{1,0:T(8,128)S(1)}, f32[8,3584]{1,0:T(8,128)S(1)}, u32[]{:S(2)}, u32[]{:S(2)}) %collective-permute-start.30) | collective-permute-done | bytes 114720 | tf_op jit(solution)/shard_map/ppermute | solution.py:512
  124.9 1.6 %collective-permute-done.31.four_ref = f32[8,3584]{1,0:T(8,128)S(1)} collective-permute-done((f32[8,3584]{1,0:T(8,128)S(1)}, f32[8,3584]{1,0:T(8,128)S(1)}, u32[]{:S(2)}, u32[]{:S(2)}) %collective-permute-start.31) | collective-permute-done | bytes 114720 | tf_op jit(solution)/shard_map/ppermute | solution.py:512
  127.8 16.4 %all_to_all.10.parts_ref = f32[32,8,256]{2,1,0:T(8,128)S(1)} all-to-all(f32[32,8,256]{2,1,0:T(8,128)S(1)} %owner.1), channel_id=1, replica_groups=mesh['z'=8,'y'=4,'core'=2,'x'=4] {'z','y'}, dimensions={0} | all-to-all | bytes 524288 | tf_op jit(solution)/shard_map/all_to_all | solution.py:574
  144.1 1.5 %last.1 = f32[12,8,16]{2,1,0:T(8,128)} custom-call(s32[4]{0:T(128)S(1)} %copy-done.3, s32[16,256]{1,0:T(8,128)S(1)} %plan.1.table, f32[32,8,256]{2,1,0:T(8,128)S(1)} %all_to_all.10.parts_ref), custom_call_target="tpu_custom_call" | custom-call | tf_op jit(solution)/shard_map/last/pallas_call | solution.py:391
  (79 shorter events, 20.3 us)
Async XLA Ops:
  0.0 2.0 %collective-permute-start = (f32[2,16,2560]{2,1,0:T(8,128)}, f32[2,16,2560]{2,1,0:T(8,128)}, u32[]{:S(2)}, u32[]{:S(2)}) collective-permute-start(f32[2,16,2560]{2,1,0:T(8,128)} %own_ref.1), channel_id=1, source_target_pairs={{0,4},{4,0},{1,5},{5,1},{2,6},{6,2},{3,7},{7,3},{8,12},{12,8},{9,1... | collective-permute-start | bytes 983048 | tf_op jit(solution)/shard_map/ppermute | solution.py:513
  4.2 26.6 %collective-permute-start.1 = (f32[320,2560]{1,0:T(8,128)}, f32[320,2560]{1,0:T(8,128)}, u32[]{:S(2)}, u32[]{:S(2)}) collective-permute-start(f32[320,2560]{1,0:T(8,128)} %bitcast.9), channel_id=1, source_target_pairs={{0,4},{4,0},{1,5},{5,1},{2,6},{6,2},{3,7},{7,3},{8,12},{12,8},{9,1... | collective-permute-start | bytes 9830408 | tf_op jit(solution)/shard_map/ppermute | solution.py:513
  4.4 26.4 %all-to-all-start = ((f32[32,1,2560]{2,1,0:T(1,128)}), f32[32,1,2560]{2,1,0:T(1,128)}, u32[]{:S(2)}, u32[]{:S(2)}) async-start(f32[32,1,2560]{2,1,0:T(1,128)} %bitcast.12), calls=%async_computation | async-start | bytes 655360 | tf_op jit(solution)/shard_map/all_to_all | solution.py:519
  35.9 10.1 %collective-permute-start.5 = (f32[160,256]{1,0:T(8,128)S(1)}, f32[160,256]{1,0:T(8,128)S(1)}, u32[]{:S(2)}, u32[]{:S(2)}) collective-permute-start(f32[160,256]{1,0:T(8,128)S(1)} %shard.1), channel_id=1, source_target_pairs={{0,32},{32,64},{64,96},{96,128},{128,160},{160,192},{192,224},{224... | collective-permute-start | bytes 491528 | tf_op jit(solution)/shard_map/ppermute | solution.py:512
  36.9 9.7 %collective-permute-start.6 = (f32[160,256]{1,0:T(8,128)S(1)}, f32[160,256]{1,0:T(8,128)S(1)}, u32[]{:S(2)}, u32[]{:S(2)}) collective-permute-start(f32[160,256]{1,0:T(8,128)S(1)} %shard.1), channel_id=1, source_target_pairs={{0,224},{32,0},{64,32},{96,64},{128,96},{160,128},{192,160},{224,1... | collective-permute-start | bytes 491528 | tf_op jit(solution)/shard_map/ppermute | solution.py:512
  39.2 11.1 %collective-permute-start.3 = (f32[160,256]{1,0:T(8,128)S(1)}, f32[160,256]{1,0:T(8,128)S(1)}, u32[]{:S(2)}, u32[]{:S(2)}) collective-permute-start(f32[160,256]{1,0:T(8,128)S(1)} %shard.1), channel_id=1, source_target_pairs={{0,64},{32,96},{64,128},{96,160},{128,192},{160,224},{192,0},{224,... | collective-permute-start | bytes 491528 | tf_op jit(solution)/shard_map/ppermute | solution.py:512
  39.2 11.1 %collective-permute-start.4 = (f32[160,256]{1,0:T(8,128)S(1)}, f32[160,256]{1,0:T(8,128)S(1)}, u32[]{:S(2)}, u32[]{:S(2)}) collective-permute-start(f32[160,256]{1,0:T(8,128)S(1)} %shard.1), channel_id=1, source_target_pairs={{0,192},{32,224},{64,0},{96,32},{128,64},{160,96},{192,128},{224,1... | collective-permute-start | bytes 491528 | tf_op jit(solution)/shard_map/ppermute | solution.py:512
  46.5 7.1 %collective-permute-start.11 = (f32[80,1024]{1,0:T(8,128)S(1)}, f32[80,1024]{1,0:T(8,128)S(1)}, u32[]{:S(2)}, u32[]{:S(2)}) collective-permute-start(f32[80,1024]{1,0:T(8,128)S(1)} %get-tuple-element.92.refs_0_), channel_id=1, source_target_pairs={{0,1},{1,2},{2,3},{3,0},{4,5},{5,6},{6,7},{7,4},{8,9},{9,10},{10,1... | collective-permute-start | bytes 983048 | tf_op jit(solution)/shard_map/ppermute | solution.py:512
  48.1 14.7 %collective-permute-start.10 = (f32[480,256]{1,0:T(8,128)S(1)}, f32[480,256]{1,0:T(8,128)S(1)}, u32[]{:S(2)}, u32[]{:S(2)}) collective-permute-start(f32[480,256]{1,0:T(8,128)S(1)} %pad_maximum_fusion.refs_0_), channel_id=1, source_target_pairs={{0,24},{8,0},{16,8},{24,16},{1,25},{9,1},{17,9},{25,17},{2,26},{10... | collective-permute-start | bytes 1474568 | tf_op jit(solution)/shard_map/ppermute | solution.py:512
  49.6 13.4 %collective-permute-start.9 = (f32[480,256]{1,0:T(8,128)S(1)}, f32[480,256]{1,0:T(8,128)S(1)}, u32[]{:S(2)}, u32[]{:S(2)}) collective-permute-start(f32[480,256]{1,0:T(8,128)S(1)} %pad_maximum_fusion.refs_0_), channel_id=1, source_target_pairs={{0,8},{8,16},{16,24},{24,0},{1,9},{9,17},{17,25},{25,1},{2,10},{10... | collective-permute-start | bytes 1474568 | tf_op jit(solution)/shard_map/ppermute | solution.py:512
  50.3 16.2 %collective-permute-start.7 = (f32[320,256]{1,0:T(8,128)S(1)}, f32[320,256]{1,0:T(8,128)S(1)}, u32[]{:S(2)}, u32[]{:S(2)}) collective-permute-start(f32[320,256]{1,0:T(8,128)S(1)} %constant_dynamic-update-slice_fusion.refs_3_), channel_id=1, source_target_pairs={{0,8},{8,16},{16,24},{24,0},{1,9},{9,17},{17,25},{25,1},{2,10},{10... | collective-permute-start | bytes 983048 | tf_op jit(solution)/shard_map/ppermute | solution.py:512
  50.7 15.9 %collective-permute-start.8 = (f32[320,256]{1,0:T(8,128)S(1)}, f32[320,256]{1,0:T(8,128)S(1)}, u32[]{:S(2)}, u32[]{:S(2)}) collective-permute-start(f32[320,256]{1,0:T(8,128)S(1)} %constant_dynamic-update-slice_fusion.refs_3_), channel_id=1, source_target_pairs={{0,24},{8,0},{16,8},{24,16},{1,25},{9,1},{17,9},{25,17},{2,26},{10... | collective-permute-start | bytes 983048 | tf_op jit(solution)/shard_map/ppermute | solution.py:512
  53.7 12.9 %collective-permute-start.12 = (f32[80,1024]{1,0:T(8,128)S(1)}, f32[80,1024]{1,0:T(8,128)S(1)}, u32[]{:S(2)}, u32[]{:S(2)}) collective-permute-start(f32[80,1024]{1,0:T(8,128)S(1)} %get-tuple-element.92.refs_0_), channel_id=1, source_target_pairs={{0,3},{1,0},{2,1},{3,2},{4,7},{5,4},{6,5},{7,6},{8,11},{9,8},{10,9... | collective-permute-start | bytes 983048 | tf_op jit(solution)/shard_map/ppermute | solution.py:512
  62.7 7.4 %collective-permute-start.18 = (f32[80,1024]{1,0:T(8,128)S(1)}, f32[80,1024]{1,0:T(8,128)S(1)}, u32[]{:S(2)}, u32[]{:S(2)}) collective-permute-start(f32[80,1024]{1,0:T(8,128)S(1)} %get-tuple-element.92.refs_0_), channel_id=1, source_target_pairs={{0,4},{4,0},{1,5},{5,1},{2,6},{6,2},{3,7},{7,3},{8,12},{12,8},{9,1... | collective-permute-start | bytes 983048 | tf_op jit(solution)/shard_map/ppermute | solution.py:513
  63.0 11.6 %collective-permute-start.17 = (f32[80,1024]{1,0:T(8,128)S(1)}, f32[80,1024]{1,0:T(8,128)S(1)}, u32[]{:S(2)}, u32[]{:S(2)}) collective-permute-start(f32[80,1024]{1,0:T(8,128)S(1)} %get-tuple-element.92.refs_0_), channel_id=1, source_target_pairs={{0,2},{1,3},{2,0},{3,1},{4,6},{5,7},{6,4},{7,5},{8,10},{9,11},{10,... | collective-permute-start | bytes 983048 | tf_op jit(solution)/shard_map/ppermute | solution.py:512
  66.6 15.8 %collective-permute-start.16 = (f32[480,256]{1,0:T(8,128)S(1)}, f32[480,256]{1,0:T(8,128)S(1)}, u32[]{:S(2)}, u32[]{:S(2)}) collective-permute-start(f32[480,256]{1,0:T(8,128)S(1)} %pad_maximum_fusion.2), channel_id=1, source_target_pairs={{0,224},{32,0},{64,32},{96,64},{128,96},{160,128},{192,160},{224,1... | collective-permute-start | bytes 1474568 | tf_op jit(solution)/shard_map/ppermute | solution.py:512
  69.4 13.3 %collective-permute-start.15 = (f32[480,256]{1,0:T(8,128)S(1)}, f32[480,256]{1,0:T(8,128)S(1)}, u32[]{:S(2)}, u32[]{:S(2)}) collective-permute-start(f32[480,256]{1,0:T(8,128)S(1)} %pad_maximum_fusion.1), channel_id=1, source_target_pairs={{0,32},{32,64},{64,96},{96,128},{128,160},{160,192},{192,224},{224... | collective-permute-start | bytes 1474568 | tf_op jit(solution)/shard_map/ppermute | solution.py:512
  69.5 10.3 %collective-permute-start.14 = (f32[400,256]{1,0:T(8,128)S(1)}, f32[400,256]{1,0:T(8,128)S(1)}, u32[]{:S(2)}, u32[]{:S(2)}) collective-permute-start(f32[400,256]{1,0:T(8,128)S(1)} %pad_maximum_fusion.4), channel_id=1, source_target_pairs={{0,24},{8,0},{16,8},{24,16},{1,25},{9,1},{17,9},{25,17},{2,26},{10... | collective-permute-start | bytes 1228808 | tf_op jit(solution)/shard_map/ppermute | solution.py:512
  70.2 12.2 %collective-permute-start.13 = (f32[400,256]{1,0:T(8,128)S(1)}, f32[400,256]{1,0:T(8,128)S(1)}, u32[]{:S(2)}, u32[]{:S(2)}) collective-permute-start(f32[400,256]{1,0:T(8,128)S(1)} %pad_maximum_fusion.3), channel_id=1, source_target_pairs={{0,8},{8,16},{16,24},{24,0},{1,9},{9,17},{17,25},{25,1},{2,10},{10... | collective-permute-start | bytes 1228808 | tf_op jit(solution)/shard_map/ppermute | solution.py:512
  74.7 1.6 %collective-permute-start.19 = (f32[80,1024]{1,0:T(8,128)S(1)}, f32[80,1024]{1,0:T(8,128)S(1)}, u32[]{:S(2)}, u32[]{:S(2)}) collective-permute-start(f32[80,1024]{1,0:T(8,128)S(1)} %collective-permute-done.11.refs_1_), channel_id=1, source_target_pairs={{0,4},{4,0},{1,5},{5,1},{2,6},{6,2},{3,7},{7,3},{8,12},{12,8},{9,1... | collective-permute-start | bytes 983048 | tf_op jit(solution)/shard_map/ppermute | solution.py:513
  76.3 9.4 %collective-permute-start.25 = (f32[80,1024]{1,0:T(8,128)S(1)}, f32[80,1024]{1,0:T(8,128)S(1)}, u32[]{:S(2)}, u32[]{:S(2)}) collective-permute-start(f32[80,1024]{1,0:T(8,128)S(1)} %collective-permute-done.12.refs_3_), channel_id=1, source_target_pairs={{0,4},{4,0},{1,5},{5,1},{2,6},{6,2},{3,7},{7,3},{8,12},{12,8},{9,1... | collective-permute-start | bytes 983048 | tf_op jit(solution)/shard_map/ppermute | solution.py:513
  82.8 11.2 %collective-permute-start.23 = (f32[240,256]{1,0:T(8,128)S(1)}, f32[240,256]{1,0:T(8,128)S(1)}, u32[]{:S(2)}, u32[]{:S(2)}) collective-permute-start(f32[240,256]{1,0:T(8,128)S(1)} %pad_maximum_fusion.6), channel_id=1, source_target_pairs={{0,224},{32,0},{64,32},{96,64},{128,96},{160,128},{192,160},{224,1... | collective-permute-start | bytes 737288 | tf_op jit(solution)/shard_map/ppermute | solution.py:512
  85.5 9.7 %collective-permute-start.24 = (f32[80,1024]{1,0:T(8,128)S(1)}, f32[80,1024]{1,0:T(8,128)S(1)}, u32[]{:S(2)}, u32[]{:S(2)}) collective-permute-start(f32[80,1024]{1,0:T(8,128)S(1)} %collective-permute-done.17.refs_2_), channel_id=1, source_target_pairs={{0,4},{4,0},{1,5},{5,1},{2,6},{6,2},{3,7},{7,3},{8,12},{12,8},{9,1... | collective-permute-start | bytes 983048 | tf_op jit(solution)/shard_map/ppermute | solution.py:513
  85.6 9.7 %collective-permute-start.22 = (f32[240,256]{1,0:T(8,128)S(1)}, f32[240,256]{1,0:T(8,128)S(1)}, u32[]{:S(2)}, u32[]{:S(2)}) collective-permute-start(f32[240,256]{1,0:T(8,128)S(1)} %pad_maximum_fusion.5), channel_id=1, source_target_pairs={{0,32},{32,64},{64,96},{96,128},{128,160},{160,192},{192,224},{224... | collective-permute-start | bytes 737288 | tf_op jit(solution)/shard_map/ppermute | solution.py:512
  85.7 8.3 %collective-permute-start.20 = (f32[160,256]{1,0:T(8,128)S(1)}, f32[160,256]{1,0:T(8,128)S(1)}, u32[]{:S(2)}, u32[]{:S(2)}) collective-permute-start(f32[160,256]{1,0:T(8,128)S(1)} %slice.46), channel_id=1, source_target_pairs={{0,8},{8,16},{16,24},{24,0},{1,9},{9,17},{17,25},{25,1},{2,10},{10... | collective-permute-start | bytes 491528 | tf_op jit(solution)/shard_map/ppermute | solution.py:512
  85.8 8.2 %collective-permute-start.21 = (f32[160,256]{1,0:T(8,128)S(1)}, f32[160,256]{1,0:T(8,128)S(1)}, u32[]{:S(2)}, u32[]{:S(2)}) collective-permute-start(f32[160,256]{1,0:T(8,128)S(1)} %slice.47), channel_id=1, source_target_pairs={{0,24},{8,0},{16,8},{24,16},{1,25},{9,1},{17,9},{25,17},{2,26},{10... | collective-permute-start | bytes 491528 | tf_op jit(solution)/shard_map/ppermute | solution.py:512
  95.2 8.0 %collective-permute-start.26 = (f32[80,256]{1,0:T(8,128)S(1)}, f32[80,256]{1,0:T(8,128)S(1)}, u32[]{:S(2)}, u32[]{:S(2)}) collective-permute-start(f32[80,256]{1,0:T(8,128)S(1)} %slice.50), channel_id=1, source_target_pairs={{0,8},{8,16},{16,24},{24,0},{1,9},{9,17},{17,25},{25,1},{2,10},{10... | collective-permute-start | bytes 245768 | tf_op jit(solution)/shard_map/ppermute | solution.py:512
  95.3 7.9 %collective-permute-start.27 = (f32[80,256]{1,0:T(8,128)S(1)}, f32[80,256]{1,0:T(8,128)S(1)}, u32[]{:S(2)}, u32[]{:S(2)}) collective-permute-start(f32[80,256]{1,0:T(8,128)S(1)} %slice.51), channel_id=1, source_target_pairs={{0,24},{8,0},{16,8},{24,16},{1,25},{9,1},{17,9},{25,17},{2,26},{10... | collective-permute-start | bytes 245768 | tf_op jit(solution)/shard_map/ppermute | solution.py:512
  112.4 3.1 %collective-permute-start.28 = (f32[4,8,3584]{2,1,0:T(8,128)S(1)}, f32[4,8,3584]{2,1,0:T(8,128)S(1)}, u32[]{:S(2)}, u32[]{:S(2)}) collective-permute-start(f32[4,8,3584]{2,1,0:T(8,128)S(1)} %get-tuple-element.124), channel_id=1, source_target_pairs={{0,4},{4,0},{1,5},{5,1},{2,6},{6,2},{3,7},{7,3},{8,12},{12,8},{9,1... | collective-permute-start | bytes 1376264 | tf_op jit(solution)/shard_map/ppermute | solution.py:513
  115.5 5.9 %collective-permute-start.29 = (f32[8,3584]{1,0:T(8,128)S(1)}, f32[8,3584]{1,0:T(8,128)S(1)}, u32[]{:S(2)}, u32[]{:S(2)}) collective-permute-start(f32[8,3584]{1,0:T(8,128)S(1)} %get-tuple-element.126), channel_id=1, source_target_pairs={{0,1},{1,2},{2,3},{3,0},{4,5},{5,6},{6,7},{7,4},{8,9},{9,10},{10,1... | collective-permute-start | bytes 344072 | tf_op jit(solution)/shard_map/ppermute | solution.py:512
  117.4 7.5 %collective-permute-start.30 = (f32[8,3584]{1,0:T(8,128)S(1)}, f32[8,3584]{1,0:T(8,128)S(1)}, u32[]{:S(2)}, u32[]{:S(2)}) collective-permute-start(f32[8,3584]{1,0:T(8,128)S(1)} %get-tuple-element.127), channel_id=1, source_target_pairs={{0,2},{1,3},{2,0},{3,1},{4,6},{5,7},{6,4},{7,5},{8,10},{9,11},{10,... | collective-permute-start | bytes 344072 | tf_op jit(solution)/shard_map/ppermute | solution.py:512
  118.8 7.7 %collective-permute-start.31 = (f32[8,3584]{1,0:T(8,128)S(1)}, f32[8,3584]{1,0:T(8,128)S(1)}, u32[]{:S(2)}, u32[]{:S(2)}) collective-permute-start(f32[8,3584]{1,0:T(8,128)S(1)} %get-tuple-element.128), channel_id=1, source_target_pairs={{0,3},{1,0},{2,1},{3,2},{4,7},{5,4},{6,5},{7,6},{8,11},{9,8},{10,9... | collective-permute-start | bytes 344072 | tf_op jit(solution)/shard_map/ppermute | solution.py:512
  (6 other events, 82.0 us)

commit v5 on v3

--- a/solution.py
+++ b/solution.py
@@ -277,26 +277,24 @@
 
 def extract(place, table, half, kern, out_ref):
     at = lambda x: lax.rem(x + 4 - place[1], 4)
-    lane = lax.broadcasted_iota(jnp.int32, (8, 128), 1) // BLK
+    lane = lax.broadcasted_iota(jnp.int32, (BLK, 128), 1) // BLK
     upper = lax.broadcasted_iota(jnp.int32, (8, 128), 0) < 4
 
     def groups(pair, carry):
         for g in (pair * 2, pair * 2 + 1):
-            tiles = [[jnp.zeros((8, 128), jnp.float32) for _ in range(2)] for _ in range(2)]
+            slabs = [None, None]
             for u in range(8):
                 slot = g * 8 + u
-                row = pl.multiple_of(table[4 * half, slot], BLK)
+                row = pl.ds(pl.multiple_of(table[4 * half, slot], BLK), BLK)
                 column = pl.multiple_of(table[4 * half + 1, slot], 128)
                 shift = table[4 * half + 2, slot]
-                target = table[4 * half + 3, slot]
+                target = lane == table[4 * half + 3, slot]
                 for part in range(2):
-                    for side in range(2):
-                        tile = kern[pl.ds(row + side * 8, 8), pl.ds(column + part * HALF, 128)]
-                        tile = pltpu.roll(tile, shift, 1)
-                        tiles[part][side] = jnp.where(lane == target, tile, tiles[part][side])
+                    slab = pltpu.roll(kern[row, pl.ds(column + part * HALF, 128)], shift, 1)
+                    slabs[part] = jnp.where(target, slab, 0.0 if u == 0 else slabs[part])
             lanes = pl.ds(pl.multiple_of(g * 128, 128), 128)
             for side in range(2):
-                real, imag = tiles[0][side], tiles[1][side]
+                real, imag = (slab[side * 8 : side * 8 + 8] for slab in slabs)
                 out_ref[at(2 * side), :, lanes] = jnp.where(upper, real, pltpu.roll(imag, 4, 0))
                 out_ref[at(2 * side + 1), :, lanes] = jnp.where(upper, pltpu.roll(real, 4, 0), imag)
         return carry
@@ -556,15 +554,15 @@
     rights = (first, first_down, first_up, second, second_down, second_up, two_down, two_up)
     total = group_call(near_runs, len(NEAR), place, rights, screens[:2], ())
     swapped[2:] = [swap(array) for array in around[2:]]
-    y_below, y_above, far_below, far_above, total, *swapped[2:] = hold(
-        (y_below, y_above, far_below, far_above, total, *swapped[2:])
+    left_high, left_low = left_call(place, around + swapped)
+    y_below, y_above, far_below, far_above, total, left_high, left_low = hold(
+        (y_below, y_above, far_below, far_above, total, left_high, left_low)
     )
 
     across_low, across_high = shift(far_below[:SPAN], "y", 1), shift(far_above[SPAN : 2 * SPAN], "y", -1)
     rights = (z_below, z_above, y_below, y_above)
     total = group_call(middle_runs, len(MIDDLE), place, rights, screens[2:4], (total,))
-    left_high, left_low = left_call(place, around + swapped)
-    across_low, across_high, total, left_high, left_low = hold((across_low, across_high, total, left_high, left_low))
+    across_low, across_high, total = hold((across_low, across_high, total))
     rights = (far_below, far_above, across_low, across_high)
     give, kern = pair_call(place, table, rights, screens[4:], total, left_high, left_low)
 

time: 145 us -> 146 us (level)
  transfers between devices with their start and end apart: 33 -> 33, of which waited for: 16 -> 19; matrix products, arithmetic and copies ran while one was open for 1% -> 1% of each run, Pallas kernels for 15% -> 15%
where the time goes in v5:
time: 146 us; the launch traced here: 145 us
  starting transfers between devices  48.2 us (33%)
  waiting for transfers between devices  37.9 us (26%)
  Pallas kernels  37.8 us (26%)
  blocking collectives  17 us (12%)
  local copies, waits for them, and re-layouts  2.98 us (2%)
    ppermute x24, starting transfers between devices, shards(): lax.ppermute(array, axis, ring(lax.axis_size(axis), by))  35.8 us
    ppermute x24, waiting for transfers between devices, shards(): lax.ppermute(array, axis, ring(lax.axis_size(axis), by))  22.4 us
    all_to_all x1, blocking collectives, shards(): parts = lax.all_to_all(parts, ('z', 'y'), 0, 0, tiled=True)  17 us
    all_to_all x1, starting transfers between devices, shards(): lax.all_to_all(pieces.reshape(32, 1, -1), ('z', 'y'), 0, 0, tiled=True)  11.6 us
    all_to_all x1, waiting for transfers between devices, shards(): lax.all_to_all(pieces.reshape(32, 1, -1), ('z', 'y'), 0, 0, tiled=True)  11.4 us
    pallas_call x1, Pallas kernels, pair_call(): pl.pallas_call(pair_kernel, out_shape=(jax.ShapeDtypeStruct((4, 8, ROOM *...  8.54 us
    pallas_call x2, Pallas kernels, group_call(): pl.pallas_call(functools.partial(group_kernel, runs, planes), out_shape=j...  7.55 us
    pallas_call x1, Pallas kernels, screen_call(): pl.pallas_call(screen_kernel, out_shape=shapes, in_specs=[SMEM, VMEM, VME...  7.35 us
  transfers between devices with their start and end apart: 33, of which 19 were waited for; matrix products, arithmetic and copies ran while one was open for 1% of the time, Pallas kernels for 15%

profile of v5, /device:TPU:2, one launch (start us, length us, event | category | flops | bytes accessed | tf_op | source)
XLA Modules:
  0.0 145.1 jit_solution(17066008043183298902)
XLA Ops:
  2.0 2.2 %pack.1 = f32[640,128]{1,0:T(8,128)} custom-call(s32[4]{0:T(128)} %pad_add_fusion.place, f32[2,16,2560]{2,1,0:T(8,128)} %own_ref.1, f32[2,16,2560]{2,1,0:T(8,128)} %collective-permute-done.other_ref), custom_call_target="tpu_custom_call" | custom-call | tf_op jit(solution)/shard_map/pack/pallas_call | solution.py:422
  4.4 11.6 %all-to-all-start = ((f32[32,1,2560]{2,1,0:T(1,128)}), f32[32,1,2560]{2,1,0:T(1,128)}, u32[]{:S(2)}, u32[]{:S(2)}) async-start(f32[32,1,2560]{2,1,0:T(1,128)} %bitcast.12), calls=%async_computation | async-start | bytes 655360 | tf_op jit(solution)/shard_map/all_to_all | solution.py:517
  19.4 11.4 %all-to-all-done = f32[32,1,2560]{2,1,0:T(1,128)} async-done(((f32[32,1,2560]{2,1,0:T(1,128)}), f32[32,1,2560]{2,1,0:T(1,128)}, u32[]{:S(2)}, u32[]{:S(2)}) %all-to-all-start) | async-done | bytes 327712 | tf_op jit(solution)/shard_map/all_to_all | solution.py:517
  31.5 2.5 %unpack.1 = (f32[80,1024]{1,0:T(8,128)S(1)}, f32[80,256]{1,0:T(8,128)S(1)}, f32[80,256]{1,0:T(8,128)S(1)}) custom-call(s32[4]{0:T(128)S(1)} %copy-done.2, s32[16,256]{1,0:T(8,128)S(1)} %plan.1.table, f32[640,128]{1,0:T(8,128)} %bitcast.6.in_ref), custom_call_target="tpu_custom_call" | custom-call | tf_op jit(solution)/shard_map/unpack/pallas_call | solution.py:471
  36.2 1.8 %collective-permute-start.5 = (f32[160,256]{1,0:T(8,128)S(1)}, f32[160,256]{1,0:T(8,128)S(1)}, u32[]{:S(2)}, u32[]{:S(2)}) collective-permute-start(f32[160,256]{1,0:T(8,128)S(1)} %shard.1), channel_id=1, source_target_pairs={{0,32},{32,64},{64,96},{96,128},{128,160},{160,192},{192,224},{224... | collective-permute-start | bytes 491528 | tf_op jit(solution)/shard_map/ppermute | solution.py:510
  38.9 2.0 %collective-permute-start.3 = (f32[160,256]{1,0:T(8,128)S(1)}, f32[160,256]{1,0:T(8,128)S(1)}, u32[]{:S(2)}, u32[]{:S(2)}) collective-permute-start(f32[160,256]{1,0:T(8,128)S(1)} %shard.1), channel_id=1, source_target_pairs={{0,64},{32,96},{64,128},{96,160},{128,192},{160,224},{192,0},{224,... | collective-permute-start | bytes 491528 | tf_op jit(solution)/shard_map/ppermute | solution.py:510
  40.9 2.6 %collective-permute-done.6 = f32[160,256]{1,0:T(8,128)S(1)} collective-permute-done((f32[160,256]{1,0:T(8,128)S(1)}, f32[160,256]{1,0:T(8,128)S(1)}, u32[]{:S(2)}, u32[]{:S(2)}) %collective-permute-start.6) | collective-permute-done | bytes 163872 | tf_op jit(solution)/shard_map/ppermute | solution.py:510
  43.5 1.5 %collective-permute-done.5 = f32[160,256]{1,0:T(8,128)S(1)} collective-permute-done((f32[160,256]{1,0:T(8,128)S(1)}, f32[160,256]{1,0:T(8,128)S(1)}, u32[]{:S(2)}, u32[]{:S(2)}) %collective-permute-start.5) | collective-permute-done | bytes 163872 | tf_op jit(solution)/shard_map/ppermute | solution.py:510
  45.1 1.5 %collective-permute-start.11 = (f32[80,1024]{1,0:T(8,128)S(1)}, f32[80,1024]{1,0:T(8,128)S(1)}, u32[]{:S(2)}, u32[]{:S(2)}) collective-permute-start(f32[80,1024]{1,0:T(8,128)S(1)} %get-tuple-element.90.refs_0_), channel_id=1, source_target_pairs={{0,1},{1,2},{2,3},{3,0},{4,5},{5,6},{6,7},{7,4},{8,9},{9,10},{10,1... | collective-permute-start | bytes 983048 | tf_op jit(solution)/shard_map/ppermute | solution.py:510
  49.6 2.0 %collective-permute-start.8 = (f32[320,256]{1,0:T(8,128)S(1)}, f32[320,256]{1,0:T(8,128)S(1)}, u32[]{:S(2)}, u32[]{:S(2)}) collective-permute-start(f32[320,256]{1,0:T(8,128)S(1)} %constant_dynamic-update-slice_fusion.refs_3_), channel_id=1, source_target_pairs={{0,24},{8,0},{16,8},{24,16},{1,25},{9,1},{17,9},{25,17},{2,26},{10... | collective-permute-start | bytes 983048 | tf_op jit(solution)/shard_map/ppermute | solution.py:510
  52.4 1.7 %collective-permute-start.12 = (f32[80,1024]{1,0:T(8,128)S(1)}, f32[80,1024]{1,0:T(8,128)S(1)}, u32[]{:S(2)}, u32[]{:S(2)}) collective-permute-start(f32[80,1024]{1,0:T(8,128)S(1)} %get-tuple-element.90.refs_0_), channel_id=1, source_target_pairs={{0,3},{1,0},{2,1},{3,2},{4,7},{5,4},{6,5},{7,6},{8,11},{9,8},{10,9... | collective-permute-start | bytes 983048 | tf_op jit(solution)/shard_map/ppermute | solution.py:510
  54.1 7.3 %screen.1 = (bf16[640,1664]{1,0:T(8,128)(2,1)S(1)}, bf16[640,1664]{1,0:T(8,128)(2,1)S(1)}, bf16[640,640]{1,0:T(8,128)(2,1)S(1)}, bf16[640,640]{1,0:T(8,128)(2,1)...) custom-call(s32[4]{0:T(128)S(1)} %copy-done.3, f32[320,2560]{1,0:T(8,128)S(1)} %bitcast.10, ...), custom_call_target="tpu_custom_call" | custom-call | tf_op jit(solution)/shard_map/screen/pallas_call | solution.py:153
  61.8 1.3 collective-permute-done.9.refs_1_
  64.2 2.4 %collective-permute-done.7.refs_4_ = f32[320,256]{1,0:T(8,128)S(1)} collective-permute-done((f32[320,256]{1,0:T(8,128)S(1)}, f32[320,256]{1,0:T(8,128)S(1)}, u32[]{:S(2)}, u32[]{:S(2)}) %collective-permute-start.7) | collective-permute-done | bytes 327712 | tf_op jit(solution)/shard_map/ppermute | solution.py:510
  68.3 3.2 %collective-permute-start.16 = (f32[480,256]{1,0:T(8,128)S(1)}, f32[480,256]{1,0:T(8,128)S(1)}, u32[]{:S(2)}, u32[]{:S(2)}) collective-permute-start(f32[480,256]{1,0:T(8,128)S(1)} %pad_maximum_fusion.2), channel_id=1, source_target_pairs={{0,224},{32,0},{64,32},{96,64},{128,96},{160,128},{192,160},{224,1... | collective-permute-start | bytes 1474568 | tf_op jit(solution)/shard_map/ppermute | solution.py:510
  71.6 3.2 %collective-permute-start.14 = (f32[400,256]{1,0:T(8,128)S(1)}, f32[400,256]{1,0:T(8,128)S(1)}, u32[]{:S(2)}, u32[]{:S(2)}) collective-permute-start(f32[400,256]{1,0:T(8,128)S(1)} %pad_maximum_fusion.4), channel_id=1, source_target_pairs={{0,24},{8,0},{16,8},{24,16},{1,25},{9,1},{17,9},{25,17},{2,26},{10... | collective-permute-start | bytes 1228808 | tf_op jit(solution)/shard_map/ppermute | solution.py:510
  75.4 1.6 %collective-permute-done.19.refs_5_ = f32[80,1024]{1,0:T(8,128)S(1)} collective-permute-done((f32[80,1024]{1,0:T(8,128)S(1)}, f32[80,1024]{1,0:T(8,128)S(1)}, u32[]{:S(2)}, u32[]{:S(2)}) %collective-permute-start.19) | collective-permute-done | bytes 327712 | tf_op jit(solution)/shard_map/ppermute | solution.py:511
  77.2 3.0 %collective-permute-done.14.refs_7_ = f32[400,256]{1,0:T(8,128)S(1)} collective-permute-done((f32[400,256]{1,0:T(8,128)S(1)}, f32[400,256]{1,0:T(8,128)S(1)}, u32[]{:S(2)}, u32[]{:S(2)}) %collective-permute-start.14) | collective-permute-done | bytes 409632 | tf_op jit(solution)/shard_map/ppermute | solution.py:510
  81.0 2.7 %collective-permute-start.23 = (f32[240,256]{1,0:T(8,128)S(1)}, f32[240,256]{1,0:T(8,128)S(1)}, u32[]{:S(2)}, u32[]{:S(2)}) collective-permute-start(f32[240,256]{1,0:T(8,128)S(1)} %pad_maximum_fusion.6), channel_id=1, source_target_pairs={{0,224},{32,0},{64,32},{96,64},{128,96},{160,128},{192,160},{224,1... | collective-permute-start | bytes 737288 | tf_op jit(solution)/shard_map/ppermute | solution.py:510
  83.8 3.7 %collective-permute-start.21 = (f32[160,256]{1,0:T(8,128)S(1)}, f32[160,256]{1,0:T(8,128)S(1)}, u32[]{:S(2)}, u32[]{:S(2)}) collective-permute-start(f32[160,256]{1,0:T(8,128)S(1)} %slice.47), channel_id=1, source_target_pairs={{0,24},{8,0},{16,8},{24,16},{1,25},{9,1},{17,9},{25,17},{2,26},{10... | collective-permute-start | bytes 491528 | tf_op jit(solution)/shard_map/ppermute | solution.py:510
  87.5 5.0 %group.2.refs_6_ = f32[640,512]{1,0:T(8,128)S(1)} custom-call(s32[4]{0:T(128)S(1)} %copy-done.3, f32[480,256]{1,0:T(8,128)S(1)} %pad_maximum_fusion.refs_0_, f32[480,256]{1,0:T(8,128)S(1)} %collective-permute-done.9.refs_1_, f32[480,256]{1,0:T(8,128)S(1)} %collective-permute-done.10.refs_2_, f32[320,256]{1,0:T(8,128)S(1)} %constant_dynamic-update-slice_fusion.refs_3_, ...), custom_call_target="tpu_custom_call" | custom-call | tf_op jit(solution)/shard_map/group/pallas_call | solution.py:252
  92.5 2.1 %left.1 = (bf16[1024,640]{1,0:T(8,128)(2,1)S(1)}, bf16[1024,640]{1,0:T(8,128)(2,1)S(1)}) custom-call(s32[4]{0:T(128)S(1)} %copy-done.3, f32[80,1024]{1,0:T(8,128)S(1)} %get-tuple-element.90.refs_0_, f32[80,1024]{1,0:T(8,128)S(1)} %collective-permute-done.11.refs_1_, f32[80,1024]{1,0:T(8,128)S(1)} %collective-permute-done.17.refs_2_, ...), custom_call_target="tpu_custom_call" | custom-call | tf_op jit(solution)/shard_map/left/pallas_call | solution.py:185
  94.8 3.2 %collective-permute-start.27 = (f32[80,256]{1,0:T(8,128)S(1)}, f32[80,256]{1,0:T(8,128)S(1)}, u32[]{:S(2)}, u32[]{:S(2)}) collective-permute-start(f32[80,256]{1,0:T(8,128)S(1)} %slice.51), channel_id=1, source_target_pairs={{0,24},{8,0},{16,8},{24,16},{1,25},{9,1},{17,9},{25,17},{2,26},{10... | collective-permute-start | bytes 245768 | tf_op jit(solution)/shard_map/ppermute | solution.py:510
  98.0 2.5 %group.3.refs_6_ = f32[640,512]{1,0:T(8,128)S(1)} custom-call(s32[4]{0:T(128)S(1)} %copy-done.3, f32[480,256]{1,0:T(8,128)S(1)} %collective-permute-done.15.refs_0_, f32[480,256]{1,0:T(8,128)S(1)} %collective-permute-done.16.refs_1_, f32[160,256]{1,0:T(8,128)S(1)} %collective-permute-done.20.refs_2_, f32[160,256]{1,0:T(8,128)S(1)} %collective-permute-done.21.refs_3_, ...), custom_call_target="tpu_custom_call" | custom-call | tf_op jit(solution)/shard_map/group/pallas_call | solution.py:252
  100.5 3.1 %collective-permute-done.26.refs_2_ = f32[80,256]{1,0:T(8,128)S(1)} collective-permute-done((f32[80,256]{1,0:T(8,128)S(1)}, f32[80,256]{1,0:T(8,128)S(1)}, u32[]{:S(2)}, u32[]{:S(2)}) %collective-permute-start.26) | collective-permute-done | bytes 81952 | tf_op jit(solution)/shard_map/ppermute | solution.py:510
  103.6 8.5 %pair.1 = (f32[4,8,3584]{2,1,0:T(8,128)S(1)}, f32[1024,512]{1,0:T(8,128)S(1)}) custom-call(s32[4]{0:T(128)S(1)} %copy-done.3, s32[16,256]{1,0:T(8,128)S(1)} %plan.1.table, f32[240,256]{1,0:T(8,128)S(1)} %collective-permute-done.22.refs_0_, f32[240,256]{1,0:T(8,128)S(1)} %collective-permute-done.23.refs_1_, f32[80,256]{1,0:T(8,128)S(1)} %collective-permute-done.26.refs_2_, ...), custom_call_target="tpu_custom_call" | custom-call | tf_op jit(solution)/shard_map/pair/pallas_call | solution.py:308
  112.3 2.9 %extract.1.one_ref = f32[4,8,3584]{2,1,0:T(8,128)S(1)} custom-call(s32[4]{0:T(128)S(1)} %copy-done.3, s32[16,256]{1,0:T(8,128)S(1)} %plan.1.table, f32[1024,512]{1,0:T(8,128)S(1)} %get-tuple-element.119.kern), custom_call_target="tpu_custom_call" | custom-call | tf_op jit(solution)/shard_map/extract/pallas_call | solution.py:327
  116.2 3.3 %collective-permute-start.30 = (f32[8,3584]{1,0:T(8,128)S(1)}, f32[8,3584]{1,0:T(8,128)S(1)}, u32[]{:S(2)}, u32[]{:S(2)}) collective-permute-start(f32[8,3584]{1,0:T(8,128)S(1)} %get-tuple-element.123), channel_id=1, source_target_pairs={{0,2},{1,3},{2,0},{3,1},{4,6},{5,7},{6,4},{7,5},{8,10},{9,11},{10,... | collective-permute-start | bytes 344072 | tf_op jit(solution)/shard_map/ppermute | solution.py:510
  121.1 2.6 %collective-permute-done.30.three_ref = f32[8,3584]{1,0:T(8,128)S(1)} collective-permute-done((f32[8,3584]{1,0:T(8,128)S(1)}, f32[8,3584]{1,0:T(8,128)S(1)}, u32[]{:S(2)}, u32[]{:S(2)}) %collective-permute-start.30) | collective-permute-done | bytes 114720 | tf_op jit(solution)/shard_map/ppermute | solution.py:510
  123.7 1.6 %collective-permute-done.31.four_ref = f32[8,3584]{1,0:T(8,128)S(1)} collective-permute-done((f32[8,3584]{1,0:T(8,128)S(1)}, f32[8,3584]{1,0:T(8,128)S(1)}, u32[]{:S(2)}, u32[]{:S(2)}) %collective-permute-start.31) | collective-permute-done | bytes 114720 | tf_op jit(solution)/shard_map/ppermute | solution.py:510
  126.5 17.0 %all_to_all.10.parts_ref = f32[32,8,256]{2,1,0:T(8,128)S(1)} all-to-all(f32[32,8,256]{2,1,0:T(8,128)S(1)} %owner.1), channel_id=1, replica_groups=mesh['z'=8,'y'=4,'core'=2,'x'=4] {'z','y'}, dimensions={0} | all-to-all | bytes 524288 | tf_op jit(solution)/shard_map/all_to_all | solution.py:572
  143.6 1.5 %last.1 = f32[12,8,16]{2,1,0:T(8,128)} custom-call(s32[4]{0:T(128)S(1)} %copy-done.3, s32[16,256]{1,0:T(8,128)S(1)} %plan.1.table, f32[32,8,256]{2,1,0:T(8,128)S(1)} %all_to_all.10.parts_ref), custom_call_target="tpu_custom_call" | custom-call | tf_op jit(solution)/shard_map/last/pallas_call | solution.py:389
  (79 shorter events, 21.9 us)
Async XLA Ops:
  0.0 2.0 %collective-permute-start = (f32[2,16,2560]{2,1,0:T(8,128)}, f32[2,16,2560]{2,1,0:T(8,128)}, u32[]{:S(2)}, u32[]{:S(2)}) collective-permute-start(f32[2,16,2560]{2,1,0:T(8,128)} %own_ref.1), channel_id=1, source_target_pairs={{0,4},{4,0},{1,5},{5,1},{2,6},{6,2},{3,7},{7,3},{8,12},{12,8},{9,1... | collective-permute-start | bytes 983048 | tf_op jit(solution)/shard_map/ppermute | solution.py:511
  4.2 26.6 %collective-permute-start.1 = (f32[320,2560]{1,0:T(8,128)}, f32[320,2560]{1,0:T(8,128)}, u32[]{:S(2)}, u32[]{:S(2)}) collective-permute-start(f32[320,2560]{1,0:T(8,128)} %bitcast.9), channel_id=1, source_target_pairs={{0,4},{4,0},{1,5},{5,1},{2,6},{6,2},{3,7},{7,3},{8,12},{12,8},{9,1... | collective-permute-start | bytes 9830408 | tf_op jit(solution)/shard_map/ppermute | solution.py:511
  4.4 26.4 %all-to-all-start = ((f32[32,1,2560]{2,1,0:T(1,128)}), f32[32,1,2560]{2,1,0:T(1,128)}, u32[]{:S(2)}, u32[]{:S(2)}) async-start(f32[32,1,2560]{2,1,0:T(1,128)} %bitcast.12), calls=%async_computation | async-start | bytes 655360 | tf_op jit(solution)/shard_map/all_to_all | solution.py:517
  35.9 7.6 %collective-permute-start.6 = (f32[160,256]{1,0:T(8,128)S(1)}, f32[160,256]{1,0:T(8,128)S(1)}, u32[]{:S(2)}, u32[]{:S(2)}) collective-permute-start(f32[160,256]{1,0:T(8,128)S(1)} %shard.1), channel_id=1, source_target_pairs={{0,224},{32,0},{64,32},{96,64},{128,96},{160,128},{192,160},{224,1... | collective-permute-start | bytes 491528 | tf_op jit(solution)/shard_map/ppermute | solution.py:510
  36.2 8.9 %collective-permute-start.5 = (f32[160,256]{1,0:T(8,128)S(1)}, f32[160,256]{1,0:T(8,128)S(1)}, u32[]{:S(2)}, u32[]{:S(2)}) collective-permute-start(f32[160,256]{1,0:T(8,128)S(1)} %shard.1), channel_id=1, source_target_pairs={{0,32},{32,64},{64,96},{96,128},{128,160},{160,192},{192,224},{224... | collective-permute-start | bytes 491528 | tf_op jit(solution)/shard_map/ppermute | solution.py:510
  38.0 11.6 %collective-permute-start.4 = (f32[160,256]{1,0:T(8,128)S(1)}, f32[160,256]{1,0:T(8,128)S(1)}, u32[]{:S(2)}, u32[]{:S(2)}) collective-permute-start(f32[160,256]{1,0:T(8,128)S(1)} %shard.1), channel_id=1, source_target_pairs={{0,192},{32,224},{64,0},{96,32},{128,64},{160,96},{192,128},{224,1... | collective-permute-start | bytes 491528 | tf_op jit(solution)/shard_map/ppermute | solution.py:510
  38.9 10.7 %collective-permute-start.3 = (f32[160,256]{1,0:T(8,128)S(1)}, f32[160,256]{1,0:T(8,128)S(1)}, u32[]{:S(2)}, u32[]{:S(2)}) collective-permute-start(f32[160,256]{1,0:T(8,128)S(1)} %shard.1), channel_id=1, source_target_pairs={{0,64},{32,96},{64,128},{96,160},{128,192},{160,224},{192,0},{224,... | collective-permute-start | bytes 491528 | tf_op jit(solution)/shard_map/ppermute | solution.py:510
  45.1 7.3 %collective-permute-start.11 = (f32[80,1024]{1,0:T(8,128)S(1)}, f32[80,1024]{1,0:T(8,128)S(1)}, u32[]{:S(2)}, u32[]{:S(2)}) collective-permute-start(f32[80,1024]{1,0:T(8,128)S(1)} %get-tuple-element.90.refs_0_), channel_id=1, source_target_pairs={{0,1},{1,2},{2,3},{3,0},{4,5},{5,6},{6,7},{7,4},{8,9},{9,10},{10,1... | collective-permute-start | bytes 983048 | tf_op jit(solution)/shard_map/ppermute | solution.py:510
  46.6 14.9 %collective-permute-start.10 = (f32[480,256]{1,0:T(8,128)S(1)}, f32[480,256]{1,0:T(8,128)S(1)}, u32[]{:S(2)}, u32[]{:S(2)}) collective-permute-start(f32[480,256]{1,0:T(8,128)S(1)} %pad_maximum_fusion.refs_0_), channel_id=1, source_target_pairs={{0,24},{8,0},{16,8},{24,16},{1,25},{9,1},{17,9},{25,17},{2,26},{10... | collective-permute-start | bytes 1474568 | tf_op jit(solution)/shard_map/ppermute | solution.py:510
  47.7 15.4 %collective-permute-start.9 = (f32[480,256]{1,0:T(8,128)S(1)}, f32[480,256]{1,0:T(8,128)S(1)}, u32[]{:S(2)}, u32[]{:S(2)}) collective-permute-start(f32[480,256]{1,0:T(8,128)S(1)} %pad_maximum_fusion.refs_0_), channel_id=1, source_target_pairs={{0,8},{8,16},{16,24},{24,0},{1,9},{9,17},{17,25},{25,1},{2,10},{10... | collective-permute-start | bytes 1474568 | tf_op jit(solution)/shard_map/ppermute | solution.py:510
  49.6 14.6 %collective-permute-start.8 = (f32[320,256]{1,0:T(8,128)S(1)}, f32[320,256]{1,0:T(8,128)S(1)}, u32[]{:S(2)}, u32[]{:S(2)}) collective-permute-start(f32[320,256]{1,0:T(8,128)S(1)} %constant_dynamic-update-slice_fusion.refs_3_), channel_id=1, source_target_pairs={{0,24},{8,0},{16,8},{24,16},{1,25},{9,1},{17,9},{25,17},{2,26},{10... | collective-permute-start | bytes 983048 | tf_op jit(solution)/shard_map/ppermute | solution.py:510
  51.6 15.0 %collective-permute-start.7 = (f32[320,256]{1,0:T(8,128)S(1)}, f32[320,256]{1,0:T(8,128)S(1)}, u32[]{:S(2)}, u32[]{:S(2)}) collective-permute-start(f32[320,256]{1,0:T(8,128)S(1)} %constant_dynamic-update-slice_fusion.refs_3_), channel_id=1, source_target_pairs={{0,8},{8,16},{16,24},{24,0},{1,9},{9,17},{17,25},{25,1},{2,10},{10... | collective-permute-start | bytes 983048 | tf_op jit(solution)/shard_map/ppermute | solution.py:510
  52.4 14.2 %collective-permute-start.12 = (f32[80,1024]{1,0:T(8,128)S(1)}, f32[80,1024]{1,0:T(8,128)S(1)}, u32[]{:S(2)}, u32[]{:S(2)}) collective-permute-start(f32[80,1024]{1,0:T(8,128)S(1)} %get-tuple-element.90.refs_0_), channel_id=1, source_target_pairs={{0,3},{1,0},{2,1},{3,2},{4,7},{5,4},{6,5},{7,6},{8,11},{9,8},{10,9... | collective-permute-start | bytes 983048 | tf_op jit(solution)/shard_map/ppermute | solution.py:510
  61.5 10.0 %collective-permute-start.18 = (f32[80,1024]{1,0:T(8,128)S(1)}, f32[80,1024]{1,0:T(8,128)S(1)}, u32[]{:S(2)}, u32[]{:S(2)}) collective-permute-start(f32[80,1024]{1,0:T(8,128)S(1)} %get-tuple-element.90.refs_0_), channel_id=1, source_target_pairs={{0,4},{4,0},{1,5},{5,1},{2,6},{6,2},{3,7},{7,3},{8,12},{12,8},{9,1... | collective-permute-start | bytes 983048 | tf_op jit(solution)/shard_map/ppermute | solution.py:511
  66.7 8.7 %collective-permute-start.17 = (f32[80,1024]{1,0:T(8,128)S(1)}, f32[80,1024]{1,0:T(8,128)S(1)}, u32[]{:S(2)}, u32[]{:S(2)}) collective-permute-start(f32[80,1024]{1,0:T(8,128)S(1)} %get-tuple-element.90.refs_0_), channel_id=1, source_target_pairs={{0,2},{1,3},{2,0},{3,1},{4,6},{5,7},{6,4},{7,5},{8,10},{9,11},{10,... | collective-permute-start | bytes 983048 | tf_op jit(solution)/shard_map/ppermute | solution.py:510
  68.0 9.2 %collective-permute-start.13 = (f32[400,256]{1,0:T(8,128)S(1)}, f32[400,256]{1,0:T(8,128)S(1)}, u32[]{:S(2)}, u32[]{:S(2)}) collective-permute-start(f32[400,256]{1,0:T(8,128)S(1)} %pad_maximum_fusion.3), channel_id=1, source_target_pairs={{0,8},{8,16},{16,24},{24,0},{1,9},{9,17},{17,25},{25,1},{2,10},{10... | collective-permute-start | bytes 1228808 | tf_op jit(solution)/shard_map/ppermute | solution.py:510
  68.1 12.2 %collective-permute-start.15 = (f32[480,256]{1,0:T(8,128)S(1)}, f32[480,256]{1,0:T(8,128)S(1)}, u32[]{:S(2)}, u32[]{:S(2)}) collective-permute-start(f32[480,256]{1,0:T(8,128)S(1)} %pad_maximum_fusion.1), channel_id=1, source_target_pairs={{0,32},{32,64},{64,96},{96,128},{128,160},{160,192},{192,224},{224... | collective-permute-start | bytes 1474568 | tf_op jit(solution)/shard_map/ppermute | solution.py:510
  68.3 11.9 %collective-permute-start.16 = (f32[480,256]{1,0:T(8,128)S(1)}, f32[480,256]{1,0:T(8,128)S(1)}, u32[]{:S(2)}, u32[]{:S(2)}) collective-permute-start(f32[480,256]{1,0:T(8,128)S(1)} %pad_maximum_fusion.2), channel_id=1, source_target_pairs={{0,224},{32,0},{64,32},{96,64},{128,96},{160,128},{192,160},{224,1... | collective-permute-start | bytes 1474568 | tf_op jit(solution)/shard_map/ppermute | solution.py:510
  71.6 8.7 %collective-permute-start.14 = (f32[400,256]{1,0:T(8,128)S(1)}, f32[400,256]{1,0:T(8,128)S(1)}, u32[]{:S(2)}, u32[]{:S(2)}) collective-permute-start(f32[400,256]{1,0:T(8,128)S(1)} %pad_maximum_fusion.4), channel_id=1, source_target_pairs={{0,24},{8,0},{16,8},{24,16},{1,25},{9,1},{17,9},{25,17},{2,26},{10... | collective-permute-start | bytes 1228808 | tf_op jit(solution)/shard_map/ppermute | solution.py:510
  75.4 1.6 %collective-permute-start.19 = (f32[80,1024]{1,0:T(8,128)S(1)}, f32[80,1024]{1,0:T(8,128)S(1)}, u32[]{:S(2)}, u32[]{:S(2)}) collective-permute-start(f32[80,1024]{1,0:T(8,128)S(1)} %collective-permute-done.11.refs_1_), channel_id=1, source_target_pairs={{0,4},{4,0},{1,5},{5,1},{2,6},{6,2},{3,7},{7,3},{8,12},{12,8},{9,1... | collective-permute-start | bytes 983048 | tf_op jit(solution)/shard_map/ppermute | solution.py:511
  77.0 10.5 %collective-permute-start.25 = (f32[80,1024]{1,0:T(8,128)S(1)}, f32[80,1024]{1,0:T(8,128)S(1)}, u32[]{:S(2)}, u32[]{:S(2)}) collective-permute-start(f32[80,1024]{1,0:T(8,128)S(1)} %collective-permute-done.12.refs_3_), channel_id=1, source_target_pairs={{0,4},{4,0},{1,5},{5,1},{2,6},{6,2},{3,7},{7,3},{8,12},{12,8},{9,1... | collective-permute-start | bytes 983048 | tf_op jit(solution)/shard_map/ppermute | solution.py:511
  80.4 14.4 %collective-permute-start.22 = (f32[240,256]{1,0:T(8,128)S(1)}, f32[240,256]{1,0:T(8,128)S(1)}, u32[]{:S(2)}, u32[]{:S(2)}) collective-permute-start(f32[240,256]{1,0:T(8,128)S(1)} %pad_maximum_fusion.5), channel_id=1, source_target_pairs={{0,32},{32,64},{64,96},{96,128},{128,160},{160,192},{192,224},{224... | collective-permute-start | bytes 737288 | tf_op jit(solution)/shard_map/ppermute | solution.py:510
  81.0 11.5 %collective-permute-start.24 = (f32[80,1024]{1,0:T(8,128)S(1)}, f32[80,1024]{1,0:T(8,128)S(1)}, u32[]{:S(2)}, u32[]{:S(2)}) collective-permute-start(f32[80,1024]{1,0:T(8,128)S(1)} %collective-permute-done.17.refs_2_), channel_id=1, source_target_pairs={{0,4},{4,0},{1,5},{5,1},{2,6},{6,2},{3,7},{7,3},{8,12},{12,8},{9,1... | collective-permute-start | bytes 983048 | tf_op jit(solution)/shard_map/ppermute | solution.py:511
  81.0 13.7 %collective-permute-start.23 = (f32[240,256]{1,0:T(8,128)S(1)}, f32[240,256]{1,0:T(8,128)S(1)}, u32[]{:S(2)}, u32[]{:S(2)}) collective-permute-start(f32[240,256]{1,0:T(8,128)S(1)} %pad_maximum_fusion.6), channel_id=1, source_target_pairs={{0,224},{32,0},{64,32},{96,64},{128,96},{160,128},{192,160},{224,1... | collective-permute-start | bytes 737288 | tf_op jit(solution)/shard_map/ppermute | solution.py:510
  83.8 10.8 %collective-permute-start.21 = (f32[160,256]{1,0:T(8,128)S(1)}, f32[160,256]{1,0:T(8,128)S(1)}, u32[]{:S(2)}, u32[]{:S(2)}) collective-permute-start(f32[160,256]{1,0:T(8,128)S(1)} %slice.47), channel_id=1, source_target_pairs={{0,24},{8,0},{16,8},{24,16},{1,25},{9,1},{17,9},{25,17},{2,26},{10... | collective-permute-start | bytes 491528 | tf_op jit(solution)/shard_map/ppermute | solution.py:510
  87.5 7.3 %collective-permute-start.20 = (f32[160,256]{1,0:T(8,128)S(1)}, f32[160,256]{1,0:T(8,128)S(1)}, u32[]{:S(2)}, u32[]{:S(2)}) collective-permute-start(f32[160,256]{1,0:T(8,128)S(1)} %slice.46), channel_id=1, source_target_pairs={{0,8},{8,16},{16,24},{24,0},{1,9},{9,17},{17,25},{25,1},{2,10},{10... | collective-permute-start | bytes 491528 | tf_op jit(solution)/shard_map/ppermute | solution.py:510
  94.8 5.8 %collective-permute-start.27 = (f32[80,256]{1,0:T(8,128)S(1)}, f32[80,256]{1,0:T(8,128)S(1)}, u32[]{:S(2)}, u32[]{:S(2)}) collective-permute-start(f32[80,256]{1,0:T(8,128)S(1)} %slice.51), channel_id=1, source_target_pairs={{0,24},{8,0},{16,8},{24,16},{1,25},{9,1},{17,9},{25,17},{2,26},{10... | collective-permute-start | bytes 245768 | tf_op jit(solution)/shard_map/ppermute | solution.py:510
  98.0 5.7 %collective-permute-start.26 = (f32[80,256]{1,0:T(8,128)S(1)}, f32[80,256]{1,0:T(8,128)S(1)}, u32[]{:S(2)}, u32[]{:S(2)}) collective-permute-start(f32[80,256]{1,0:T(8,128)S(1)} %slice.50), channel_id=1, source_target_pairs={{0,8},{8,16},{16,24},{24,0},{1,9},{9,17},{17,25},{25,1},{2,10},{10... | collective-permute-start | bytes 245768 | tf_op jit(solution)/shard_map/ppermute | solution.py:510
  112.2 3.0 %collective-permute-start.28 = (f32[4,8,3584]{2,1,0:T(8,128)S(1)}, f32[4,8,3584]{2,1,0:T(8,128)S(1)}, u32[]{:S(2)}, u32[]{:S(2)}) collective-permute-start(f32[4,8,3584]{2,1,0:T(8,128)S(1)} %get-tuple-element.120), channel_id=1, source_target_pairs={{0,4},{4,0},{1,5},{5,1},{2,6},{6,2},{3,7},{7,3},{8,12},{12,8},{9,1... | collective-permute-start | bytes 1376264 | tf_op jit(solution)/shard_map/ppermute | solution.py:511
  115.2 5.9 %collective-permute-start.29 = (f32[8,3584]{1,0:T(8,128)S(1)}, f32[8,3584]{1,0:T(8,128)S(1)}, u32[]{:S(2)}, u32[]{:S(2)}) collective-permute-start(f32[8,3584]{1,0:T(8,128)S(1)} %get-tuple-element.122), channel_id=1, source_target_pairs={{0,1},{1,2},{2,3},{3,0},{4,5},{5,6},{6,7},{7,4},{8,9},{9,10},{10,1... | collective-permute-start | bytes 344072 | tf_op jit(solution)/shard_map/ppermute | solution.py:510
  116.2 7.5 %collective-permute-start.30 = (f32[8,3584]{1,0:T(8,128)S(1)}, f32[8,3584]{1,0:T(8,128)S(1)}, u32[]{:S(2)}, u32[]{:S(2)}) collective-permute-start(f32[8,3584]{1,0:T(8,128)S(1)} %get-tuple-element.123), channel_id=1, source_target_pairs={{0,2},{1,3},{2,0},{3,1},{4,6},{5,7},{6,4},{7,5},{8,10},{9,11},{10,... | collective-permute-start | bytes 344072 | tf_op jit(solution)/shard_map/ppermute | solution.py:510
  119.5 5.8 %collective-permute-start.31 = (f32[8,3584]{1,0:T(8,128)S(1)}, f32[8,3584]{1,0:T(8,128)S(1)}, u32[]{:S(2)}, u32[]{:S(2)}) collective-permute-start(f32[8,3584]{1,0:T(8,128)S(1)} %get-tuple-element.124), channel_id=1, source_target_pairs={{0,3},{1,0},{2,1},{3,2},{4,7},{5,4},{6,5},{7,6},{8,11},{9,8},{10,9... | collective-permute-start | bytes 344072 | tf_op jit(solution)/shard_map/ppermute | solution.py:510
  (6 other events, 79.5 us)

commit v6 on v5

--- a/solution.py
+++ b/solution.py
@@ -554,15 +554,15 @@
     rights = (first, first_down, first_up, second, second_down, second_up, two_down, two_up)
     total = group_call(near_runs, len(NEAR), place, rights, screens[:2], ())
     swapped[2:] = [swap(array) for array in around[2:]]
-    left_high, left_low = left_call(place, around + swapped)
-    y_below, y_above, far_below, far_above, total, left_high, left_low = hold(
-        (y_below, y_above, far_below, far_above, total, left_high, left_low)
+    y_below, y_above, far_below, far_above, total, *swapped[2:] = hold(
+        (y_below, y_above, far_below, far_above, total, *swapped[2:])
     )
 
     across_low, across_high = shift(far_below[:SPAN], "y", 1), shift(far_above[SPAN : 2 * SPAN], "y", -1)
     rights = (z_below, z_above, y_below, y_above)
     total = group_call(middle_runs, len(MIDDLE), place, rights, screens[2:4], (total,))
-    across_low, across_high, total = hold((across_low, across_high, total))
+    left_high, left_low = left_call(place, around + swapped)
+    across_low, across_high, total, left_high, left_low = hold((across_low, across_high, total, left_high, left_low))
     rights = (far_below, far_above, across_low, across_high)
     give, kern = pair_call(place, table, rights, screens[4:], total, left_high, left_low)
 

time: 146 us -> 145 us (level)
  transfers between devices with their start and end apart: 33 -> 33, of which waited for: 19 -> 16; matrix products, arithmetic and copies ran while one was open for 1% -> 1% of each run, Pallas kernels for 15% -> 15%
where the time goes in v6:
time: 145 us; the launch traced here: 144 us
  starting transfers between devices  49.1 us (34%)
  Pallas kernels  37.8 us (26%)
  waiting for transfers between devices  37.1 us (26%)
  blocking collectives  16.3 us (11%)
  local copies, waits for them, and re-layouts  2.98 us (2%)
    ppermute x24, starting transfers between devices, shards(): lax.ppermute(array, axis, ring(lax.axis_size(axis), by))  36.7 us
    ppermute x24, waiting for transfers between devices, shards(): lax.ppermute(array, axis, ring(lax.axis_size(axis), by))  21.5 us
    all_to_all x1, blocking collectives, shards(): parts = lax.all_to_all(parts, ('z', 'y'), 0, 0, tiled=True)  16.3 us
    all_to_all x1, starting transfers between devices, shards(): lax.all_to_all(pieces.reshape(32, 1, -1), ('z', 'y'), 0, 0, tiled=True)  11.6 us
    all_to_all x1, waiting for transfers between devices, shards(): lax.all_to_all(pieces.reshape(32, 1, -1), ('z', 'y'), 0, 0, tiled=True)  11.4 us
    pallas_call x1, Pallas kernels, pair_call(): pl.pallas_call(pair_kernel, out_shape=(jax.ShapeDtypeStruct((4, 8, ROOM *...  8.55 us
    pallas_call x2, Pallas kernels, group_call(): pl.pallas_call(functools.partial(group_kernel, runs, planes), out_shape=j...  7.55 us
    pallas_call x1, Pallas kernels, screen_call(): pl.pallas_call(screen_kernel, out_shape=shapes, in_specs=[SMEM, VMEM, VME...  7.35 us
  transfers between devices with their start and end apart: 33, of which 16 were waited for; matrix products, arithmetic and copies ran while one was open for 1% of the time, Pallas kernels for 15%

profile of v6, /device:TPU:2, one launch (start us, length us, event | category | flops | bytes accessed | tf_op | source)
XLA Modules:
  0.0 144.5 jit_solution(8258622789520934320)
XLA Ops:
  2.0 2.2 %pack.1 = f32[640,128]{1,0:T(8,128)} custom-call(s32[4]{0:T(128)} %pad_add_fusion.place, f32[2,16,2560]{2,1,0:T(8,128)} %own_ref.1, f32[2,16,2560]{2,1,0:T(8,128)} %collective-permute-done.other_ref), custom_call_target="tpu_custom_call" | custom-call | tf_op jit(solution)/shard_map/pack/pallas_call | solution.py:422
  4.4 11.6 %all-to-all-start = ((f32[32,1,2560]{2,1,0:T(1,128)}), f32[32,1,2560]{2,1,0:T(1,128)}, u32[]{:S(2)}, u32[]{:S(2)}) async-start(f32[32,1,2560]{2,1,0:T(1,128)} %bitcast.12), calls=%async_computation | async-start | bytes 655360 | tf_op jit(solution)/shard_map/all_to_all | solution.py:517
  19.4 11.4 %all-to-all-done = f32[32,1,2560]{2,1,0:T(1,128)} async-done(((f32[32,1,2560]{2,1,0:T(1,128)}), f32[32,1,2560]{2,1,0:T(1,128)}, u32[]{:S(2)}, u32[]{:S(2)}) %all-to-all-start) | async-done | bytes 327712 | tf_op jit(solution)/shard_map/all_to_all | solution.py:517
  31.5 2.5 %unpack.1 = (f32[80,1024]{1,0:T(8,128)S(1)}, f32[80,256]{1,0:T(8,128)S(1)}, f32[80,256]{1,0:T(8,128)S(1)}) custom-call(s32[4]{0:T(128)S(1)} %copy-done.2, s32[16,256]{1,0:T(8,128)S(1)} %plan.1.table, f32[640,128]{1,0:T(8,128)} %bitcast.6.in_ref), custom_call_target="tpu_custom_call" | custom-call | tf_op jit(solution)/shard_map/unpack/pallas_call | solution.py:471
  36.9 2.3 %collective-permute-start.6 = (f32[160,256]{1,0:T(8,128)S(1)}, f32[160,256]{1,0:T(8,128)S(1)}, u32[]{:S(2)}, u32[]{:S(2)}) collective-permute-start(f32[160,256]{1,0:T(8,128)S(1)} %shard.1), channel_id=1, source_target_pairs={{0,224},{32,0},{64,32},{96,64},{128,96},{160,128},{192,160},{224,1... | collective-permute-start | bytes 491528 | tf_op jit(solution)/shard_map/ppermute | solution.py:510
  39.2 4.1 %collective-permute-start.4 = (f32[160,256]{1,0:T(8,128)S(1)}, f32[160,256]{1,0:T(8,128)S(1)}, u32[]{:S(2)}, u32[]{:S(2)}) collective-permute-start(f32[160,256]{1,0:T(8,128)S(1)} %shard.1), channel_id=1, source_target_pairs={{0,192},{32,224},{64,0},{96,32},{128,64},{160,96},{192,128},{224,1... | collective-permute-start | bytes 491528 | tf_op jit(solution)/shard_map/ppermute | solution.py:510
  43.4 2.6 %collective-permute-done.5 = f32[160,256]{1,0:T(8,128)S(1)} collective-permute-done((f32[160,256]{1,0:T(8,128)S(1)}, f32[160,256]{1,0:T(8,128)S(1)}, u32[]{:S(2)}, u32[]{:S(2)}) %collective-permute-start.5) | collective-permute-done | bytes 163872 | tf_op jit(solution)/shard_map/ppermute | solution.py:510
  46.5 1.5 %collective-permute-start.11 = (f32[80,1024]{1,0:T(8,128)S(1)}, f32[80,1024]{1,0:T(8,128)S(1)}, u32[]{:S(2)}, u32[]{:S(2)}) collective-permute-start(f32[80,1024]{1,0:T(8,128)S(1)} %get-tuple-element.92.refs_0_), channel_id=1, source_target_pairs={{0,1},{1,2},{2,3},{3,0},{4,5},{5,6},{6,7},{7,4},{8,9},{9,10},{10,1... | collective-permute-start | bytes 983048 | tf_op jit(solution)/shard_map/ppermute | solution.py:510
  48.1 1.6 %collective-permute-start.10 = (f32[480,256]{1,0:T(8,128)S(1)}, f32[480,256]{1,0:T(8,128)S(1)}, u32[]{:S(2)}, u32[]{:S(2)}) collective-permute-start(f32[480,256]{1,0:T(8,128)S(1)} %pad_maximum_fusion.refs_0_), channel_id=1, source_target_pairs={{0,24},{8,0},{16,8},{24,16},{1,25},{9,1},{17,9},{25,17},{2,26},{10... | collective-permute-start | bytes 1474568 | tf_op jit(solution)/shard_map/ppermute | solution.py:510
  50.7 3.0 %collective-permute-start.8 = (f32[320,256]{1,0:T(8,128)S(1)}, f32[320,256]{1,0:T(8,128)S(1)}, u32[]{:S(2)}, u32[]{:S(2)}) collective-permute-start(f32[320,256]{1,0:T(8,128)S(1)} %constant_dynamic-update-slice_fusion.refs_3_), channel_id=1, source_target_pairs={{0,24},{8,0},{16,8},{24,16},{1,25},{9,1},{17,9},{25,17},{2,26},{10... | collective-permute-start | bytes 983048 | tf_op jit(solution)/shard_map/ppermute | solution.py:510
  53.7 1.7 %collective-permute-start.12 = (f32[80,1024]{1,0:T(8,128)S(1)}, f32[80,1024]{1,0:T(8,128)S(1)}, u32[]{:S(2)}, u32[]{:S(2)}) collective-permute-start(f32[80,1024]{1,0:T(8,128)S(1)} %get-tuple-element.92.refs_0_), channel_id=1, source_target_pairs={{0,3},{1,0},{2,1},{3,2},{4,7},{5,4},{6,5},{7,6},{8,11},{9,8},{10,9... | collective-permute-start | bytes 983048 | tf_op jit(solution)/shard_map/ppermute | solution.py:510
  55.4 7.3 %screen.1 = (bf16[640,1664]{1,0:T(8,128)(2,1)S(1)}, bf16[640,1664]{1,0:T(8,128)(2,1)S(1)}, bf16[640,640]{1,0:T(8,128)(2,1)S(1)}, bf16[640,640]{1,0:T(8,128)(2,1)...) custom-call(s32[4]{0:T(128)S(1)} %copy-done.3, f32[320,2560]{1,0:T(8,128)S(1)} %bitcast.10, ...), custom_call_target="tpu_custom_call" | custom-call | tf_op jit(solution)/shard_map/screen/pallas_call | solution.py:153
  63.0 3.5 %collective-permute-done.7.refs_4_ = f32[320,256]{1,0:T(8,128)S(1)} collective-permute-done((f32[320,256]{1,0:T(8,128)S(1)}, f32[320,256]{1,0:T(8,128)S(1)}, u32[]{:S(2)}, u32[]{:S(2)}) %collective-permute-start.7) | collective-permute-done | bytes 327712 | tf_op jit(solution)/shard_map/ppermute | solution.py:510
  67.9 2.6 %collective-permute-start.16 = (f32[480,256]{1,0:T(8,128)S(1)}, f32[480,256]{1,0:T(8,128)S(1)}, u32[]{:S(2)}, u32[]{:S(2)}) collective-permute-start(f32[480,256]{1,0:T(8,128)S(1)} %pad_maximum_fusion.2), channel_id=1, source_target_pairs={{0,224},{32,0},{64,32},{96,64},{128,96},{160,128},{192,160},{224,1... | collective-permute-start | bytes 1474568 | tf_op jit(solution)/shard_map/ppermute | solution.py:510
  71.5 1.4 %collective-permute-start.13 = (f32[400,256]{1,0:T(8,128)S(1)}, f32[400,256]{1,0:T(8,128)S(1)}, u32[]{:S(2)}, u32[]{:S(2)}) collective-permute-start(f32[400,256]{1,0:T(8,128)S(1)} %pad_maximum_fusion.3), channel_id=1, source_target_pairs={{0,8},{8,16},{16,24},{24,0},{1,9},{9,17},{17,25},{25,1},{2,10},{10... | collective-permute-start | bytes 1228808 | tf_op jit(solution)/shard_map/ppermute | solution.py:510
  73.0 2.3 %collective-permute-done.17.refs_2_ = f32[80,1024]{1,0:T(8,128)S(1)} collective-permute-done((f32[80,1024]{1,0:T(8,128)S(1)}, f32[80,1024]{1,0:T(8,128)S(1)}, u32[]{:S(2)}, u32[]{:S(2)}) %collective-permute-start.17) | collective-permute-done | bytes 327712 | tf_op jit(solution)/shard_map/ppermute | solution.py:510
  75.2 1.6 %collective-permute-done.19.refs_5_ = f32[80,1024]{1,0:T(8,128)S(1)} collective-permute-done((f32[80,1024]{1,0:T(8,128)S(1)}, f32[80,1024]{1,0:T(8,128)S(1)}, u32[]{:S(2)}, u32[]{:S(2)}) %collective-permute-start.19) | collective-permute-done | bytes 327712 | tf_op jit(solution)/shard_map/ppermute | solution.py:511
  77.0 2.9 %collective-permute-done.14.refs_7_ = f32[400,256]{1,0:T(8,128)S(1)} collective-permute-done((f32[400,256]{1,0:T(8,128)S(1)}, f32[400,256]{1,0:T(8,128)S(1)}, u32[]{:S(2)}, u32[]{:S(2)}) %collective-permute-start.14) | collective-permute-done | bytes 409632 | tf_op jit(solution)/shard_map/ppermute | solution.py:510
  79.9 2.5 %collective-permute-done.13.refs_6_ = f32[400,256]{1,0:T(8,128)S(1)} collective-permute-done((f32[400,256]{1,0:T(8,128)S(1)}, f32[400,256]{1,0:T(8,128)S(1)}, u32[]{:S(2)}, u32[]{:S(2)}) %collective-permute-start.13) | collective-permute-done | bytes 409632 | tf_op jit(solution)/shard_map/ppermute | solution.py:510
  82.8 2.8 %collective-permute-start.23 = (f32[240,256]{1,0:T(8,128)S(1)}, f32[240,256]{1,0:T(8,128)S(1)}, u32[]{:S(2)}, u32[]{:S(2)}) collective-permute-start(f32[240,256]{1,0:T(8,128)S(1)} %pad_maximum_fusion.6), channel_id=1, source_target_pairs={{0,224},{32,0},{64,32},{96,64},{128,96},{160,128},{192,160},{224,1... | collective-permute-start | bytes 737288 | tf_op jit(solution)/shard_map/ppermute | solution.py:510
  85.8 3.2 %collective-permute-start.21 = (f32[160,256]{1,0:T(8,128)S(1)}, f32[160,256]{1,0:T(8,128)S(1)}, u32[]{:S(2)}, u32[]{:S(2)}) collective-permute-start(f32[160,256]{1,0:T(8,128)S(1)} %slice.47), channel_id=1, source_target_pairs={{0,24},{8,0},{16,8},{24,16},{1,25},{9,1},{17,9},{25,17},{2,26},{10... | collective-permute-start | bytes 491528 | tf_op jit(solution)/shard_map/ppermute | solution.py:510
  89.0 5.0 %group.2.refs_6_ = f32[640,512]{1,0:T(8,128)S(1)} custom-call(s32[4]{0:T(128)S(1)} %copy-done.3, f32[480,256]{1,0:T(8,128)S(1)} %pad_maximum_fusion.refs_0_, f32[480,256]{1,0:T(8,128)S(1)} %collective-permute-done.9.refs_1_, f32[480,256]{1,0:T(8,128)S(1)} %collective-permute-done.10.refs_2_, f32[320,256]{1,0:T(8,128)S(1)} %constant_dynamic-update-slice_fusion.refs_3_, ...), custom_call_target="tpu_custom_call" | custom-call | tf_op jit(solution)/shard_map/group/pallas_call | solution.py:252
  95.4 3.2 %collective-permute-start.27 = (f32[80,256]{1,0:T(8,128)S(1)}, f32[80,256]{1,0:T(8,128)S(1)}, u32[]{:S(2)}, u32[]{:S(2)}) collective-permute-start(f32[80,256]{1,0:T(8,128)S(1)} %slice.51), channel_id=1, source_target_pairs={{0,24},{8,0},{16,8},{24,16},{1,25},{9,1},{17,9},{25,17},{2,26},{10... | collective-permute-start | bytes 245768 | tf_op jit(solution)/shard_map/ppermute | solution.py:510
  98.6 2.1 %left.1 = (bf16[1024,640]{1,0:T(8,128)(2,1)S(1)}, bf16[1024,640]{1,0:T(8,128)(2,1)S(1)}) custom-call(s32[4]{0:T(128)S(1)} %copy-done.3, f32[80,1024]{1,0:T(8,128)S(1)} %get-tuple-element.92.refs_0_, f32[80,1024]{1,0:T(8,128)S(1)} %collective-permute-done.11.refs_1_, f32[80,1024]{1,0:T(8,128)S(1)} %collective-permute-done.17.refs_2_, ...), custom_call_target="tpu_custom_call" | custom-call | tf_op jit(solution)/shard_map/left/pallas_call | solution.py:185
  100.7 2.5 %group.3.refs_6_ = f32[640,512]{1,0:T(8,128)S(1)} custom-call(s32[4]{0:T(128)S(1)} %copy-done.3, f32[480,256]{1,0:T(8,128)S(1)} %collective-permute-done.15.refs_0_, f32[480,256]{1,0:T(8,128)S(1)} %collective-permute-done.16.refs_1_, f32[160,256]{1,0:T(8,128)S(1)} %collective-permute-done.20.refs_2_, f32[160,256]{1,0:T(8,128)S(1)} %collective-permute-done.21.refs_3_, ...), custom_call_target="tpu_custom_call" | custom-call | tf_op jit(solution)/shard_map/group/pallas_call | solution.py:252
  103.3 8.6 %pair.1 = (f32[4,8,3584]{2,1,0:T(8,128)S(1)}, f32[1024,512]{1,0:T(8,128)S(1)}) custom-call(s32[4]{0:T(128)S(1)} %copy-done.3, s32[16,256]{1,0:T(8,128)S(1)} %plan.1.table, f32[240,256]{1,0:T(8,128)S(1)} %collective-permute-done.22.refs_0_, f32[240,256]{1,0:T(8,128)S(1)} %collective-permute-done.23.refs_1_, f32[80,256]{1,0:T(8,128)S(1)} %collective-permute-done.26.refs_2_, ...), custom_call_target="tpu_custom_call" | custom-call | tf_op jit(solution)/shard_map/pair/pallas_call | solution.py:308
  111.9 2.9 %extract.1.one_ref = f32[4,8,3584]{2,1,0:T(8,128)S(1)} custom-call(s32[4]{0:T(128)S(1)} %copy-done.3, s32[16,256]{1,0:T(8,128)S(1)} %plan.1.table, f32[1024,512]{1,0:T(8,128)S(1)} %get-tuple-element.123.kern), custom_call_target="tpu_custom_call" | custom-call | tf_op jit(solution)/shard_map/extract/pallas_call | solution.py:327
  114.9 1.9 %collective-permute-start.29 = (f32[8,3584]{1,0:T(8,128)S(1)}, f32[8,3584]{1,0:T(8,128)S(1)}, u32[]{:S(2)}, u32[]{:S(2)}) collective-permute-start(f32[8,3584]{1,0:T(8,128)S(1)} %get-tuple-element.126), channel_id=1, source_target_pairs={{0,1},{1,2},{2,3},{3,0},{4,5},{5,6},{6,7},{7,4},{8,9},{9,10},{10,1... | collective-permute-start | bytes 344072 | tf_op jit(solution)/shard_map/ppermute | solution.py:510
  118.1 1.7 %collective-permute-start.31 = (f32[8,3584]{1,0:T(8,128)S(1)}, f32[8,3584]{1,0:T(8,128)S(1)}, u32[]{:S(2)}, u32[]{:S(2)}) collective-permute-start(f32[8,3584]{1,0:T(8,128)S(1)} %get-tuple-element.128), channel_id=1, source_target_pairs={{0,3},{1,0},{2,1},{3,2},{4,7},{5,4},{6,5},{7,6},{8,11},{9,8},{10,9... | collective-permute-start | bytes 344072 | tf_op jit(solution)/shard_map/ppermute | solution.py:510
  120.3 4.0 %collective-permute-done.30.three_ref = f32[8,3584]{1,0:T(8,128)S(1)} collective-permute-done((f32[8,3584]{1,0:T(8,128)S(1)}, f32[8,3584]{1,0:T(8,128)S(1)}, u32[]{:S(2)}, u32[]{:S(2)}) %collective-permute-start.30) | collective-permute-done | bytes 114720 | tf_op jit(solution)/shard_map/ppermute | solution.py:510
  126.6 16.3 %all_to_all.10.parts_ref = f32[32,8,256]{2,1,0:T(8,128)S(1)} all-to-all(f32[32,8,256]{2,1,0:T(8,128)S(1)} %owner.1), channel_id=1, replica_groups=mesh['z'=8,'y'=4,'core'=2,'x'=4] {'z','y'}, dimensions={0} | all-to-all | bytes 524288 | tf_op jit(solution)/shard_map/all_to_all | solution.py:572
  142.9 1.5 %last.1 = f32[12,8,16]{2,1,0:T(8,128)} custom-call(s32[4]{0:T(128)S(1)} %copy-done.3, s32[16,256]{1,0:T(8,128)S(1)} %plan.1.table, f32[32,8,256]{2,1,0:T(8,128)S(1)} %all_to_all.10.parts_ref), custom_call_target="tpu_custom_call" | custom-call | tf_op jit(solution)/shard_map/last/pallas_call | solution.py:389
  (79 shorter events, 19.6 us)
Async XLA Ops:
  0.0 2.0 %collective-permute-start = (f32[2,16,2560]{2,1,0:T(8,128)}, f32[2,16,2560]{2,1,0:T(8,128)}, u32[]{:S(2)}, u32[]{:S(2)}) collective-permute-start(f32[2,16,2560]{2,1,0:T(8,128)} %own_ref.1), channel_id=1, source_target_pairs={{0,4},{4,0},{1,5},{5,1},{2,6},{6,2},{3,7},{7,3},{8,12},{12,8},{9,1... | collective-permute-start | bytes 983048 | tf_op jit(solution)/shard_map/ppermute | solution.py:511
  4.2 26.6 %collective-permute-start.1 = (f32[320,2560]{1,0:T(8,128)}, f32[320,2560]{1,0:T(8,128)}, u32[]{:S(2)}, u32[]{:S(2)}) collective-permute-start(f32[320,2560]{1,0:T(8,128)} %bitcast.9), channel_id=1, source_target_pairs={{0,4},{4,0},{1,5},{5,1},{2,6},{6,2},{3,7},{7,3},{8,12},{12,8},{9,1... | collective-permute-start | bytes 9830408 | tf_op jit(solution)/shard_map/ppermute | solution.py:511
  4.4 26.4 %all-to-all-start = ((f32[32,1,2560]{2,1,0:T(1,128)}), f32[32,1,2560]{2,1,0:T(1,128)}, u32[]{:S(2)}, u32[]{:S(2)}) async-start(f32[32,1,2560]{2,1,0:T(1,128)} %bitcast.12), calls=%async_computation | async-start | bytes 655360 | tf_op jit(solution)/shard_map/all_to_all | solution.py:517
  35.9 10.1 %collective-permute-start.5 = (f32[160,256]{1,0:T(8,128)S(1)}, f32[160,256]{1,0:T(8,128)S(1)}, u32[]{:S(2)}, u32[]{:S(2)}) collective-permute-start(f32[160,256]{1,0:T(8,128)S(1)} %shard.1), channel_id=1, source_target_pairs={{0,32},{32,64},{64,96},{96,128},{128,160},{160,192},{192,224},{224... | collective-permute-start | bytes 491528 | tf_op jit(solution)/shard_map/ppermute | solution.py:510
  36.9 9.7 %collective-permute-start.6 = (f32[160,256]{1,0:T(8,128)S(1)}, f32[160,256]{1,0:T(8,128)S(1)}, u32[]{:S(2)}, u32[]{:S(2)}) collective-permute-start(f32[160,256]{1,0:T(8,128)S(1)} %shard.1), channel_id=1, source_target_pairs={{0,224},{32,0},{64,32},{96,64},{128,96},{160,128},{192,160},{224,1... | collective-permute-start | bytes 491528 | tf_op jit(solution)/shard_map/ppermute | solution.py:510
  39.2 11.1 %collective-permute-start.3 = (f32[160,256]{1,0:T(8,128)S(1)}, f32[160,256]{1,0:T(8,128)S(1)}, u32[]{:S(2)}, u32[]{:S(2)}) collective-permute-start(f32[160,256]{1,0:T(8,128)S(1)} %shard.1), channel_id=1, source_target_pairs={{0,64},{32,96},{64,128},{96,160},{128,192},{160,224},{192,0},{224,... | collective-permute-start | bytes 491528 | tf_op jit(solution)/shard_map/ppermute | solution.py:510
  39.2 11.1 %collective-permute-start.4 = (f32[160,256]{1,0:T(8,128)S(1)}, f32[160,256]{1,0:T(8,128)S(1)}, u32[]{:S(2)}, u32[]{:S(2)}) collective-permute-start(f32[160,256]{1,0:T(8,128)S(1)} %shard.1), channel_id=1, source_target_pairs={{0,192},{32,224},{64,0},{96,32},{128,64},{160,96},{192,128},{224,1... | collective-permute-start | bytes 491528 | tf_op jit(solution)/shard_map/ppermute | solution.py:510
  46.5 7.1 %collective-permute-start.11 = (f32[80,1024]{1,0:T(8,128)S(1)}, f32[80,1024]{1,0:T(8,128)S(1)}, u32[]{:S(2)}, u32[]{:S(2)}) collective-permute-start(f32[80,1024]{1,0:T(8,128)S(1)} %get-tuple-element.92.refs_0_), channel_id=1, source_target_pairs={{0,1},{1,2},{2,3},{3,0},{4,5},{5,6},{6,7},{7,4},{8,9},{9,10},{10,1... | collective-permute-start | bytes 983048 | tf_op jit(solution)/shard_map/ppermute | solution.py:510
  48.1 14.7 %collective-permute-start.10 = (f32[480,256]{1,0:T(8,128)S(1)}, f32[480,256]{1,0:T(8,128)S(1)}, u32[]{:S(2)}, u32[]{:S(2)}) collective-permute-start(f32[480,256]{1,0:T(8,128)S(1)} %pad_maximum_fusion.refs_0_), channel_id=1, source_target_pairs={{0,24},{8,0},{16,8},{24,16},{1,25},{9,1},{17,9},{25,17},{2,26},{10... | collective-permute-start | bytes 1474568 | tf_op jit(solution)/shard_map/ppermute | solution.py:510
  49.6 13.4 %collective-permute-start.9 = (f32[480,256]{1,0:T(8,128)S(1)}, f32[480,256]{1,0:T(8,128)S(1)}, u32[]{:S(2)}, u32[]{:S(2)}) collective-permute-start(f32[480,256]{1,0:T(8,128)S(1)} %pad_maximum_fusion.refs_0_), channel_id=1, source_target_pairs={{0,8},{8,16},{16,24},{24,0},{1,9},{9,17},{17,25},{25,1},{2,10},{10... | collective-permute-start | bytes 1474568 | tf_op jit(solution)/shard_map/ppermute | solution.py:510
  50.3 16.2 %collective-permute-start.7 = (f32[320,256]{1,0:T(8,128)S(1)}, f32[320,256]{1,0:T(8,128)S(1)}, u32[]{:S(2)}, u32[]{:S(2)}) collective-permute-start(f32[320,256]{1,0:T(8,128)S(1)} %constant_dynamic-update-slice_fusion.refs_3_), channel_id=1, source_target_pairs={{0,8},{8,16},{16,24},{24,0},{1,9},{9,17},{17,25},{25,1},{2,10},{10... | collective-permute-start | bytes 983048 | tf_op jit(solution)/shard_map/ppermute | solution.py:510
  50.7 15.9 %collective-permute-start.8 = (f32[320,256]{1,0:T(8,128)S(1)}, f32[320,256]{1,0:T(8,128)S(1)}, u32[]{:S(2)}, u32[]{:S(2)}) collective-permute-start(f32[320,256]{1,0:T(8,128)S(1)} %constant_dynamic-update-slice_fusion.refs_3_), channel_id=1, source_target_pairs={{0,24},{8,0},{16,8},{24,16},{1,25},{9,1},{17,9},{25,17},{2,26},{10... | collective-permute-start | bytes 983048 | tf_op jit(solution)/shard_map/ppermute | solution.py:510
  53.7 12.9 %collective-permute-start.12 = (f32[80,1024]{1,0:T(8,128)S(1)}, f32[80,1024]{1,0:T(8,128)S(1)}, u32[]{:S(2)}, u32[]{:S(2)}) collective-permute-start(f32[80,1024]{1,0:T(8,128)S(1)} %get-tuple-element.92.refs_0_), channel_id=1, source_target_pairs={{0,3},{1,0},{2,1},{3,2},{4,7},{5,4},{6,5},{7,6},{8,11},{9,8},{10,9... | collective-permute-start | bytes 983048 | tf_op jit(solution)/shard_map/ppermute | solution.py:510
  62.7 8.8 %collective-permute-start.18 = (f32[80,1024]{1,0:T(8,128)S(1)}, f32[80,1024]{1,0:T(8,128)S(1)}, u32[]{:S(2)}, u32[]{:S(2)}) collective-permute-start(f32[80,1024]{1,0:T(8,128)S(1)} %get-tuple-element.92.refs_0_), channel_id=1, source_target_pairs={{0,4},{4,0},{1,5},{5,1},{2,6},{6,2},{3,7},{7,3},{8,12},{12,8},{9,1... | collective-permute-start | bytes 983048 | tf_op jit(solution)/shard_map/ppermute | solution.py:511
  66.6 8.7 %collective-permute-start.17 = (f32[80,1024]{1,0:T(8,128)S(1)}, f32[80,1024]{1,0:T(8,128)S(1)}, u32[]{:S(2)}, u32[]{:S(2)}) collective-permute-start(f32[80,1024]{1,0:T(8,128)S(1)} %get-tuple-element.92.refs_0_), channel_id=1, source_target_pairs={{0,2},{1,3},{2,0},{3,1},{4,6},{5,7},{6,4},{7,5},{8,10},{9,11},{10,... | collective-permute-start | bytes 983048 | tf_op jit(solution)/shard_map/ppermute | solution.py:510
  67.9 14.6 %collective-permute-start.16 = (f32[480,256]{1,0:T(8,128)S(1)}, f32[480,256]{1,0:T(8,128)S(1)}, u32[]{:S(2)}, u32[]{:S(2)}) collective-permute-start(f32[480,256]{1,0:T(8,128)S(1)} %pad_maximum_fusion.2), channel_id=1, source_target_pairs={{0,224},{32,0},{64,32},{96,64},{128,96},{160,128},{192,160},{224,1... | collective-permute-start | bytes 1474568 | tf_op jit(solution)/shard_map/ppermute | solution.py:510
  70.6 12.2 %collective-permute-start.15 = (f32[480,256]{1,0:T(8,128)S(1)}, f32[480,256]{1,0:T(8,128)S(1)}, u32[]{:S(2)}, u32[]{:S(2)}) collective-permute-start(f32[480,256]{1,0:T(8,128)S(1)} %pad_maximum_fusion.1), channel_id=1, source_target_pairs={{0,32},{32,64},{64,96},{96,128},{128,160},{160,192},{192,224},{224... | collective-permute-start | bytes 1474568 | tf_op jit(solution)/shard_map/ppermute | solution.py:510
  70.7 9.2 %collective-permute-start.14 = (f32[400,256]{1,0:T(8,128)S(1)}, f32[400,256]{1,0:T(8,128)S(1)}, u32[]{:S(2)}, u32[]{:S(2)}) collective-permute-start(f32[400,256]{1,0:T(8,128)S(1)} %pad_maximum_fusion.4), channel_id=1, source_target_pairs={{0,24},{8,0},{16,8},{24,16},{1,25},{9,1},{17,9},{25,17},{2,26},{10... | collective-permute-start | bytes 1228808 | tf_op jit(solution)/shard_map/ppermute | solution.py:510
  71.5 11.0 %collective-permute-start.13 = (f32[400,256]{1,0:T(8,128)S(1)}, f32[400,256]{1,0:T(8,128)S(1)}, u32[]{:S(2)}, u32[]{:S(2)}) collective-permute-start(f32[400,256]{1,0:T(8,128)S(1)} %pad_maximum_fusion.3), channel_id=1, source_target_pairs={{0,8},{8,16},{16,24},{24,0},{1,9},{9,17},{17,25},{25,1},{2,10},{10... | collective-permute-start | bytes 1228808 | tf_op jit(solution)/shard_map/ppermute | solution.py:510
  75.2 1.6 %collective-permute-start.19 = (f32[80,1024]{1,0:T(8,128)S(1)}, f32[80,1024]{1,0:T(8,128)S(1)}, u32[]{:S(2)}, u32[]{:S(2)}) collective-permute-start(f32[80,1024]{1,0:T(8,128)S(1)} %collective-permute-done.11.refs_1_), channel_id=1, source_target_pairs={{0,4},{4,0},{1,5},{5,1},{2,6},{6,2},{3,7},{7,3},{8,12},{12,8},{9,1... | collective-permute-start | bytes 983048 | tf_op jit(solution)/shard_map/ppermute | solution.py:511
  76.9 9.0 %collective-permute-start.25 = (f32[80,1024]{1,0:T(8,128)S(1)}, f32[80,1024]{1,0:T(8,128)S(1)}, u32[]{:S(2)}, u32[]{:S(2)}) collective-permute-start(f32[80,1024]{1,0:T(8,128)S(1)} %collective-permute-done.12.refs_3_), channel_id=1, source_target_pairs={{0,4},{4,0},{1,5},{5,1},{2,6},{6,2},{3,7},{7,3},{8,12},{12,8},{9,1... | collective-permute-start | bytes 983048 | tf_op jit(solution)/shard_map/ppermute | solution.py:511
  82.8 11.2 %collective-permute-start.23 = (f32[240,256]{1,0:T(8,128)S(1)}, f32[240,256]{1,0:T(8,128)S(1)}, u32[]{:S(2)}, u32[]{:S(2)}) collective-permute-start(f32[240,256]{1,0:T(8,128)S(1)} %pad_maximum_fusion.6), channel_id=1, source_target_pairs={{0,224},{32,0},{64,32},{96,64},{128,96},{160,128},{192,160},{224,1... | collective-permute-start | bytes 737288 | tf_op jit(solution)/shard_map/ppermute | solution.py:510
  85.6 9.7 %collective-permute-start.24 = (f32[80,1024]{1,0:T(8,128)S(1)}, f32[80,1024]{1,0:T(8,128)S(1)}, u32[]{:S(2)}, u32[]{:S(2)}) collective-permute-start(f32[80,1024]{1,0:T(8,128)S(1)} %collective-permute-done.17.refs_2_), channel_id=1, source_target_pairs={{0,4},{4,0},{1,5},{5,1},{2,6},{6,2},{3,7},{7,3},{8,12},{12,8},{9,1... | collective-permute-start | bytes 983048 | tf_op jit(solution)/shard_map/ppermute | solution.py:511
  85.6 9.7 %collective-permute-start.22 = (f32[240,256]{1,0:T(8,128)S(1)}, f32[240,256]{1,0:T(8,128)S(1)}, u32[]{:S(2)}, u32[]{:S(2)}) collective-permute-start(f32[240,256]{1,0:T(8,128)S(1)} %pad_maximum_fusion.5), channel_id=1, source_target_pairs={{0,32},{32,64},{64,96},{96,128},{128,160},{160,192},{192,224},{224... | collective-permute-start | bytes 737288 | tf_op jit(solution)/shard_map/ppermute | solution.py:510
  85.7 8.3 %collective-permute-start.20 = (f32[160,256]{1,0:T(8,128)S(1)}, f32[160,256]{1,0:T(8,128)S(1)}, u32[]{:S(2)}, u32[]{:S(2)}) collective-permute-start(f32[160,256]{1,0:T(8,128)S(1)} %slice.46), channel_id=1, source_target_pairs={{0,8},{8,16},{16,24},{24,0},{1,9},{9,17},{17,25},{25,1},{2,10},{10... | collective-permute-start | bytes 491528 | tf_op jit(solution)/shard_map/ppermute | solution.py:510
  85.8 8.2 %collective-permute-start.21 = (f32[160,256]{1,0:T(8,128)S(1)}, f32[160,256]{1,0:T(8,128)S(1)}, u32[]{:S(2)}, u32[]{:S(2)}) collective-permute-start(f32[160,256]{1,0:T(8,128)S(1)} %slice.47), channel_id=1, source_target_pairs={{0,24},{8,0},{16,8},{24,16},{1,25},{9,1},{17,9},{25,17},{2,26},{10... | collective-permute-start | bytes 491528 | tf_op jit(solution)/shard_map/ppermute | solution.py:510
  95.3 8.0 %collective-permute-start.26 = (f32[80,256]{1,0:T(8,128)S(1)}, f32[80,256]{1,0:T(8,128)S(1)}, u32[]{:S(2)}, u32[]{:S(2)}) collective-permute-start(f32[80,256]{1,0:T(8,128)S(1)} %slice.50), channel_id=1, source_target_pairs={{0,8},{8,16},{16,24},{24,0},{1,9},{9,17},{17,25},{25,1},{2,10},{10... | collective-permute-start | bytes 245768 | tf_op jit(solution)/shard_map/ppermute | solution.py:510
  95.4 7.9 %collective-permute-start.27 = (f32[80,256]{1,0:T(8,128)S(1)}, f32[80,256]{1,0:T(8,128)S(1)}, u32[]{:S(2)}, u32[]{:S(2)}) collective-permute-start(f32[80,256]{1,0:T(8,128)S(1)} %slice.51), channel_id=1, source_target_pairs={{0,24},{8,0},{16,8},{24,16},{1,25},{9,1},{17,9},{25,17},{2,26},{10... | collective-permute-start | bytes 245768 | tf_op jit(solution)/shard_map/ppermute | solution.py:510
  111.8 3.0 %collective-permute-start.28 = (f32[4,8,3584]{2,1,0:T(8,128)S(1)}, f32[4,8,3584]{2,1,0:T(8,128)S(1)}, u32[]{:S(2)}, u32[]{:S(2)}) collective-permute-start(f32[4,8,3584]{2,1,0:T(8,128)S(1)} %get-tuple-element.124), channel_id=1, source_target_pairs={{0,4},{4,0},{1,5},{5,1},{2,6},{6,2},{3,7},{7,3},{8,12},{12,8},{9,1... | collective-permute-start | bytes 1376264 | tf_op jit(solution)/shard_map/ppermute | solution.py:511
  114.9 5.4 %collective-permute-start.29 = (f32[8,3584]{1,0:T(8,128)S(1)}, f32[8,3584]{1,0:T(8,128)S(1)}, u32[]{:S(2)}, u32[]{:S(2)}) collective-permute-start(f32[8,3584]{1,0:T(8,128)S(1)} %get-tuple-element.126), channel_id=1, source_target_pairs={{0,1},{1,2},{2,3},{3,0},{4,5},{5,6},{6,7},{7,4},{8,9},{9,10},{10,1... | collective-permute-start | bytes 344072 | tf_op jit(solution)/shard_map/ppermute | solution.py:510
  116.7 7.5 %collective-permute-start.30 = (f32[8,3584]{1,0:T(8,128)S(1)}, f32[8,3584]{1,0:T(8,128)S(1)}, u32[]{:S(2)}, u32[]{:S(2)}) collective-permute-start(f32[8,3584]{1,0:T(8,128)S(1)} %get-tuple-element.127), channel_id=1, source_target_pairs={{0,2},{1,3},{2,0},{3,1},{4,6},{5,7},{6,4},{7,5},{8,10},{9,11},{10,... | collective-permute-start | bytes 344072 | tf_op jit(solution)/shard_map/ppermute | solution.py:510
  118.1 7.2 %collective-permute-start.31 = (f32[8,3584]{1,0:T(8,128)S(1)}, f32[8,3584]{1,0:T(8,128)S(1)}, u32[]{:S(2)}, u32[]{:S(2)}) collective-permute-start(f32[8,3584]{1,0:T(8,128)S(1)} %get-tuple-element.128), channel_id=1, source_target_pairs={{0,3},{1,0},{2,1},{3,2},{4,7},{5,4},{6,5},{7,6},{8,11},{9,8},{10,9... | collective-permute-start | bytes 344072 | tf_op jit(solution)/shard_map/ppermute | solution.py:510
  (6 other events, 82.0 us)

commit v7 on v6

--- a/solution.py
+++ b/solution.py
@@ -527,26 +527,23 @@
     below, above, columns = hold((shift(shard, "z", 1), shift(shard, "z", -1), columns))
     first = join(shard, below, above)
     first_down, first_up = shift(first, "y", 1), shift(first, "y", -1)
+    below2, above2, first, columns = hold((below2, above2, first, columns))
     around = [columns, shift(columns, "x", 1), None, None]
-    below2, above2, first, columns = hold((below2, above2, first, columns))
     second = join(below2, above2)
     second_down, second_up = shift(second, "y", 1), shift(second, "y", -1)
-    around[3] = shift(columns, "x", 3)
     screens = screen_call(place, after(screen, second), other)
     first_down, first_up, around[1], below2, above2, *screens = hold(
         (first_down, first_up, around[1], below2, above2, *screens)
     )
-    second_down, second_up, first_down, around[3] = hold((second_down, second_up, first_down, around[3]))
+    around[2:] = [shift(after(columns, first_down), "x", by) for by in (2, 3)]
+    second_down, second_up, first_down = hold((second_down, second_up, first_down))
 
     z_below = shift(join(second_down[:block], second_up[:block], second[:block]), "z", 1)
     z_above = shift(join(second_down[block:], second_up[block:], second[block:]), "z", -1)
     two_down = shift(join(first_down[: 3 * SPAN], second_down[:block]), "y", 1)
     two_up = shift(join(first_up[3 * SPAN :], second_up[block:]), "y", -1)
-    around[2] = shift(after(columns, second_down), "x", 2)
     swapped = [swap(columns), swap(around[1]), None, None]
-    two_down, two_up, z_below, z_above, around[2], swapped[0], swapped[1] = hold(
-        (two_down, two_up, z_below, z_above, around[2], swapped[0], swapped[1])
-    )
+    two_down, two_up, z_below, z_above, *around[2:] = hold((two_down, two_up, z_below, z_above, *around[2:]))
 
     y_below, y_above = shift(z_below[:block], "y", 1), shift(z_above[block : 2 * block], "y", -1)
     far_below = shift(join(z_below[:block], z_below[2 * block : 2 * block + SPAN]), "z", 1)
@@ -554,8 +551,8 @@
     rights = (first, first_down, first_up, second, second_down, second_up, two_down, two_up)
     total = group_call(near_runs, len(NEAR), place, rights, screens[:2], ())
     swapped[2:] = [swap(array) for array in around[2:]]
-    y_below, y_above, far_below, far_above, total, *swapped[2:] = hold(
-        (y_below, y_above, far_below, far_above, total, *swapped[2:])
+    y_below, y_above, far_below, far_above, total, *swapped = hold(
+        (y_below, y_above, far_below, far_above, total, *swapped)
     )
 
     across_low, across_high = shift(far_below[:SPAN], "y", 1), shift(far_above[SPAN : 2 * SPAN], "y", -1)

time: 145 us -> 147 us (1.014)
  waiting for transfers between devices: 37.1 us -> 42.7 us
  starting transfers between devices: 49.1 us -> 43.8 us
  blocking collectives: 16.3 us -> 17.8 us
    ppermute x24, waiting for transfers between devices: 21.5 us -> 28.8 us  [shards(): lax.ppermute(array, axis, ring(lax.axis_size(axis), by))]
    ppermute x24, starting transfers between devices: 36.7 us -> 30.7 us  [shards(): lax.ppermute(array, axis, ring(lax.axis_size(axis), by))]
    ppermute x8, waiting for transfers between devices: 4.21 us -> 2.59 us  [shards(): swap = lambda array: lax.ppermute(array, 'core', SWAP)]
    all_to_all x1, blocking collectives: 16.3 us -> 17.8 us  [shards(): parts = lax.all_to_all(parts, ('z', 'y'), 0, 0, tiled=True)]
  transfers between devices with their start and end apart: 33 -> 33, of which waited for: 16 -> 14; matrix products, arithmetic and copies ran while one was open for 1% -> 1% of each run, Pallas kernels for 15% -> 14%
where the time goes in v7:
time: 147 us; the launch traced here: 146 us
  starting transfers between devices  43.8 us (30%)
  waiting for transfers between devices  42.7 us (29%)
  Pallas kernels  37.8 us (26%)
  blocking collectives  17.8 us (12%)
  local copies, waits for them, and re-layouts  2.98 us (2%)
    ppermute x24, starting transfers between devices, shards(): lax.ppermute(array, axis, ring(lax.axis_size(axis), by))  30.7 us
    ppermute x24, waiting for transfers between devices, shards(): lax.ppermute(array, axis, ring(lax.axis_size(axis), by))  28.8 us
    all_to_all x1, blocking collectives, shards(): parts = lax.all_to_all(parts, ('z', 'y'), 0, 0, tiled=True)  17.8 us
    all_to_all x1, starting transfers between devices, shards(): lax.all_to_all(pieces.reshape(32, 1, -1), ('z', 'y'), 0, 0, tiled=True)  11.6 us
    all_to_all x1, waiting for transfers between devices, shards(): lax.all_to_all(pieces.reshape(32, 1, -1), ('z', 'y'), 0, 0, tiled=True)  11.4 us
    pallas_call x1, Pallas kernels, pair_call(): pl.pallas_call(pair_kernel, out_shape=(jax.ShapeDtypeStruct((4, 8, ROOM *...  8.55 us
    pallas_call x2, Pallas kernels, group_call(): pl.pallas_call(functools.partial(group_kernel, runs, planes), out_shape=j...  7.55 us
    pallas_call x1, Pallas kernels, screen_call(): pl.pallas_call(screen_kernel, out_shape=shapes, in_specs=[SMEM, VMEM, VME...  7.35 us
  transfers between devices with their start and end apart: 33, of which 14 were waited for; matrix products, arithmetic and copies ran while one was open for 1% of the time, Pallas kernels for 14%

profile of v7, /device:TPU:2, one launch (start us, length us, event | category | flops | bytes accessed | tf_op | source)
XLA Modules:
  0.0 146.3 jit_solution(12397020793682656221)
XLA Ops:
  2.0 2.2 %pack.1 = f32[640,128]{1,0:T(8,128)} custom-call(s32[4]{0:T(128)} %pad_add_fusion.place, f32[2,16,2560]{2,1,0:T(8,128)} %own_ref.1, f32[2,16,2560]{2,1,0:T(8,128)} %collective-permute-done.other_ref), custom_call_target="tpu_custom_call" | custom-call | tf_op jit(solution)/shard_map/pack/pallas_call | solution.py:422
  4.4 11.6 %all-to-all-start = ((f32[32,1,2560]{2,1,0:T(1,128)}), f32[32,1,2560]{2,1,0:T(1,128)}, u32[]{:S(2)}, u32[]{:S(2)}) async-start(f32[32,1,2560]{2,1,0:T(1,128)} %bitcast.12), calls=%async_computation | async-start | bytes 655360 | tf_op jit(solution)/shard_map/all_to_all | solution.py:517
  19.4 11.4 %all-to-all-done = f32[32,1,2560]{2,1,0:T(1,128)} async-done(((f32[32,1,2560]{2,1,0:T(1,128)}), f32[32,1,2560]{2,1,0:T(1,128)}, u32[]{:S(2)}, u32[]{:S(2)}) %all-to-all-start) | async-done | bytes 327712 | tf_op jit(solution)/shard_map/all_to_all | solution.py:517
  31.5 2.5 %unpack.1 = (f32[80,1024]{1,0:T(8,128)S(1)}, f32[80,256]{1,0:T(8,128)S(1)}, f32[80,256]{1,0:T(8,128)S(1)}) custom-call(s32[4]{0:T(128)S(1)} %copy-done.2, s32[16,256]{1,0:T(8,128)S(1)} %plan.1.table, f32[640,128]{1,0:T(8,128)} %bitcast.6.in_ref), custom_call_target="tpu_custom_call" | custom-call | tf_op jit(solution)/shard_map/unpack/pallas_call | solution.py:471
  36.9 2.3 %collective-permute-start.6 = (f32[160,256]{1,0:T(8,128)S(1)}, f32[160,256]{1,0:T(8,128)S(1)}, u32[]{:S(2)}, u32[]{:S(2)}) collective-permute-start(f32[160,256]{1,0:T(8,128)S(1)} %shard.1), channel_id=1, source_target_pairs={{0,224},{32,0},{64,32},{96,64},{128,96},{160,128},{192,160},{224,1... | collective-permute-start | bytes 491528 | tf_op jit(solution)/shard_map/ppermute | solution.py:510
  39.2 4.1 %collective-permute-start.4 = (f32[160,256]{1,0:T(8,128)S(1)}, f32[160,256]{1,0:T(8,128)S(1)}, u32[]{:S(2)}, u32[]{:S(2)}) collective-permute-start(f32[160,256]{1,0:T(8,128)S(1)} %shard.1), channel_id=1, source_target_pairs={{0,192},{32,224},{64,0},{96,32},{128,64},{160,96},{192,128},{224,1... | collective-permute-start | bytes 491528 | tf_op jit(solution)/shard_map/ppermute | solution.py:510
  43.4 2.6 %collective-permute-done.5 = f32[160,256]{1,0:T(8,128)S(1)} collective-permute-done((f32[160,256]{1,0:T(8,128)S(1)}, f32[160,256]{1,0:T(8,128)S(1)}, u32[]{:S(2)}, u32[]{:S(2)}) %collective-permute-start.5) | collective-permute-done | bytes 163872 | tf_op jit(solution)/shard_map/ppermute | solution.py:510
  46.6 1.6 %collective-permute-start.10 = (f32[480,256]{1,0:T(8,128)S(1)}, f32[480,256]{1,0:T(8,128)S(1)}, u32[]{:S(2)}, u32[]{:S(2)}) collective-permute-start(f32[480,256]{1,0:T(8,128)S(1)} %pad_maximum_fusion.refs_0_), channel_id=1, source_target_pairs={{0,24},{8,0},{16,8},{24,16},{1,25},{9,1},{17,9},{25,17},{2,26},{10... | collective-permute-start | bytes 1474568 | tf_op jit(solution)/shard_map/ppermute | solution.py:510
  48.7 1.6 %collective-permute-done.3 = f32[160,256]{1,0:T(8,128)S(1)} collective-permute-done((f32[160,256]{1,0:T(8,128)S(1)}, f32[160,256]{1,0:T(8,128)S(1)}, u32[]{:S(2)}, u32[]{:S(2)}) %collective-permute-start.3) | collective-permute-done | bytes 163872 | tf_op jit(solution)/shard_map/ppermute | solution.py:510
  50.3 1.6 %collective-permute-start.11 = (f32[80,1024]{1,0:T(8,128)S(1)}, f32[80,1024]{1,0:T(8,128)S(1)}, u32[]{:S(2)}, u32[]{:S(2)}) collective-permute-start(f32[80,1024]{1,0:T(8,128)S(1)} %get-tuple-element.92.refs_0_), channel_id=1, source_target_pairs={{0,1},{1,2},{2,3},{3,0},{4,5},{5,6},{6,7},{7,4},{8,9},{9,10},{10,1... | collective-permute-start | bytes 983048 | tf_op jit(solution)/shard_map/ppermute | solution.py:510
  52.2 3.0 %collective-permute-start.8 = (f32[320,256]{1,0:T(8,128)S(1)}, f32[320,256]{1,0:T(8,128)S(1)}, u32[]{:S(2)}, u32[]{:S(2)}) collective-permute-start(f32[320,256]{1,0:T(8,128)S(1)} %constant_dynamic-update-slice_fusion.refs_3_), channel_id=1, source_target_pairs={{0,24},{8,0},{16,8},{24,16},{1,25},{9,1},{17,9},{25,17},{2,26},{10... | collective-permute-start | bytes 983048 | tf_op jit(solution)/shard_map/ppermute | solution.py:510
  55.2 7.3 %screen.1 = (bf16[640,1664]{1,0:T(8,128)(2,1)S(1)}, bf16[640,1664]{1,0:T(8,128)(2,1)S(1)}, bf16[640,640]{1,0:T(8,128)(2,1)S(1)}, bf16[640,640]{1,0:T(8,128)(2,1)...) custom-call(s32[4]{0:T(128)S(1)} %copy-done.3, f32[320,2560]{1,0:T(8,128)S(1)} %bitcast.10, ...), custom_call_target="tpu_custom_call" | custom-call | tf_op jit(solution)/shard_map/screen/pallas_call | solution.py:153
  63.9 2.0 %collective-permute-start.17 = (f32[80,1024]{1,0:T(8,128)S(1)}, f32[80,1024]{1,0:T(8,128)S(1)}, u32[]{:S(2)}, u32[]{:S(2)}) collective-permute-start(f32[80,1024]{1,0:T(8,128)S(1)} %get-tuple-element.92.refs_0_), channel_id=1, source_target_pairs={{0,3},{1,0},{2,1},{3,2},{4,7},{5,4},{6,5},{7,6},{8,11},{9,8},{10,9... | collective-permute-start | bytes 983048 | tf_op jit(solution)/shard_map/ppermute | solution.py:510
  66.1 2.3 %collective-permute-start.15 = (f32[480,256]{1,0:T(8,128)S(1)}, f32[480,256]{1,0:T(8,128)S(1)}, u32[]{:S(2)}, u32[]{:S(2)}) collective-permute-start(f32[480,256]{1,0:T(8,128)S(1)} %pad_maximum_fusion.2), channel_id=1, source_target_pairs={{0,224},{32,0},{64,32},{96,64},{128,96},{160,128},{192,160},{224,1... | collective-permute-start | bytes 1474568 | tf_op jit(solution)/shard_map/ppermute | solution.py:510
  68.6 1.5 %collective-permute-start.13 = (f32[400,256]{1,0:T(8,128)S(1)}, f32[400,256]{1,0:T(8,128)S(1)}, u32[]{:S(2)}, u32[]{:S(2)}) collective-permute-start(f32[400,256]{1,0:T(8,128)S(1)} %pad_maximum_fusion.4), channel_id=1, source_target_pairs={{0,24},{8,0},{16,8},{24,16},{1,25},{9,1},{17,9},{25,17},{2,26},{10... | collective-permute-start | bytes 1228808 | tf_op jit(solution)/shard_map/ppermute | solution.py:510
  70.2 4.7 %collective-permute-done.16.refs_2_ = f32[80,1024]{1,0:T(8,128)S(1)} collective-permute-done((f32[80,1024]{1,0:T(8,128)S(1)}, f32[80,1024]{1,0:T(8,128)S(1)}, u32[]{:S(2)}, u32[]{:S(2)}) %collective-permute-start.16) | collective-permute-done | bytes 327712 | tf_op jit(solution)/shard_map/ppermute | solution.py:510
  74.9 3.6 %collective-permute-done.17.refs_3_ = f32[80,1024]{1,0:T(8,128)S(1)} collective-permute-done((f32[80,1024]{1,0:T(8,128)S(1)}, f32[80,1024]{1,0:T(8,128)S(1)}, u32[]{:S(2)}, u32[]{:S(2)}) %collective-permute-start.17) | collective-permute-done | bytes 327712 | tf_op jit(solution)/shard_map/ppermute | solution.py:510
  79.0 6.1 %collective-permute-done.12.refs_6_ = f32[400,256]{1,0:T(8,128)S(1)} collective-permute-done((f32[400,256]{1,0:T(8,128)S(1)}, f32[400,256]{1,0:T(8,128)S(1)}, u32[]{:S(2)}, u32[]{:S(2)}) %collective-permute-start.12) | collective-permute-done | bytes 409632 | tf_op jit(solution)/shard_map/ppermute | solution.py:510
  86.3 1.7 %collective-permute-start.20 = (f32[240,256]{1,0:T(8,128)S(1)}, f32[240,256]{1,0:T(8,128)S(1)}, u32[]{:S(2)}, u32[]{:S(2)}) collective-permute-start(f32[240,256]{1,0:T(8,128)S(1)} %pad_maximum_fusion.5), channel_id=1, source_target_pairs={{0,32},{32,64},{64,96},{96,128},{128,160},{160,192},{192,224},{224... | collective-permute-start | bytes 737288 | tf_op jit(solution)/shard_map/ppermute | solution.py:510
  88.0 3.7 %collective-permute-done.18.refs_2_ = f32[160,256]{1,0:T(8,128)S(1)} collective-permute-done((f32[160,256]{1,0:T(8,128)S(1)}, f32[160,256]{1,0:T(8,128)S(1)}, u32[]{:S(2)}, u32[]{:S(2)}) %collective-permute-start.18) | collective-permute-done | bytes 163872 | tf_op jit(solution)/shard_map/ppermute | solution.py:510
  91.7 5.0 %group.2.refs_6_ = f32[640,512]{1,0:T(8,128)S(1)} custom-call(s32[4]{0:T(128)S(1)} %copy-done.3, f32[480,256]{1,0:T(8,128)S(1)} %pad_maximum_fusion.refs_0_, f32[480,256]{1,0:T(8,128)S(1)} %collective-permute-done.9.refs_1_, f32[480,256]{1,0:T(8,128)S(1)} %collective-permute-done.10.refs_2_, f32[320,256]{1,0:T(8,128)S(1)} %constant_dynamic-update-slice_fusion.refs_3_, ...), custom_call_target="tpu_custom_call" | custom-call | tf_op jit(solution)/shard_map/group/pallas_call | solution.py:252
  97.1 1.8 %collective-permute-start.26 = (f32[80,256]{1,0:T(8,128)S(1)}, f32[80,256]{1,0:T(8,128)S(1)}, u32[]{:S(2)}, u32[]{:S(2)}) collective-permute-start(f32[80,256]{1,0:T(8,128)S(1)} %slice.50), channel_id=1, source_target_pairs={{0,8},{8,16},{16,24},{24,0},{1,9},{9,17},{17,25},{25,1},{2,10},{10... | collective-permute-start | bytes 245768 | tf_op jit(solution)/shard_map/ppermute | solution.py:510
  98.9 1.5 %collective-permute-start.27 = (f32[80,256]{1,0:T(8,128)S(1)}, f32[80,256]{1,0:T(8,128)S(1)}, u32[]{:S(2)}, u32[]{:S(2)}) collective-permute-start(f32[80,256]{1,0:T(8,128)S(1)} %slice.51), channel_id=1, source_target_pairs={{0,24},{8,0},{16,8},{24,16},{1,25},{9,1},{17,9},{25,17},{2,26},{10... | collective-permute-start | bytes 245768 | tf_op jit(solution)/shard_map/ppermute | solution.py:510
  100.4 2.1 %left.1 = (bf16[1024,640]{1,0:T(8,128)(2,1)S(1)}, bf16[1024,640]{1,0:T(8,128)(2,1)S(1)}) custom-call(s32[4]{0:T(128)S(1)} %copy-done.3, f32[80,1024]{1,0:T(8,128)S(1)} %get-tuple-element.92.refs_0_, f32[80,1024]{1,0:T(8,128)S(1)} %collective-permute-done.11.refs_1_, f32[80,1024]{1,0:T(8,128)S(1)} %collective-permute-done.16.refs_2_, ...), custom_call_target="tpu_custom_call" | custom-call | tf_op jit(solution)/shard_map/left/pallas_call | solution.py:185
  102.5 2.5 %group.3.refs_6_ = f32[640,512]{1,0:T(8,128)S(1)} custom-call(s32[4]{0:T(128)S(1)} %copy-done.3, f32[480,256]{1,0:T(8,128)S(1)} %collective-permute-done.14.refs_0_, f32[480,256]{1,0:T(8,128)S(1)} %collective-permute-done.15.refs_1_, f32[160,256]{1,0:T(8,128)S(1)} %collective-permute-done.18.refs_2_, f32[160,256]{1,0:T(8,128)S(1)} %collective-permute-done.19.refs_3_, ...), custom_call_target="tpu_custom_call" | custom-call | tf_op jit(solution)/shard_map/group/pallas_call | solution.py:252
  105.1 8.6 %pair.1 = (f32[4,8,3584]{2,1,0:T(8,128)S(1)}, f32[1024,512]{1,0:T(8,128)S(1)}) custom-call(s32[4]{0:T(128)S(1)} %copy-done.3, s32[16,256]{1,0:T(8,128)S(1)} %plan.1.table, f32[240,256]{1,0:T(8,128)S(1)} %collective-permute-done.20.refs_0_, f32[240,256]{1,0:T(8,128)S(1)} %collective-permute-done.21.refs_1_, f32[80,256]{1,0:T(8,128)S(1)} %collective-permute-done.26.refs_2_, ...), custom_call_target="tpu_custom_call" | custom-call | tf_op jit(solution)/shard_map/pair/pallas_call | solution.py:308
  113.7 2.9 %extract.1.one_ref = f32[4,8,3584]{2,1,0:T(8,128)S(1)} custom-call(s32[4]{0:T(128)S(1)} %copy-done.3, s32[16,256]{1,0:T(8,128)S(1)} %plan.1.table, f32[1024,512]{1,0:T(8,128)S(1)} %get-tuple-element.123.kern), custom_call_target="tpu_custom_call" | custom-call | tf_op jit(solution)/shard_map/extract/pallas_call | solution.py:327
  117.6 2.5 %collective-permute-start.31 = (f32[8,3584]{1,0:T(8,128)S(1)}, f32[8,3584]{1,0:T(8,128)S(1)}, u32[]{:S(2)}, u32[]{:S(2)}) collective-permute-start(f32[8,3584]{1,0:T(8,128)S(1)} %get-tuple-element.128), channel_id=1, source_target_pairs={{0,3},{1,0},{2,1},{3,2},{4,7},{5,4},{6,5},{7,6},{8,11},{9,8},{10,9... | collective-permute-start | bytes 344072 | tf_op jit(solution)/shard_map/ppermute | solution.py:510
  120.1 2.6 %collective-permute-done.29.two_ref = f32[8,3584]{1,0:T(8,128)S(1)} collective-permute-done((f32[8,3584]{1,0:T(8,128)S(1)}, f32[8,3584]{1,0:T(8,128)S(1)}, u32[]{:S(2)}, u32[]{:S(2)}) %collective-permute-start.29) | collective-permute-done | bytes 114720 | tf_op jit(solution)/shard_map/ppermute | solution.py:510
  122.7 1.7 %collective-permute-done.30.three_ref = f32[8,3584]{1,0:T(8,128)S(1)} collective-permute-done((f32[8,3584]{1,0:T(8,128)S(1)}, f32[8,3584]{1,0:T(8,128)S(1)}, u32[]{:S(2)}, u32[]{:S(2)}) %collective-permute-start.30) | collective-permute-done | bytes 114720 | tf_op jit(solution)/shard_map/ppermute | solution.py:510
  126.9 17.8 %all_to_all.10.parts_ref = f32[32,8,256]{2,1,0:T(8,128)S(1)} all-to-all(f32[32,8,256]{2,1,0:T(8,128)S(1)} %owner.1), channel_id=1, replica_groups=mesh['z'=8,'y'=4,'core'=2,'x'=4] {'z','y'}, dimensions={0} | all-to-all | bytes 524288 | tf_op jit(solution)/shard_map/all_to_all | solution.py:569
  144.7 1.5 %last.1 = f32[12,8,16]{2,1,0:T(8,128)} custom-call(s32[4]{0:T(128)S(1)} %copy-done.3, s32[16,256]{1,0:T(8,128)S(1)} %plan.1.table, f32[32,8,256]{2,1,0:T(8,128)S(1)} %all_to_all.10.parts_ref), custom_call_target="tpu_custom_call" | custom-call | tf_op jit(solution)/shard_map/last/pallas_call | solution.py:389
  (79 shorter events, 18.0 us)
Async XLA Ops:
  0.0 2.0 %collective-permute-start = (f32[2,16,2560]{2,1,0:T(8,128)}, f32[2,16,2560]{2,1,0:T(8,128)}, u32[]{:S(2)}, u32[]{:S(2)}) collective-permute-start(f32[2,16,2560]{2,1,0:T(8,128)} %own_ref.1), channel_id=1, source_target_pairs={{0,4},{4,0},{1,5},{5,1},{2,6},{6,2},{3,7},{7,3},{8,12},{12,8},{9,1... | collective-permute-start | bytes 983048 | tf_op jit(solution)/shard_map/ppermute | solution.py:511
  4.2 26.6 %collective-permute-start.1 = (f32[320,2560]{1,0:T(8,128)}, f32[320,2560]{1,0:T(8,128)}, u32[]{:S(2)}, u32[]{:S(2)}) collective-permute-start(f32[320,2560]{1,0:T(8,128)} %bitcast.9), channel_id=1, source_target_pairs={{0,4},{4,0},{1,5},{5,1},{2,6},{6,2},{3,7},{7,3},{8,12},{12,8},{9,1... | collective-permute-start | bytes 9830408 | tf_op jit(solution)/shard_map/ppermute | solution.py:511
  4.4 26.4 %all-to-all-start = ((f32[32,1,2560]{2,1,0:T(1,128)}), f32[32,1,2560]{2,1,0:T(1,128)}, u32[]{:S(2)}, u32[]{:S(2)}) async-start(f32[32,1,2560]{2,1,0:T(1,128)} %bitcast.12), calls=%async_computation | async-start | bytes 655360 | tf_op jit(solution)/shard_map/all_to_all | solution.py:517
  35.9 10.1 %collective-permute-start.5 = (f32[160,256]{1,0:T(8,128)S(1)}, f32[160,256]{1,0:T(8,128)S(1)}, u32[]{:S(2)}, u32[]{:S(2)}) collective-permute-start(f32[160,256]{1,0:T(8,128)S(1)} %shard.1), channel_id=1, source_target_pairs={{0,32},{32,64},{64,96},{96,128},{128,160},{160,192},{192,224},{224... | collective-permute-start | bytes 491528 | tf_op jit(solution)/shard_map/ppermute | solution.py:510
  36.9 9.7 %collective-permute-start.6 = (f32[160,256]{1,0:T(8,128)S(1)}, f32[160,256]{1,0:T(8,128)S(1)}, u32[]{:S(2)}, u32[]{:S(2)}) collective-permute-start(f32[160,256]{1,0:T(8,128)S(1)} %shard.1), channel_id=1, source_target_pairs={{0,224},{32,0},{64,32},{96,64},{128,96},{160,128},{192,160},{224,1... | collective-permute-start | bytes 491528 | tf_op jit(solution)/shard_map/ppermute | solution.py:510
  39.2 11.1 %collective-permute-start.3 = (f32[160,256]{1,0:T(8,128)S(1)}, f32[160,256]{1,0:T(8,128)S(1)}, u32[]{:S(2)}, u32[]{:S(2)}) collective-permute-start(f32[160,256]{1,0:T(8,128)S(1)} %shard.1), channel_id=1, source_target_pairs={{0,64},{32,96},{64,128},{96,160},{128,192},{160,224},{192,0},{224,... | collective-permute-start | bytes 491528 | tf_op jit(solution)/shard_map/ppermute | solution.py:510
  39.2 11.1 %collective-permute-start.4 = (f32[160,256]{1,0:T(8,128)S(1)}, f32[160,256]{1,0:T(8,128)S(1)}, u32[]{:S(2)}, u32[]{:S(2)}) collective-permute-start(f32[160,256]{1,0:T(8,128)S(1)} %shard.1), channel_id=1, source_target_pairs={{0,192},{32,224},{64,0},{96,32},{128,64},{160,96},{192,128},{224,1... | collective-permute-start | bytes 491528 | tf_op jit(solution)/shard_map/ppermute | solution.py:510
  46.6 16.0 %collective-permute-start.10 = (f32[480,256]{1,0:T(8,128)S(1)}, f32[480,256]{1,0:T(8,128)S(1)}, u32[]{:S(2)}, u32[]{:S(2)}) collective-permute-start(f32[480,256]{1,0:T(8,128)S(1)} %pad_maximum_fusion.refs_0_), channel_id=1, source_target_pairs={{0,24},{8,0},{16,8},{24,16},{1,25},{9,1},{17,9},{25,17},{2,26},{10... | collective-permute-start | bytes 1474568 | tf_op jit(solution)/shard_map/ppermute | solution.py:510
  48.1 14.5 %collective-permute-start.9 = (f32[480,256]{1,0:T(8,128)S(1)}, f32[480,256]{1,0:T(8,128)S(1)}, u32[]{:S(2)}, u32[]{:S(2)}) collective-permute-start(f32[480,256]{1,0:T(8,128)S(1)} %pad_maximum_fusion.refs_0_), channel_id=1, source_target_pairs={{0,8},{8,16},{16,24},{24,0},{1,9},{9,17},{17,25},{25,1},{2,10},{10... | collective-permute-start | bytes 1474568 | tf_op jit(solution)/shard_map/ppermute | solution.py:510
  50.3 12.3 %collective-permute-start.11 = (f32[80,1024]{1,0:T(8,128)S(1)}, f32[80,1024]{1,0:T(8,128)S(1)}, u32[]{:S(2)}, u32[]{:S(2)}) collective-permute-start(f32[80,1024]{1,0:T(8,128)S(1)} %get-tuple-element.92.refs_0_), channel_id=1, source_target_pairs={{0,1},{1,2},{2,3},{3,0},{4,5},{5,6},{6,7},{7,4},{8,9},{9,10},{10,1... | collective-permute-start | bytes 983048 | tf_op jit(solution)/shard_map/ppermute | solution.py:510
  51.9 14.1 %collective-permute-start.7 = (f32[320,256]{1,0:T(8,128)S(1)}, f32[320,256]{1,0:T(8,128)S(1)}, u32[]{:S(2)}, u32[]{:S(2)}) collective-permute-start(f32[320,256]{1,0:T(8,128)S(1)} %constant_dynamic-update-slice_fusion.refs_3_), channel_id=1, source_target_pairs={{0,8},{8,16},{16,24},{24,0},{1,9},{9,17},{17,25},{25,1},{2,10},{10... | collective-permute-start | bytes 983048 | tf_op jit(solution)/shard_map/ppermute | solution.py:510
  52.2 13.7 %collective-permute-start.8 = (f32[320,256]{1,0:T(8,128)S(1)}, f32[320,256]{1,0:T(8,128)S(1)}, u32[]{:S(2)}, u32[]{:S(2)}) collective-permute-start(f32[320,256]{1,0:T(8,128)S(1)} %constant_dynamic-update-slice_fusion.refs_3_), channel_id=1, source_target_pairs={{0,24},{8,0},{16,8},{24,16},{1,25},{9,1},{17,9},{25,17},{2,26},{10... | collective-permute-start | bytes 983048 | tf_op jit(solution)/shard_map/ppermute | solution.py:510
  62.6 12.2 %collective-permute-start.16 = (f32[80,1024]{1,0:T(8,128)S(1)}, f32[80,1024]{1,0:T(8,128)S(1)}, u32[]{:S(2)}, u32[]{:S(2)}) collective-permute-start(f32[80,1024]{1,0:T(8,128)S(1)} %get-tuple-element.92.refs_0_), channel_id=1, source_target_pairs={{0,2},{1,3},{2,0},{3,1},{4,6},{5,7},{6,4},{7,5},{8,10},{9,11},{10,... | collective-permute-start | bytes 983048 | tf_op jit(solution)/shard_map/ppermute | solution.py:510
  63.9 14.5 %collective-permute-start.17 = (f32[80,1024]{1,0:T(8,128)S(1)}, f32[80,1024]{1,0:T(8,128)S(1)}, u32[]{:S(2)}, u32[]{:S(2)}) collective-permute-start(f32[80,1024]{1,0:T(8,128)S(1)} %get-tuple-element.92.refs_0_), channel_id=1, source_target_pairs={{0,3},{1,0},{2,1},{3,2},{4,7},{5,4},{6,5},{7,6},{8,11},{9,8},{10,9... | collective-permute-start | bytes 983048 | tf_op jit(solution)/shard_map/ppermute | solution.py:510
  66.1 19.0 %collective-permute-start.15 = (f32[480,256]{1,0:T(8,128)S(1)}, f32[480,256]{1,0:T(8,128)S(1)}, u32[]{:S(2)}, u32[]{:S(2)}) collective-permute-start(f32[480,256]{1,0:T(8,128)S(1)} %pad_maximum_fusion.2), channel_id=1, source_target_pairs={{0,224},{32,0},{64,32},{96,64},{128,96},{160,128},{192,160},{224,1... | collective-permute-start | bytes 1474568 | tf_op jit(solution)/shard_map/ppermute | solution.py:510
  68.4 16.6 %collective-permute-start.14 = (f32[480,256]{1,0:T(8,128)S(1)}, f32[480,256]{1,0:T(8,128)S(1)}, u32[]{:S(2)}, u32[]{:S(2)}) collective-permute-start(f32[480,256]{1,0:T(8,128)S(1)} %pad_maximum_fusion.1), channel_id=1, source_target_pairs={{0,32},{32,64},{64,96},{96,128},{128,160},{160,192},{192,224},{224... | collective-permute-start | bytes 1474568 | tf_op jit(solution)/shard_map/ppermute | solution.py:510
  68.6 9.9 %collective-permute-start.13 = (f32[400,256]{1,0:T(8,128)S(1)}, f32[400,256]{1,0:T(8,128)S(1)}, u32[]{:S(2)}, u32[]{:S(2)}) collective-permute-start(f32[400,256]{1,0:T(8,128)S(1)} %pad_maximum_fusion.4), channel_id=1, source_target_pairs={{0,24},{8,0},{16,8},{24,16},{1,25},{9,1},{17,9},{25,17},{2,26},{10... | collective-permute-start | bytes 1228808 | tf_op jit(solution)/shard_map/ppermute | solution.py:510
  74.9 10.2 %collective-permute-start.12 = (f32[400,256]{1,0:T(8,128)S(1)}, f32[400,256]{1,0:T(8,128)S(1)}, u32[]{:S(2)}, u32[]{:S(2)}) collective-permute-start(f32[400,256]{1,0:T(8,128)S(1)} %pad_maximum_fusion.3), channel_id=1, source_target_pairs={{0,8},{8,16},{16,24},{24,0},{1,9},{9,17},{17,25},{25,1},{2,10},{10... | collective-permute-start | bytes 1228808 | tf_op jit(solution)/shard_map/ppermute | solution.py:510
  78.4 7.4 %collective-permute-start.22 = (f32[80,1024]{1,0:T(8,128)S(1)}, f32[80,1024]{1,0:T(8,128)S(1)}, u32[]{:S(2)}, u32[]{:S(2)}) collective-permute-start(f32[80,1024]{1,0:T(8,128)S(1)} %get-tuple-element.92.refs_0_), channel_id=1, source_target_pairs={{0,4},{4,0},{1,5},{5,1},{2,6},{6,2},{3,7},{7,3},{8,12},{12,8},{9,1... | collective-permute-start | bytes 983048 | tf_op jit(solution)/shard_map/ppermute | solution.py:511
  78.4 7.9 %collective-permute-start.23 = (f32[80,1024]{1,0:T(8,128)S(1)}, f32[80,1024]{1,0:T(8,128)S(1)}, u32[]{:S(2)}, u32[]{:S(2)}) collective-permute-start(f32[80,1024]{1,0:T(8,128)S(1)} %collective-permute-done.11.refs_1_), channel_id=1, source_target_pairs={{0,4},{4,0},{1,5},{5,1},{2,6},{6,2},{3,7},{7,3},{8,12},{12,8},{9,1... | collective-permute-start | bytes 983048 | tf_op jit(solution)/shard_map/ppermute | solution.py:511
  85.1 6.6 %collective-permute-start.18 = (f32[160,256]{1,0:T(8,128)S(1)}, f32[160,256]{1,0:T(8,128)S(1)}, u32[]{:S(2)}, u32[]{:S(2)}) collective-permute-start(f32[160,256]{1,0:T(8,128)S(1)} %slice.46), channel_id=1, source_target_pairs={{0,8},{8,16},{16,24},{24,0},{1,9},{9,17},{17,25},{25,1},{2,10},{10... | collective-permute-start | bytes 491528 | tf_op jit(solution)/shard_map/ppermute | solution.py:510
  85.2 11.8 %collective-permute-start.24 = (f32[80,1024]{1,0:T(8,128)S(1)}, f32[80,1024]{1,0:T(8,128)S(1)}, u32[]{:S(2)}, u32[]{:S(2)}) collective-permute-start(f32[80,1024]{1,0:T(8,128)S(1)} %collective-permute-done.16.refs_2_), channel_id=1, source_target_pairs={{0,4},{4,0},{1,5},{5,1},{2,6},{6,2},{3,7},{7,3},{8,12},{12,8},{9,1... | collective-permute-start | bytes 983048 | tf_op jit(solution)/shard_map/ppermute | solution.py:511
  85.3 11.8 %collective-permute-start.25 = (f32[80,1024]{1,0:T(8,128)S(1)}, f32[80,1024]{1,0:T(8,128)S(1)}, u32[]{:S(2)}, u32[]{:S(2)}) collective-permute-start(f32[80,1024]{1,0:T(8,128)S(1)} %collective-permute-done.17.refs_3_), channel_id=1, source_target_pairs={{0,4},{4,0},{1,5},{5,1},{2,6},{6,2},{3,7},{7,3},{8,12},{12,8},{9,1... | collective-permute-start | bytes 983048 | tf_op jit(solution)/shard_map/ppermute | solution.py:511
  85.9 11.2 %collective-permute-start.21 = (f32[240,256]{1,0:T(8,128)S(1)}, f32[240,256]{1,0:T(8,128)S(1)}, u32[]{:S(2)}, u32[]{:S(2)}) collective-permute-start(f32[240,256]{1,0:T(8,128)S(1)} %pad_maximum_fusion.6), channel_id=1, source_target_pairs={{0,224},{32,0},{64,32},{96,64},{128,96},{160,128},{192,160},{224,1... | collective-permute-start | bytes 737288 | tf_op jit(solution)/shard_map/ppermute | solution.py:510
  86.3 10.7 %collective-permute-start.20 = (f32[240,256]{1,0:T(8,128)S(1)}, f32[240,256]{1,0:T(8,128)S(1)}, u32[]{:S(2)}, u32[]{:S(2)}) collective-permute-start(f32[240,256]{1,0:T(8,128)S(1)} %pad_maximum_fusion.5), channel_id=1, source_target_pairs={{0,32},{32,64},{64,96},{96,128},{128,160},{160,192},{192,224},{224... | collective-permute-start | bytes 737288 | tf_op jit(solution)/shard_map/ppermute | solution.py:510
  91.7 5.3 %collective-permute-start.19 = (f32[160,256]{1,0:T(8,128)S(1)}, f32[160,256]{1,0:T(8,128)S(1)}, u32[]{:S(2)}, u32[]{:S(2)}) collective-permute-start(f32[160,256]{1,0:T(8,128)S(1)} %slice.47), channel_id=1, source_target_pairs={{0,24},{8,0},{16,8},{24,16},{1,25},{9,1},{17,9},{25,17},{2,26},{10... | collective-permute-start | bytes 491528 | tf_op jit(solution)/shard_map/ppermute | solution.py:510
  97.1 8.0 %collective-permute-start.26 = (f32[80,256]{1,0:T(8,128)S(1)}, f32[80,256]{1,0:T(8,128)S(1)}, u32[]{:S(2)}, u32[]{:S(2)}) collective-permute-start(f32[80,256]{1,0:T(8,128)S(1)} %slice.50), channel_id=1, source_target_pairs={{0,8},{8,16},{16,24},{24,0},{1,9},{9,17},{17,25},{25,1},{2,10},{10... | collective-permute-start | bytes 245768 | tf_op jit(solution)/shard_map/ppermute | solution.py:510
  98.9 6.1 %collective-permute-start.27 = (f32[80,256]{1,0:T(8,128)S(1)}, f32[80,256]{1,0:T(8,128)S(1)}, u32[]{:S(2)}, u32[]{:S(2)}) collective-permute-start(f32[80,256]{1,0:T(8,128)S(1)} %slice.51), channel_id=1, source_target_pairs={{0,24},{8,0},{16,8},{24,16},{1,25},{9,1},{17,9},{25,17},{2,26},{10... | collective-permute-start | bytes 245768 | tf_op jit(solution)/shard_map/ppermute | solution.py:510
  113.6 3.0 %collective-permute-start.28 = (f32[4,8,3584]{2,1,0:T(8,128)S(1)}, f32[4,8,3584]{2,1,0:T(8,128)S(1)}, u32[]{:S(2)}, u32[]{:S(2)}) collective-permute-start(f32[4,8,3584]{2,1,0:T(8,128)S(1)} %get-tuple-element.124), channel_id=1, source_target_pairs={{0,4},{4,0},{1,5},{5,1},{2,6},{6,2},{3,7},{7,3},{8,12},{12,8},{9,1... | collective-permute-start | bytes 1376264 | tf_op jit(solution)/shard_map/ppermute | solution.py:511
  116.7 6.1 %collective-permute-start.29 = (f32[8,3584]{1,0:T(8,128)S(1)}, f32[8,3584]{1,0:T(8,128)S(1)}, u32[]{:S(2)}, u32[]{:S(2)}) collective-permute-start(f32[8,3584]{1,0:T(8,128)S(1)} %get-tuple-element.126), channel_id=1, source_target_pairs={{0,1},{1,2},{2,3},{3,0},{4,5},{5,6},{6,7},{7,4},{8,9},{9,10},{10,1... | collective-permute-start | bytes 344072 | tf_op jit(solution)/shard_map/ppermute | solution.py:510
  116.7 7.6 %collective-permute-start.30 = (f32[8,3584]{1,0:T(8,128)S(1)}, f32[8,3584]{1,0:T(8,128)S(1)}, u32[]{:S(2)}, u32[]{:S(2)}) collective-permute-start(f32[8,3584]{1,0:T(8,128)S(1)} %get-tuple-element.127), channel_id=1, source_target_pairs={{0,2},{1,3},{2,0},{3,1},{4,6},{5,7},{6,4},{7,5},{8,10},{9,11},{10,... | collective-permute-start | bytes 344072 | tf_op jit(solution)/shard_map/ppermute | solution.py:510
  117.6 8.1 %collective-permute-start.31 = (f32[8,3584]{1,0:T(8,128)S(1)}, f32[8,3584]{1,0:T(8,128)S(1)}, u32[]{:S(2)}, u32[]{:S(2)}) collective-permute-start(f32[8,3584]{1,0:T(8,128)S(1)} %get-tuple-element.128), channel_id=1, source_target_pairs={{0,3},{1,0},{2,1},{3,2},{4,7},{5,4},{6,5},{7,6},{8,11},{9,8},{10,9... | collective-permute-start | bytes 344072 | tf_op jit(solution)/shard_map/ppermute | solution.py:510
  (6 other events, 81.7 us)

commit v8 on v6

--- a/solution.py
+++ b/solution.py
@@ -536,13 +536,13 @@
     first_down, first_up, around[1], below2, above2, *screens = hold(
         (first_down, first_up, around[1], below2, above2, *screens)
     )
+    around[2] = shift(after(columns, first_down), "x", 2)
     second_down, second_up, first_down, around[3] = hold((second_down, second_up, first_down, around[3]))
 
     z_below = shift(join(second_down[:block], second_up[:block], second[:block]), "z", 1)
     z_above = shift(join(second_down[block:], second_up[block:], second[block:]), "z", -1)
     two_down = shift(join(first_down[: 3 * SPAN], second_down[:block]), "y", 1)
     two_up = shift(join(first_up[3 * SPAN :], second_up[block:]), "y", -1)
-    around[2] = shift(after(columns, second_down), "x", 2)
     swapped = [swap(columns), swap(around[1]), None, None]
     two_down, two_up, z_below, z_above, around[2], swapped[0], swapped[1] = hold(
         (two_down, two_up, z_below, z_above, around[2], swapped[0], swapped[1])

time: 145 us -> 145 us (level)
  transfers between devices with their start and end apart: 33 -> 33, of which waited for: 16 -> 16; matrix products, arithmetic and copies ran while one was open for 1% -> 1% of each run, Pallas kernels for 15% -> 14%
where the time goes in v8:
time: 145 us
  starting transfers between devices  49.2 us (34%)
  Pallas kernels  37.8 us (26%)
  waiting for transfers between devices  37.3 us (26%)
  blocking collectives  16.4 us (11%)
  local copies, waits for them, and re-layouts  2.98 us (2%)
    ppermute x24, starting transfers between devices, shards(): lax.ppermute(array, axis, ring(lax.axis_size(axis), by))  36.8 us
    ppermute x24, waiting for transfers between devices, shards(): lax.ppermute(array, axis, ring(lax.axis_size(axis), by))  21.8 us
    all_to_all x1, blocking collectives, shards(): parts = lax.all_to_all(parts, ('z', 'y'), 0, 0, tiled=True)  16.4 us
    all_to_all x1, starting transfers between devices, shards(): lax.all_to_all(pieces.reshape(32, 1, -1), ('z', 'y'), 0, 0, tiled=True)  11.6 us
    all_to_all x1, waiting for transfers between devices, shards(): lax.all_to_all(pieces.reshape(32, 1, -1), ('z', 'y'), 0, 0, tiled=True)  11.4 us
    pallas_call x1, Pallas kernels, pair_call(): pl.pallas_call(pair_kernel, out_shape=(jax.ShapeDtypeStruct((4, 8, ROOM *...  8.77 us
    pallas_call x2, Pallas kernels, group_call(): pl.pallas_call(functools.partial(group_kernel, runs, planes), out_shape=j...  7.55 us
    pallas_call x1, Pallas kernels, screen_call(): pl.pallas_call(screen_kernel, out_shape=shapes, in_specs=[SMEM, VMEM, VME...  7.35 us
  transfers between devices with their start and end apart: 33, of which 16 were waited for; matrix products, arithmetic and copies ran while one was open for 1% of the time, Pallas kernels for 14%

profile of v8, /device:TPU:2, one launch (start us, length us, event | category | flops | bytes accessed | tf_op | source)
XLA Modules:
  0.0 144.9 jit_solution(17985240799923918458)
XLA Ops:
  2.0 2.2 %pack.1 = f32[640,128]{1,0:T(8,128)} custom-call(s32[4]{0:T(128)} %pad_add_fusion.place, f32[2,16,2560]{2,1,0:T(8,128)} %own_ref.1, f32[2,16,2560]{2,1,0:T(8,128)} %collective-permute-done.other_ref), custom_call_target="tpu_custom_call" | custom-call | tf_op jit(solution)/shard_map/pack/pallas_call | solution.py:422
  4.4 11.6 %all-to-all-start = ((f32[32,1,2560]{2,1,0:T(1,128)}), f32[32,1,2560]{2,1,0:T(1,128)}, u32[]{:S(2)}, u32[]{:S(2)}) async-start(f32[32,1,2560]{2,1,0:T(1,128)} %bitcast.12), calls=%async_computation | async-start | bytes 655360 | tf_op jit(solution)/shard_map/all_to_all | solution.py:517
  19.4 11.4 %all-to-all-done = f32[32,1,2560]{2,1,0:T(1,128)} async-done(((f32[32,1,2560]{2,1,0:T(1,128)}), f32[32,1,2560]{2,1,0:T(1,128)}, u32[]{:S(2)}, u32[]{:S(2)}) %all-to-all-start) | async-done | bytes 327712 | tf_op jit(solution)/shard_map/all_to_all | solution.py:517
  31.5 2.5 %unpack.1 = (f32[80,1024]{1,0:T(8,128)S(1)}, f32[80,256]{1,0:T(8,128)S(1)}, f32[80,256]{1,0:T(8,128)S(1)}) custom-call(s32[4]{0:T(128)S(1)} %copy-done.2, s32[16,256]{1,0:T(8,128)S(1)} %plan.1.table, f32[640,128]{1,0:T(8,128)} %bitcast.6.in_ref), custom_call_target="tpu_custom_call" | custom-call | tf_op jit(solution)/shard_map/unpack/pallas_call | solution.py:471
  36.9 2.3 %collective-permute-start.6 = (f32[160,256]{1,0:T(8,128)S(1)}, f32[160,256]{1,0:T(8,128)S(1)}, u32[]{:S(2)}, u32[]{:S(2)}) collective-permute-start(f32[160,256]{1,0:T(8,128)S(1)} %shard.1), channel_id=1, source_target_pairs={{0,224},{32,0},{64,32},{96,64},{128,96},{160,128},{192,160},{224,1... | collective-permute-start | bytes 491528 | tf_op jit(solution)/shard_map/ppermute | solution.py:510
  39.2 4.1 %collective-permute-start.4 = (f32[160,256]{1,0:T(8,128)S(1)}, f32[160,256]{1,0:T(8,128)S(1)}, u32[]{:S(2)}, u32[]{:S(2)}) collective-permute-start(f32[160,256]{1,0:T(8,128)S(1)} %shard.1), channel_id=1, source_target_pairs={{0,192},{32,224},{64,0},{96,32},{128,64},{160,96},{192,128},{224,1... | collective-permute-start | bytes 491528 | tf_op jit(solution)/shard_map/ppermute | solution.py:510
  43.4 2.6 %collective-permute-done.5 = f32[160,256]{1,0:T(8,128)S(1)} collective-permute-done((f32[160,256]{1,0:T(8,128)S(1)}, f32[160,256]{1,0:T(8,128)S(1)}, u32[]{:S(2)}, u32[]{:S(2)}) %collective-permute-start.5) | collective-permute-done | bytes 163872 | tf_op jit(solution)/shard_map/ppermute | solution.py:510
  48.1 1.6 %collective-permute-start.10 = (f32[480,256]{1,0:T(8,128)S(1)}, f32[480,256]{1,0:T(8,128)S(1)}, u32[]{:S(2)}, u32[]{:S(2)}) collective-permute-start(f32[480,256]{1,0:T(8,128)S(1)} %pad_maximum_fusion.refs_0_), channel_id=1, source_target_pairs={{0,24},{8,0},{16,8},{24,16},{1,25},{9,1},{17,9},{25,17},{2,26},{10... | collective-permute-start | bytes 1474568 | tf_op jit(solution)/shard_map/ppermute | solution.py:510
  50.7 3.0 %collective-permute-start.8 = (f32[320,256]{1,0:T(8,128)S(1)}, f32[320,256]{1,0:T(8,128)S(1)}, u32[]{:S(2)}, u32[]{:S(2)}) collective-permute-start(f32[320,256]{1,0:T(8,128)S(1)} %constant_dynamic-update-slice_fusion.refs_3_), channel_id=1, source_target_pairs={{0,24},{8,0},{16,8},{24,16},{1,25},{9,1},{17,9},{25,17},{2,26},{10... | collective-permute-start | bytes 983048 | tf_op jit(solution)/shard_map/ppermute | solution.py:510
  53.7 1.7 %collective-permute-start.12 = (f32[80,1024]{1,0:T(8,128)S(1)}, f32[80,1024]{1,0:T(8,128)S(1)}, u32[]{:S(2)}, u32[]{:S(2)}) collective-permute-start(f32[80,1024]{1,0:T(8,128)S(1)} %get-tuple-element.92.refs_0_), channel_id=1, source_target_pairs={{0,3},{1,0},{2,1},{3,2},{4,7},{5,4},{6,5},{7,6},{8,11},{9,8},{10,9... | collective-permute-start | bytes 983048 | tf_op jit(solution)/shard_map/ppermute | solution.py:510
  55.4 7.3 %screen.1 = (bf16[640,1664]{1,0:T(8,128)(2,1)S(1)}, bf16[640,1664]{1,0:T(8,128)(2,1)S(1)}, bf16[640,640]{1,0:T(8,128)(2,1)S(1)}, bf16[640,640]{1,0:T(8,128)(2,1)...) custom-call(s32[4]{0:T(128)S(1)} %copy-done.3, f32[320,2560]{1,0:T(8,128)S(1)} %bitcast.10, ...), custom_call_target="tpu_custom_call" | custom-call | tf_op jit(solution)/shard_map/screen/pallas_call | solution.py:153
  64.4 2.2 %collective-permute-done.7.refs_4_ = f32[320,256]{1,0:T(8,128)S(1)} collective-permute-done((f32[320,256]{1,0:T(8,128)S(1)}, f32[320,256]{1,0:T(8,128)S(1)}, u32[]{:S(2)}, u32[]{:S(2)}) %collective-permute-start.7) | collective-permute-done | bytes 327712 | tf_op jit(solution)/shard_map/ppermute | solution.py:510
  66.6 2.7 %collective-permute-start.16 = (f32[480,256]{1,0:T(8,128)S(1)}, f32[480,256]{1,0:T(8,128)S(1)}, u32[]{:S(2)}, u32[]{:S(2)}) collective-permute-start(f32[480,256]{1,0:T(8,128)S(1)} %pad_maximum_fusion.2), channel_id=1, source_target_pairs={{0,224},{32,0},{64,32},{96,64},{128,96},{160,128},{192,160},{224,1... | collective-permute-start | bytes 1474568 | tf_op jit(solution)/shard_map/ppermute | solution.py:510
  70.2 1.6 %collective-permute-start.13 = (f32[400,256]{1,0:T(8,128)S(1)}, f32[400,256]{1,0:T(8,128)S(1)}, u32[]{:S(2)}, u32[]{:S(2)}) collective-permute-start(f32[400,256]{1,0:T(8,128)S(1)} %pad_maximum_fusion.3), channel_id=1, source_target_pairs={{0,8},{8,16},{16,24},{24,0},{1,9},{9,17},{17,25},{25,1},{2,10},{10... | collective-permute-start | bytes 1228808 | tf_op jit(solution)/shard_map/ppermute | solution.py:510
  71.8 2.9 %collective-permute-done.17.refs_2_ = f32[80,1024]{1,0:T(8,128)S(1)} collective-permute-done((f32[80,1024]{1,0:T(8,128)S(1)}, f32[80,1024]{1,0:T(8,128)S(1)}, u32[]{:S(2)}, u32[]{:S(2)}) %collective-permute-start.17) | collective-permute-done | bytes 327712 | tf_op jit(solution)/shard_map/ppermute | solution.py:510
  74.7 1.6 %collective-permute-done.19.refs_5_ = f32[80,1024]{1,0:T(8,128)S(1)} collective-permute-done((f32[80,1024]{1,0:T(8,128)S(1)}, f32[80,1024]{1,0:T(8,128)S(1)}, u32[]{:S(2)}, u32[]{:S(2)}) %collective-permute-start.19) | collective-permute-done | bytes 327712 | tf_op jit(solution)/shard_map/ppermute | solution.py:511
  76.4 3.4 %collective-permute-done.14.refs_7_ = f32[400,256]{1,0:T(8,128)S(1)} collective-permute-done((f32[400,256]{1,0:T(8,128)S(1)}, f32[400,256]{1,0:T(8,128)S(1)}, u32[]{:S(2)}, u32[]{:S(2)}) %collective-permute-start.14) | collective-permute-done | bytes 409632 | tf_op jit(solution)/shard_map/ppermute | solution.py:510
  79.9 2.5 %collective-permute-done.13.refs_6_ = f32[400,256]{1,0:T(8,128)S(1)} collective-permute-done((f32[400,256]{1,0:T(8,128)S(1)}, f32[400,256]{1,0:T(8,128)S(1)}, u32[]{:S(2)}, u32[]{:S(2)}) %collective-permute-start.13) | collective-permute-done | bytes 409632 | tf_op jit(solution)/shard_map/ppermute | solution.py:510
  82.8 2.8 %collective-permute-start.23 = (f32[240,256]{1,0:T(8,128)S(1)}, f32[240,256]{1,0:T(8,128)S(1)}, u32[]{:S(2)}, u32[]{:S(2)}) collective-permute-start(f32[240,256]{1,0:T(8,128)S(1)} %pad_maximum_fusion.6), channel_id=1, source_target_pairs={{0,224},{32,0},{64,32},{96,64},{128,96},{160,128},{192,160},{224,1... | collective-permute-start | bytes 737288 | tf_op jit(solution)/shard_map/ppermute | solution.py:510
  85.8 3.2 %collective-permute-start.21 = (f32[160,256]{1,0:T(8,128)S(1)}, f32[160,256]{1,0:T(8,128)S(1)}, u32[]{:S(2)}, u32[]{:S(2)}) collective-permute-start(f32[160,256]{1,0:T(8,128)S(1)} %slice.47), channel_id=1, source_target_pairs={{0,24},{8,0},{16,8},{24,16},{1,25},{9,1},{17,9},{25,17},{2,26},{10... | collective-permute-start | bytes 491528 | tf_op jit(solution)/shard_map/ppermute | solution.py:510
  89.0 5.0 %group.2.refs_6_ = f32[640,512]{1,0:T(8,128)S(1)} custom-call(s32[4]{0:T(128)S(1)} %copy-done.3, f32[480,256]{1,0:T(8,128)S(1)} %pad_maximum_fusion.refs_0_, f32[480,256]{1,0:T(8,128)S(1)} %collective-permute-done.9.refs_1_, f32[480,256]{1,0:T(8,128)S(1)} %collective-permute-done.10.refs_2_, f32[320,256]{1,0:T(8,128)S(1)} %constant_dynamic-update-slice_fusion.refs_3_, ...), custom_call_target="tpu_custom_call" | custom-call | tf_op jit(solution)/shard_map/group/pallas_call | solution.py:252
  95.3 3.2 %collective-permute-start.27 = (f32[80,256]{1,0:T(8,128)S(1)}, f32[80,256]{1,0:T(8,128)S(1)}, u32[]{:S(2)}, u32[]{:S(2)}) collective-permute-start(f32[80,256]{1,0:T(8,128)S(1)} %slice.51), channel_id=1, source_target_pairs={{0,24},{8,0},{16,8},{24,16},{1,25},{9,1},{17,9},{25,17},{2,26},{10... | collective-permute-start | bytes 245768 | tf_op jit(solution)/shard_map/ppermute | solution.py:510
  98.6 2.1 %left.1 = (bf16[1024,640]{1,0:T(8,128)(2,1)S(1)}, bf16[1024,640]{1,0:T(8,128)(2,1)S(1)}) custom-call(s32[4]{0:T(128)S(1)} %copy-done.3, f32[80,1024]{1,0:T(8,128)S(1)} %get-tuple-element.92.refs_0_, f32[80,1024]{1,0:T(8,128)S(1)} %collective-permute-done.11.refs_1_, f32[80,1024]{1,0:T(8,128)S(1)} %collective-permute-done.17.refs_2_, ...), custom_call_target="tpu_custom_call" | custom-call | tf_op jit(solution)/shard_map/left/pallas_call | solution.py:185
  100.7 2.5 %group.3.refs_6_ = f32[640,512]{1,0:T(8,128)S(1)} custom-call(s32[4]{0:T(128)S(1)} %copy-done.3, f32[480,256]{1,0:T(8,128)S(1)} %collective-permute-done.15.refs_0_, f32[480,256]{1,0:T(8,128)S(1)} %collective-permute-done.16.refs_1_, f32[160,256]{1,0:T(8,128)S(1)} %collective-permute-done.20.refs_2_, f32[160,256]{1,0:T(8,128)S(1)} %collective-permute-done.21.refs_3_, ...), custom_call_target="tpu_custom_call" | custom-call | tf_op jit(solution)/shard_map/group/pallas_call | solution.py:252
  103.2 8.8 %pair.1 = (f32[4,8,3584]{2,1,0:T(8,128)S(1)}, f32[1024,512]{1,0:T(8,128)S(1)}) custom-call(s32[4]{0:T(128)S(1)} %copy-done.3, s32[16,256]{1,0:T(8,128)S(1)} %plan.1.table, f32[240,256]{1,0:T(8,128)S(1)} %collective-permute-done.22.refs_0_, f32[240,256]{1,0:T(8,128)S(1)} %collective-permute-done.23.refs_1_, f32[80,256]{1,0:T(8,128)S(1)} %collective-permute-done.26.refs_2_, ...), custom_call_target="tpu_custom_call" | custom-call | tf_op jit(solution)/shard_map/pair/pallas_call | solution.py:308
  112.1 2.6 %extract.1.one_ref = f32[4,8,3584]{2,1,0:T(8,128)S(1)} custom-call(s32[4]{0:T(128)S(1)} %copy-done.3, s32[16,256]{1,0:T(8,128)S(1)} %plan.1.table, f32[1024,512]{1,0:T(8,128)S(1)} %get-tuple-element.123.kern), custom_call_target="tpu_custom_call" | custom-call | tf_op jit(solution)/shard_map/extract/pallas_call | solution.py:327
  114.8 1.9 %collective-permute-start.29 = (f32[8,3584]{1,0:T(8,128)S(1)}, f32[8,3584]{1,0:T(8,128)S(1)}, u32[]{:S(2)}, u32[]{:S(2)}) collective-permute-start(f32[8,3584]{1,0:T(8,128)S(1)} %get-tuple-element.126), channel_id=1, source_target_pairs={{0,1},{1,2},{2,3},{3,0},{4,5},{5,6},{6,7},{7,4},{8,9},{9,10},{10,1... | collective-permute-start | bytes 344072 | tf_op jit(solution)/shard_map/ppermute | solution.py:510
  118.1 1.7 %collective-permute-start.31 = (f32[8,3584]{1,0:T(8,128)S(1)}, f32[8,3584]{1,0:T(8,128)S(1)}, u32[]{:S(2)}, u32[]{:S(2)}) collective-permute-start(f32[8,3584]{1,0:T(8,128)S(1)} %get-tuple-element.128), channel_id=1, source_target_pairs={{0,3},{1,0},{2,1},{3,2},{4,7},{5,4},{6,5},{7,6},{8,11},{9,8},{10,9... | collective-permute-start | bytes 344072 | tf_op jit(solution)/shard_map/ppermute | solution.py:510
  120.6 3.5 %collective-permute-done.30.three_ref = f32[8,3584]{1,0:T(8,128)S(1)} collective-permute-done((f32[8,3584]{1,0:T(8,128)S(1)}, f32[8,3584]{1,0:T(8,128)S(1)}, u32[]{:S(2)}, u32[]{:S(2)}) %collective-permute-start.30) | collective-permute-done | bytes 114720 | tf_op jit(solution)/shard_map/ppermute | solution.py:510
  124.2 1.6 %collective-permute-done.31.four_ref = f32[8,3584]{1,0:T(8,128)S(1)} collective-permute-done((f32[8,3584]{1,0:T(8,128)S(1)}, f32[8,3584]{1,0:T(8,128)S(1)}, u32[]{:S(2)}, u32[]{:S(2)}) %collective-permute-start.31) | collective-permute-done | bytes 114720 | tf_op jit(solution)/shard_map/ppermute | solution.py:510
  127.0 16.4 %all_to_all.10.parts_ref = f32[32,8,256]{2,1,0:T(8,128)S(1)} all-to-all(f32[32,8,256]{2,1,0:T(8,128)S(1)} %owner.1), channel_id=1, replica_groups=mesh['z'=8,'y'=4,'core'=2,'x'=4] {'z','y'}, dimensions={0} | all-to-all | bytes 524288 | tf_op jit(solution)/shard_map/all_to_all | solution.py:572
  143.4 1.5 %last.1 = f32[12,8,16]{2,1,0:T(8,128)} custom-call(s32[4]{0:T(128)S(1)} %copy-done.3, s32[16,256]{1,0:T(8,128)S(1)} %plan.1.table, f32[32,8,256]{2,1,0:T(8,128)S(1)} %all_to_all.10.parts_ref), custom_call_target="tpu_custom_call" | custom-call | tf_op jit(solution)/shard_map/last/pallas_call | solution.py:389
  (79 shorter events, 20.3 us)
Async XLA Ops:
  0.0 2.0 %collective-permute-start = (f32[2,16,2560]{2,1,0:T(8,128)}, f32[2,16,2560]{2,1,0:T(8,128)}, u32[]{:S(2)}, u32[]{:S(2)}) collective-permute-start(f32[2,16,2560]{2,1,0:T(8,128)} %own_ref.1), channel_id=1, source_target_pairs={{0,4},{4,0},{1,5},{5,1},{2,6},{6,2},{3,7},{7,3},{8,12},{12,8},{9,1... | collective-permute-start | bytes 983048 | tf_op jit(solution)/shard_map/ppermute | solution.py:511
  4.2 26.6 %collective-permute-start.1 = (f32[320,2560]{1,0:T(8,128)}, f32[320,2560]{1,0:T(8,128)}, u32[]{:S(2)}, u32[]{:S(2)}) collective-permute-start(f32[320,2560]{1,0:T(8,128)} %bitcast.9), channel_id=1, source_target_pairs={{0,4},{4,0},{1,5},{5,1},{2,6},{6,2},{3,7},{7,3},{8,12},{12,8},{9,1... | collective-permute-start | bytes 9830408 | tf_op jit(solution)/shard_map/ppermute | solution.py:511
  4.4 26.4 %all-to-all-start = ((f32[32,1,2560]{2,1,0:T(1,128)}), f32[32,1,2560]{2,1,0:T(1,128)}, u32[]{:S(2)}, u32[]{:S(2)}) async-start(f32[32,1,2560]{2,1,0:T(1,128)} %bitcast.12), calls=%async_computation | async-start | bytes 655360 | tf_op jit(solution)/shard_map/all_to_all | solution.py:517
  35.9 10.1 %collective-permute-start.5 = (f32[160,256]{1,0:T(8,128)S(1)}, f32[160,256]{1,0:T(8,128)S(1)}, u32[]{:S(2)}, u32[]{:S(2)}) collective-permute-start(f32[160,256]{1,0:T(8,128)S(1)} %shard.1), channel_id=1, source_target_pairs={{0,32},{32,64},{64,96},{96,128},{128,160},{160,192},{192,224},{224... | collective-permute-start | bytes 491528 | tf_op jit(solution)/shard_map/ppermute | solution.py:510
  36.9 9.7 %collective-permute-start.6 = (f32[160,256]{1,0:T(8,128)S(1)}, f32[160,256]{1,0:T(8,128)S(1)}, u32[]{:S(2)}, u32[]{:S(2)}) collective-permute-start(f32[160,256]{1,0:T(8,128)S(1)} %shard.1), channel_id=1, source_target_pairs={{0,224},{32,0},{64,32},{96,64},{128,96},{160,128},{192,160},{224,1... | collective-permute-start | bytes 491528 | tf_op jit(solution)/shard_map/ppermute | solution.py:510
  39.2 11.1 %collective-permute-start.3 = (f32[160,256]{1,0:T(8,128)S(1)}, f32[160,256]{1,0:T(8,128)S(1)}, u32[]{:S(2)}, u32[]{:S(2)}) collective-permute-start(f32[160,256]{1,0:T(8,128)S(1)} %shard.1), channel_id=1, source_target_pairs={{0,64},{32,96},{64,128},{96,160},{128,192},{160,224},{192,0},{224,... | collective-permute-start | bytes 491528 | tf_op jit(solution)/shard_map/ppermute | solution.py:510
  39.2 11.1 %collective-permute-start.4 = (f32[160,256]{1,0:T(8,128)S(1)}, f32[160,256]{1,0:T(8,128)S(1)}, u32[]{:S(2)}, u32[]{:S(2)}) collective-permute-start(f32[160,256]{1,0:T(8,128)S(1)} %shard.1), channel_id=1, source_target_pairs={{0,192},{32,224},{64,0},{96,32},{128,64},{160,96},{192,128},{224,1... | collective-permute-start | bytes 491528 | tf_op jit(solution)/shard_map/ppermute | solution.py:510
  46.5 7.1 %collective-permute-start.11 = (f32[80,1024]{1,0:T(8,128)S(1)}, f32[80,1024]{1,0:T(8,128)S(1)}, u32[]{:S(2)}, u32[]{:S(2)}) collective-permute-start(f32[80,1024]{1,0:T(8,128)S(1)} %get-tuple-element.92.refs_0_), channel_id=1, source_target_pairs={{0,1},{1,2},{2,3},{3,0},{4,5},{5,6},{6,7},{7,4},{8,9},{9,10},{10,1... | collective-permute-start | bytes 983048 | tf_op jit(solution)/shard_map/ppermute | solution.py:510
  48.1 14.7 %collective-permute-start.10 = (f32[480,256]{1,0:T(8,128)S(1)}, f32[480,256]{1,0:T(8,128)S(1)}, u32[]{:S(2)}, u32[]{:S(2)}) collective-permute-start(f32[480,256]{1,0:T(8,128)S(1)} %pad_maximum_fusion.refs_0_), channel_id=1, source_target_pairs={{0,24},{8,0},{16,8},{24,16},{1,25},{9,1},{17,9},{25,17},{2,26},{10... | collective-permute-start | bytes 1474568 | tf_op jit(solution)/shard_map/ppermute | solution.py:510
  49.6 13.4 %collective-permute-start.9 = (f32[480,256]{1,0:T(8,128)S(1)}, f32[480,256]{1,0:T(8,128)S(1)}, u32[]{:S(2)}, u32[]{:S(2)}) collective-permute-start(f32[480,256]{1,0:T(8,128)S(1)} %pad_maximum_fusion.refs_0_), channel_id=1, source_target_pairs={{0,8},{8,16},{16,24},{24,0},{1,9},{9,17},{17,25},{25,1},{2,10},{10... | collective-permute-start | bytes 1474568 | tf_op jit(solution)/shard_map/ppermute | solution.py:510
  50.3 16.2 %collective-permute-start.7 = (f32[320,256]{1,0:T(8,128)S(1)}, f32[320,256]{1,0:T(8,128)S(1)}, u32[]{:S(2)}, u32[]{:S(2)}) collective-permute-start(f32[320,256]{1,0:T(8,128)S(1)} %constant_dynamic-update-slice_fusion.refs_3_), channel_id=1, source_target_pairs={{0,8},{8,16},{16,24},{24,0},{1,9},{9,17},{17,25},{25,1},{2,10},{10... | collective-permute-start | bytes 983048 | tf_op jit(solution)/shard_map/ppermute | solution.py:510
  50.7 15.9 %collective-permute-start.8 = (f32[320,256]{1,0:T(8,128)S(1)}, f32[320,256]{1,0:T(8,128)S(1)}, u32[]{:S(2)}, u32[]{:S(2)}) collective-permute-start(f32[320,256]{1,0:T(8,128)S(1)} %constant_dynamic-update-slice_fusion.refs_3_), channel_id=1, source_target_pairs={{0,24},{8,0},{16,8},{24,16},{1,25},{9,1},{17,9},{25,17},{2,26},{10... | collective-permute-start | bytes 983048 | tf_op jit(solution)/shard_map/ppermute | solution.py:510
  53.7 12.9 %collective-permute-start.12 = (f32[80,1024]{1,0:T(8,128)S(1)}, f32[80,1024]{1,0:T(8,128)S(1)}, u32[]{:S(2)}, u32[]{:S(2)}) collective-permute-start(f32[80,1024]{1,0:T(8,128)S(1)} %get-tuple-element.92.refs_0_), channel_id=1, source_target_pairs={{0,3},{1,0},{2,1},{3,2},{4,7},{5,4},{6,5},{7,6},{8,11},{9,8},{10,9... | collective-permute-start | bytes 983048 | tf_op jit(solution)/shard_map/ppermute | solution.py:510
  62.7 7.4 %collective-permute-start.18 = (f32[80,1024]{1,0:T(8,128)S(1)}, f32[80,1024]{1,0:T(8,128)S(1)}, u32[]{:S(2)}, u32[]{:S(2)}) collective-permute-start(f32[80,1024]{1,0:T(8,128)S(1)} %get-tuple-element.92.refs_0_), channel_id=1, source_target_pairs={{0,4},{4,0},{1,5},{5,1},{2,6},{6,2},{3,7},{7,3},{8,12},{12,8},{9,1... | collective-permute-start | bytes 983048 | tf_op jit(solution)/shard_map/ppermute | solution.py:511
  63.0 11.6 %collective-permute-start.17 = (f32[80,1024]{1,0:T(8,128)S(1)}, f32[80,1024]{1,0:T(8,128)S(1)}, u32[]{:S(2)}, u32[]{:S(2)}) collective-permute-start(f32[80,1024]{1,0:T(8,128)S(1)} %get-tuple-element.92.refs_0_), channel_id=1, source_target_pairs={{0,2},{1,3},{2,0},{3,1},{4,6},{5,7},{6,4},{7,5},{8,10},{9,11},{10,... | collective-permute-start | bytes 983048 | tf_op jit(solution)/shard_map/ppermute | solution.py:510
  66.6 15.8 %collective-permute-start.16 = (f32[480,256]{1,0:T(8,128)S(1)}, f32[480,256]{1,0:T(8,128)S(1)}, u32[]{:S(2)}, u32[]{:S(2)}) collective-permute-start(f32[480,256]{1,0:T(8,128)S(1)} %pad_maximum_fusion.2), channel_id=1, source_target_pairs={{0,224},{32,0},{64,32},{96,64},{128,96},{160,128},{192,160},{224,1... | collective-permute-start | bytes 1474568 | tf_op jit(solution)/shard_map/ppermute | solution.py:510
  69.4 13.3 %collective-permute-start.15 = (f32[480,256]{1,0:T(8,128)S(1)}, f32[480,256]{1,0:T(8,128)S(1)}, u32[]{:S(2)}, u32[]{:S(2)}) collective-permute-start(f32[480,256]{1,0:T(8,128)S(1)} %pad_maximum_fusion.1), channel_id=1, source_target_pairs={{0,32},{32,64},{64,96},{96,128},{128,160},{160,192},{192,224},{224... | collective-permute-start | bytes 1474568 | tf_op jit(solution)/shard_map/ppermute | solution.py:510
  69.5 10.3 %collective-permute-start.14 = (f32[400,256]{1,0:T(8,128)S(1)}, f32[400,256]{1,0:T(8,128)S(1)}, u32[]{:S(2)}, u32[]{:S(2)}) collective-permute-start(f32[400,256]{1,0:T(8,128)S(1)} %pad_maximum_fusion.4), channel_id=1, source_target_pairs={{0,24},{8,0},{16,8},{24,16},{1,25},{9,1},{17,9},{25,17},{2,26},{10... | collective-permute-start | bytes 1228808 | tf_op jit(solution)/shard_map/ppermute | solution.py:510
  70.2 12.2 %collective-permute-start.13 = (f32[400,256]{1,0:T(8,128)S(1)}, f32[400,256]{1,0:T(8,128)S(1)}, u32[]{:S(2)}, u32[]{:S(2)}) collective-permute-start(f32[400,256]{1,0:T(8,128)S(1)} %pad_maximum_fusion.3), channel_id=1, source_target_pairs={{0,8},{8,16},{16,24},{24,0},{1,9},{9,17},{17,25},{25,1},{2,10},{10... | collective-permute-start | bytes 1228808 | tf_op jit(solution)/shard_map/ppermute | solution.py:510
  74.7 1.6 %collective-permute-start.19 = (f32[80,1024]{1,0:T(8,128)S(1)}, f32[80,1024]{1,0:T(8,128)S(1)}, u32[]{:S(2)}, u32[]{:S(2)}) collective-permute-start(f32[80,1024]{1,0:T(8,128)S(1)} %collective-permute-done.11.refs_1_), channel_id=1, source_target_pairs={{0,4},{4,0},{1,5},{5,1},{2,6},{6,2},{3,7},{7,3},{8,12},{12,8},{9,1... | collective-permute-start | bytes 983048 | tf_op jit(solution)/shard_map/ppermute | solution.py:511
  76.3 9.4 %collective-permute-start.25 = (f32[80,1024]{1,0:T(8,128)S(1)}, f32[80,1024]{1,0:T(8,128)S(1)}, u32[]{:S(2)}, u32[]{:S(2)}) collective-permute-start(f32[80,1024]{1,0:T(8,128)S(1)} %collective-permute-done.12.refs_3_), channel_id=1, source_target_pairs={{0,4},{4,0},{1,5},{5,1},{2,6},{6,2},{3,7},{7,3},{8,12},{12,8},{9,1... | collective-permute-start | bytes 983048 | tf_op jit(solution)/shard_map/ppermute | solution.py:511
  82.8 11.2 %collective-permute-start.23 = (f32[240,256]{1,0:T(8,128)S(1)}, f32[240,256]{1,0:T(8,128)S(1)}, u32[]{:S(2)}, u32[]{:S(2)}) collective-permute-start(f32[240,256]{1,0:T(8,128)S(1)} %pad_maximum_fusion.6), channel_id=1, source_target_pairs={{0,224},{32,0},{64,32},{96,64},{128,96},{160,128},{192,160},{224,1... | collective-permute-start | bytes 737288 | tf_op jit(solution)/shard_map/ppermute | solution.py:510
  85.5 9.7 %collective-permute-start.24 = (f32[80,1024]{1,0:T(8,128)S(1)}, f32[80,1024]{1,0:T(8,128)S(1)}, u32[]{:S(2)}, u32[]{:S(2)}) collective-permute-start(f32[80,1024]{1,0:T(8,128)S(1)} %collective-permute-done.17.refs_2_), channel_id=1, source_target_pairs={{0,4},{4,0},{1,5},{5,1},{2,6},{6,2},{3,7},{7,3},{8,12},{12,8},{9,1... | collective-permute-start | bytes 983048 | tf_op jit(solution)/shard_map/ppermute | solution.py:511
  85.6 9.7 %collective-permute-start.22 = (f32[240,256]{1,0:T(8,128)S(1)}, f32[240,256]{1,0:T(8,128)S(1)}, u32[]{:S(2)}, u32[]{:S(2)}) collective-permute-start(f32[240,256]{1,0:T(8,128)S(1)} %pad_maximum_fusion.5), channel_id=1, source_target_pairs={{0,32},{32,64},{64,96},{96,128},{128,160},{160,192},{192,224},{224... | collective-permute-start | bytes 737288 | tf_op jit(solution)/shard_map/ppermute | solution.py:510
  85.7 8.3 %collective-permute-start.20 = (f32[160,256]{1,0:T(8,128)S(1)}, f32[160,256]{1,0:T(8,128)S(1)}, u32[]{:S(2)}, u32[]{:S(2)}) collective-permute-start(f32[160,256]{1,0:T(8,128)S(1)} %slice.46), channel_id=1, source_target_pairs={{0,8},{8,16},{16,24},{24,0},{1,9},{9,17},{17,25},{25,1},{2,10},{10... | collective-permute-start | bytes 491528 | tf_op jit(solution)/shard_map/ppermute | solution.py:510
  85.8 8.2 %collective-permute-start.21 = (f32[160,256]{1,0:T(8,128)S(1)}, f32[160,256]{1,0:T(8,128)S(1)}, u32[]{:S(2)}, u32[]{:S(2)}) collective-permute-start(f32[160,256]{1,0:T(8,128)S(1)} %slice.47), channel_id=1, source_target_pairs={{0,24},{8,0},{16,8},{24,16},{1,25},{9,1},{17,9},{25,17},{2,26},{10... | collective-permute-start | bytes 491528 | tf_op jit(solution)/shard_map/ppermute | solution.py:510
  95.2 8.0 %collective-permute-start.26 = (f32[80,256]{1,0:T(8,128)S(1)}, f32[80,256]{1,0:T(8,128)S(1)}, u32[]{:S(2)}, u32[]{:S(2)}) collective-permute-start(f32[80,256]{1,0:T(8,128)S(1)} %slice.50), channel_id=1, source_target_pairs={{0,8},{8,16},{16,24},{24,0},{1,9},{9,17},{17,25},{25,1},{2,10},{10... | collective-permute-start | bytes 245768 | tf_op jit(solution)/shard_map/ppermute | solution.py:510
  95.3 7.9 %collective-permute-start.27 = (f32[80,256]{1,0:T(8,128)S(1)}, f32[80,256]{1,0:T(8,128)S(1)}, u32[]{:S(2)}, u32[]{:S(2)}) collective-permute-start(f32[80,256]{1,0:T(8,128)S(1)} %slice.51), channel_id=1, source_target_pairs={{0,24},{8,0},{16,8},{24,16},{1,25},{9,1},{17,9},{25,17},{2,26},{10... | collective-permute-start | bytes 245768 | tf_op jit(solution)/shard_map/ppermute | solution.py:510
  112.0 2.7 %collective-permute-start.28 = (f32[4,8,3584]{2,1,0:T(8,128)S(1)}, f32[4,8,3584]{2,1,0:T(8,128)S(1)}, u32[]{:S(2)}, u32[]{:S(2)}) collective-permute-start(f32[4,8,3584]{2,1,0:T(8,128)S(1)} %get-tuple-element.124), channel_id=1, source_target_pairs={{0,4},{4,0},{1,5},{5,1},{2,6},{6,2},{3,7},{7,3},{8,12},{12,8},{9,1... | collective-permute-start | bytes 1376264 | tf_op jit(solution)/shard_map/ppermute | solution.py:511
  114.8 5.8 %collective-permute-start.29 = (f32[8,3584]{1,0:T(8,128)S(1)}, f32[8,3584]{1,0:T(8,128)S(1)}, u32[]{:S(2)}, u32[]{:S(2)}) collective-permute-start(f32[8,3584]{1,0:T(8,128)S(1)} %get-tuple-element.126), channel_id=1, source_target_pairs={{0,1},{1,2},{2,3},{3,0},{4,5},{5,6},{6,7},{7,4},{8,9},{9,10},{10,1... | collective-permute-start | bytes 344072 | tf_op jit(solution)/shard_map/ppermute | solution.py:510
  116.7 7.5 %collective-permute-start.30 = (f32[8,3584]{1,0:T(8,128)S(1)}, f32[8,3584]{1,0:T(8,128)S(1)}, u32[]{:S(2)}, u32[]{:S(2)}) collective-permute-start(f32[8,3584]{1,0:T(8,128)S(1)} %get-tuple-element.127), channel_id=1, source_target_pairs={{0,2},{1,3},{2,0},{3,1},{4,6},{5,7},{6,4},{7,5},{8,10},{9,11},{10,... | collective-permute-start | bytes 344072 | tf_op jit(solution)/shard_map/ppermute | solution.py:510
  118.1 7.7 %collective-permute-start.31 = (f32[8,3584]{1,0:T(8,128)S(1)}, f32[8,3584]{1,0:T(8,128)S(1)}, u32[]{:S(2)}, u32[]{:S(2)}) collective-permute-start(f32[8,3584]{1,0:T(8,128)S(1)} %get-tuple-element.128), channel_id=1, source_target_pairs={{0,3},{1,0},{2,1},{3,2},{4,7},{5,4},{6,5},{7,6},{8,11},{9,8},{10,9... | collective-permute-start | bytes 344072 | tf_op jit(solution)/shard_map/ppermute | solution.py:510
  (6 other events, 82.0 us)
